TPU v7x, 32 devices: a whole 2x2x4 slice. The times are simulated.
32 devices in a mesh: ctx: 4 (over y, x), wa: 8 (over z, core).
Axes of the slice: x: 2, y: 2, z: 4, core: 2. Of those that a mesh axis runs over, the one named last changes fastest.
Arguments:
- block_input: float32 [8, 512, 2048], P('wa', 'ctx'), may hold values from -6 to 6
- query_weight: bfloat16 [2048, 4096], P('wa'), may hold values from -0.125 to 0.125
- key_projection_matrix: bfloat16 [2048, 512], P('wa'), may hold values from -0.125 to 0.125
- value_projection_matrix: bfloat16 [2048, 512], P('wa'), may hold values from -0.125 to 0.125
- output_weight: bfloat16 [4096, 2048], P('wa'), may hold values from -0.1875 to 0.1875
- attention_gain: bfloat16 [2048], P('wa'), may hold values from 0.5 to 1.5
- feedforward_gain: bfloat16 [2048], P('wa'), may hold values from 0.5 to 1.5
- query_gain: bfloat16 [128], P('wa'), may hold values from 0.796875 to 1.296875
- key_gain: bfloat16 [128], P('wa'), may hold values from 0.796875 to 1.296875
- expert_gate: bfloat16 [32, 2048, 768], P(('ctx', 'wa')), may hold values from -0.125 to 0.125
- expert_up: bfloat16 [32, 2048, 768], P(('ctx', 'wa')), may hold values from -0.125 to 0.125
- expert_down: bfloat16 [32, 768, 2048], P(('ctx', 'wa')), may hold values from -0.3125 to 0.3125
- expert_ids: int32 [8, 512, 8], P('wa', 'ctx'), may hold values from 0 to 31, all different within a row; in each aligned block of 128 rows (0 to 127, 128 to 255, ..., all dimensions but the last counted through in order) at most 64 rows name the same one
- route_gates: bfloat16 [8, 512, 8], P('wa', 'ctx'), may hold values from 0.25 to 1
- cotangent: float32 [8, 512, 2048], P('wa', 'ctx'), may hold values from -6 to 6
Outputs:
- block_output: float32 [8, 512, 2048], P('wa', 'ctx')
- input_grad: float32 [8, 512, 2048], P('wa', 'ctx')
- query_weight_grad: float32 [2048, 4096], P('wa')
- key_weight_grad: float32 [2048, 512], P('wa')
- value_weight_grad: float32 [2048, 512], P('wa')
- output_weight_grad: float32 [4096, 2048], P('wa')
- attention_gain_grad: float32 [2048], P('wa')
- feedforward_gain_grad: float32 [2048], P('wa')
- query_gain_grad: float32 [128], P('wa')
- key_gain_grad: float32 [128], P('wa')
- expert_gate_grad: float32 [32, 2048, 768], P(('ctx', 'wa'))
- expert_up_grad: float32 [32, 2048, 768], P(('ctx', 'wa'))
- expert_down_grad: float32 [32, 768, 2048], P(('ctx', 'wa'))
Inputs may be any that keep to these rules, and one draw needn't show every extreme that they name: `expert_ids`: each row names 8 different experts; the rows of one sequence block (128 rows in sequence order) name any one expert at most 64 times, a bound that some block reaches.
All inputs are finite; a program needn't handle non-finite values.
Results may differ from a plain program's by a relative error of at most 0.033.
Values may be sent and summed in bfloat16 or wider, within the bound.
No kernel may reach another device: no remote copies, remote signals or barrier semaphores. Data moves between devices by JAX's collectives and lax.ppermute only.
A program may use at most 320 MiB of HBM per device.

v0:
```python
import jax
import jax.numpy as jnp
from jax import lax
from jax.sharding import PartitionSpec as P

MODEL_WIDTH = 2048
QUERY_HEADS = 32
KEY_VALUE_HEADS = 4
HEAD_SIZE = 128
TOP = 8


EPSILON = 1e-06
ROPE_BASE = 1000000.0
VERY_NEGATIVE = -1e30


def inv_root(values):
    return lax.rsqrt(jnp.mean(values * values, axis=-1, keepdims=True) + EPSILON)


def rope_tables(positions):
    half_width = HEAD_SIZE // 2
    frequency = ROPE_BASE ** (-(jnp.arange(half_width).astype(positions.dtype) * 2.0 / HEAD_SIZE))
    angles = positions[:, None] * frequency[None, :]
    return (jnp.cos(angles)[:, None, :], jnp.sin(angles)[:, None, :])


def rotate(values, cosine, sine):
    half_width = values.shape[-1] // 2
    first_half = values[..., :half_width]
    second_half = values[..., half_width:]
    return jnp.concatenate(
        [first_half * cosine - second_half * sine, second_half * cosine + first_half * sine],
        axis=-1,
    )


def unrotate(values, cosine, sine):
    half_width = values.shape[-1] // 2
    first_half = values[..., :half_width]
    second_half = values[..., half_width:]
    return jnp.concatenate(
        [first_half * cosine + second_half * sine, second_half * cosine - first_half * sine],
        axis=-1,
    )


def on_device(
    block_input,
    query_weight,
    key_projection_matrix,
    value_projection_matrix,
    output_weight,
    attention_gain,
    feedforward_gain,
    query_gain,
    key_gain,
    expert_gate,
    expert_up,
    expert_down,
    expert_ids,
    route_gates,
    cotangent,
):
    block_rows = block_input[0]
    local_token_count = block_rows.shape[0]
    queries_per_group = QUERY_HEADS // KEY_VALUE_HEADS
    score_scale = HEAD_SIZE ** (-0.5)
    (
        full_query,
        full_key,
        full_value,
        full_output,
        gain_attention,
        gain_feedforward,
        gain_query,
        gain_key,
    ) = (
        lax.all_gather(query_weight, "wa", axis=0, tiled=True),
        lax.all_gather(key_projection_matrix, "wa", axis=0, tiled=True),
        lax.all_gather(value_projection_matrix, "wa", axis=0, tiled=True),
        lax.all_gather(output_weight, "wa", axis=0, tiled=True),
        lax.all_gather(attention_gain, "wa", axis=0, tiled=True),
        lax.all_gather(feedforward_gain, "wa", axis=0, tiled=True),
        lax.all_gather(query_gain, "wa", axis=0, tiled=True),
        lax.all_gather(key_gain, "wa", axis=0, tiled=True),
    )
    offset = lax.axis_index("ctx") * local_token_count
    positions = offset + jnp.arange(local_token_count, dtype=jnp.int32)
    cosine, sine = rope_tables(positions.astype(jnp.float32))
    root_x = inv_root(block_rows)
    x_hat = block_rows * root_x
    normalized_input = (x_hat * gain_attention.astype(jnp.float32)).astype(jnp.bfloat16)
    query = jnp.dot(normalized_input, full_query, preferred_element_type=jnp.float32).reshape(
        local_token_count, QUERY_HEADS, HEAD_SIZE
    )
    unrotated_key = jnp.dot(normalized_input, full_key, preferred_element_type=jnp.float32).reshape(
        local_token_count, KEY_VALUE_HEADS, HEAD_SIZE
    )
    value_matrix_rows = (
        jnp.dot(normalized_input, full_value, preferred_element_type=jnp.float32)
        .astype(jnp.bfloat16)
        .reshape(local_token_count, KEY_VALUE_HEADS, HEAD_SIZE)
    )
    root_q = inv_root(query)
    q_hat = query * root_q
    root_k = inv_root(unrotated_key)
    k_hat = unrotated_key * root_k
    rotated_query = rotate(q_hat * gain_query.astype(jnp.float32), cosine, sine).astype(
        jnp.bfloat16
    )
    k_rot = rotate(k_hat * gain_key.astype(jnp.float32), cosine, sine).astype(jnp.bfloat16)
    grouped_query = rotated_query.reshape(
        local_token_count, KEY_VALUE_HEADS, queries_per_group, HEAD_SIZE
    )
    running_row_maximum = jnp.full(
        (KEY_VALUE_HEADS, queries_per_group, local_token_count), VERY_NEGATIVE, jnp.float32
    )
    key_piece = lax.all_gather(k_rot, "ctx", axis=0, tiled=True)
    value_piece = lax.all_gather(value_matrix_rows, "ctx", axis=0, tiled=True)
    row_count = key_piece.shape[0]
    key_positions = jnp.arange(row_count, dtype=jnp.int32)
    allowed = positions[:, None] >= key_positions[None, :]
    scores = (
        jnp.einsum("qhgd,khd->hgqk", grouped_query, key_piece, preferred_element_type=jnp.float32)
        * score_scale
    )
    masked = jnp.where(allowed, scores, VERY_NEGATIVE)
    new_max = jnp.maximum(running_row_maximum, jnp.max(masked, axis=-1))
    weights = jnp.where(allowed, jnp.exp(masked - new_max[..., None]), 0.0)
    total = jnp.sum(weights, axis=-1)
    accum = jnp.einsum(
        "hgqk,khd->hgqd",
        weights.astype(jnp.bfloat16),
        value_piece,
        preferred_element_type=jnp.float32,
    )
    running_row_maximum, total, accum = (new_max, total, accum)
    log_total = running_row_maximum + jnp.log(total)
    attn_heads = (accum / total[..., None]).astype(jnp.bfloat16)
    attended_output = attn_heads.transpose(2, 0, 1, 3).reshape(
        local_token_count, QUERY_HEADS * HEAD_SIZE
    )
    hidden = block_rows + jnp.dot(attended_output, full_output, preferred_element_type=jnp.float32)
    root_h = inv_root(hidden)
    h_hat = hidden * root_h
    ffn_in = (h_hat * gain_feedforward.astype(jnp.float32)).astype(jnp.bfloat16)
    experts = lax.axis_size(("ctx", "wa"))
    capacity = 2 * local_token_count * TOP // experts
    routes = expert_ids[0].reshape(-1)
    one_hot = (routes[:, None] == jnp.arange(experts, dtype=jnp.int32)[None, :]).astype(jnp.int32)
    slot_index = jnp.sum((jnp.cumsum(one_hot, axis=0) - 1) * one_hot, axis=1)
    route_rows = jnp.broadcast_to(
        ffn_in[:, None, :], (local_token_count, TOP, MODEL_WIDTH)
    ).reshape(-1, MODEL_WIDTH)
    outgoing = (
        jnp.zeros((experts, capacity, MODEL_WIDTH), jnp.bfloat16)
        .at[routes, slot_index]
        .set(route_rows)
    )
    gate_w = expert_gate[0]
    up_w = expert_up[0]
    down_w = expert_down[0]
    arrived = lax.all_to_all(outgoing, ("ctx", "wa"), split_axis=0, concat_axis=0, tiled=True)
    gate_pre = jnp.einsum("snd,df->snf", arrived, gate_w, preferred_element_type=jnp.float32)
    up_pre = jnp.einsum("snd,df->snf", arrived, up_w, preferred_element_type=jnp.float32)
    middle = (gate_pre * jax.nn.sigmoid(gate_pre) * up_pre).astype(jnp.bfloat16)
    produced = jnp.einsum("snf,fd->snd", middle, down_w, preferred_element_type=jnp.float32).astype(
        jnp.bfloat16
    )
    returned = lax.all_to_all(produced, ("ctx", "wa"), split_axis=0, concat_axis=0, tiled=True)
    returned, arrived, gate_pre, up_pre = (returned, arrived, gate_pre, up_pre)
    gate_flat = route_gates[0].reshape(-1).astype(jnp.float32)
    picked = returned[routes, slot_index].astype(jnp.float32)
    mixture = jnp.sum(
        (gate_flat[:, None] * picked).reshape(local_token_count, TOP, MODEL_WIDTH), axis=1
    )
    block_output = hidden + mixture
    out_cotangent = cotangent[0]
    down_grad = (
        (gate_flat.reshape(local_token_count, TOP)[:, :, None] * out_cotangent[:, None, :])
        .astype(jnp.bfloat16)
        .reshape(-1, MODEL_WIDTH)
    )
    outgoing_grad = (
        jnp.zeros((experts, capacity, MODEL_WIDTH), jnp.bfloat16)
        .at[routes, slot_index]
        .set(down_grad)
    )
    arrived_grad = lax.all_to_all(
        outgoing_grad, ("ctx", "wa"), split_axis=0, concat_axis=0, tiled=True
    )
    sigmoid_gate = jax.nn.sigmoid(gate_pre)
    activated = gate_pre * sigmoid_gate
    middle = (activated * up_pre).astype(jnp.bfloat16)
    grad_down = jnp.einsum("snf,snd->fd", middle, arrived_grad, preferred_element_type=jnp.float32)
    d_middle = jnp.einsum("snd,fd->snf", arrived_grad, down_w, preferred_element_type=jnp.float32)
    d_gate_pre = (
        d_middle * up_pre * sigmoid_gate * (1.0 + gate_pre * (1.0 - sigmoid_gate))
    ).astype(jnp.bfloat16)
    d_up_pre = (d_middle * activated).astype(jnp.bfloat16)
    grad_gate = jnp.einsum("snd,snf->df", arrived, d_gate_pre, preferred_element_type=jnp.float32)
    grad_up = jnp.einsum("snd,snf->df", arrived, d_up_pre, preferred_element_type=jnp.float32)
    d_rows = (
        jnp.einsum("snf,df->snd", d_gate_pre, gate_w, preferred_element_type=jnp.float32)
        + jnp.einsum("snf,df->snd", d_up_pre, up_w, preferred_element_type=jnp.float32)
    ).astype(jnp.bfloat16)
    back_rows = lax.all_to_all(d_rows, ("ctx", "wa"), split_axis=0, concat_axis=0, tiled=True)
    d_ffn = jnp.sum(
        back_rows[routes, slot_index]
        .astype(jnp.float32)
        .reshape(local_token_count, TOP, MODEL_WIDTH),
        axis=1,
    )
    grad_feedforward = jnp.sum(d_ffn * h_hat, axis=0)
    grad_hat = d_ffn * gain_feedforward.astype(jnp.float32)
    d_hidden = out_cotangent + root_h * (
        grad_hat - h_hat * jnp.mean(grad_hat * h_hat, axis=-1, keepdims=True)
    )
    d_out = d_hidden.astype(jnp.bfloat16)
    grad_attended_output = jnp.dot(d_out, full_output.T, preferred_element_type=jnp.float32).astype(
        jnp.bfloat16
    )
    grad_attention_per_group = grad_attended_output.reshape(
        local_token_count, KEY_VALUE_HEADS, queries_per_group, HEAD_SIZE
    )
    row_delta = jnp.sum(
        grad_attention_per_group.transpose(1, 2, 0, 3).astype(jnp.float32)
        * attn_heads.astype(jnp.float32),
        axis=-1,
    )
    key_piece = lax.all_gather(k_rot, "ctx", axis=0, tiled=True)
    value_piece = lax.all_gather(value_matrix_rows, "ctx", axis=0, tiled=True)
    row_count = key_piece.shape[0]
    key_positions = jnp.arange(row_count, dtype=jnp.int32)
    allowed = positions[:, None] >= key_positions[None, :]
    scores = (
        jnp.einsum("qhgd,khd->hgqk", grouped_query, key_piece, preferred_element_type=jnp.float32)
        * score_scale
    )
    probabilities = jnp.where(allowed, jnp.exp(scores - log_total[..., None]), 0.0)
    d_prob = jnp.einsum(
        "qhgd,khd->hgqk", grad_attention_per_group, value_piece, preferred_element_type=jnp.float32
    )
    d_scores = probabilities * (d_prob - row_delta[..., None])
    prob_round = probabilities.astype(jnp.bfloat16)
    d_round = d_scores.astype(jnp.bfloat16)
    value_part = jnp.einsum(
        "hgqk,qhgd->khd", prob_round, grad_attention_per_group, preferred_element_type=jnp.float32
    )
    key_part = (
        jnp.einsum("hgqk,qhgd->khd", d_round, grouped_query, preferred_element_type=jnp.float32)
        * score_scale
    )
    d_query_acc = (
        jnp.einsum("hgqk,khd->hgqd", d_round, key_piece, preferred_element_type=jnp.float32)
        * score_scale
    )
    d_keys = key_part
    d_values = value_part
    d_query_acc, d_keys, d_values = (d_query_acc, d_keys, d_values)
    d_key_rot, value_gradient = (
        lax.psum_scatter(
            d_keys.astype(jnp.bfloat16), "ctx", scatter_dimension=0, tiled=True
        ).astype(jnp.float32),
        lax.psum_scatter(
            d_values.astype(jnp.bfloat16), "ctx", scatter_dimension=0, tiled=True
        ).astype(jnp.float32),
    )
    d_query_rot = d_query_acc.transpose(2, 0, 1, 3).reshape(
        local_token_count, QUERY_HEADS, HEAD_SIZE
    )
    d_qn = unrotate(d_query_rot, cosine, sine)
    d_kn = unrotate(d_key_rot, cosine, sine)
    grad_qgain = jnp.sum(d_qn * q_hat, axis=(0, 1))
    grad_kgain = jnp.sum(d_kn * k_hat, axis=(0, 1))
    grad_q = d_qn * gain_query.astype(jnp.float32)
    d_query = root_q * (grad_q - q_hat * jnp.mean(grad_q * q_hat, axis=-1, keepdims=True))
    grad_k = d_kn * gain_key.astype(jnp.float32)
    key_gradient = root_k * (grad_k - k_hat * jnp.mean(grad_k * k_hat, axis=-1, keepdims=True))
    d_query_b = d_query.reshape(local_token_count, QUERY_HEADS * HEAD_SIZE).astype(jnp.bfloat16)
    key_gradient_block = key_gradient.reshape(
        local_token_count, KEY_VALUE_HEADS * HEAD_SIZE
    ).astype(jnp.bfloat16)
    value_gradient_block = value_gradient.reshape(
        local_token_count, KEY_VALUE_HEADS * HEAD_SIZE
    ).astype(jnp.bfloat16)
    d_normed = (
        jnp.dot(d_query_b, full_query.T, preferred_element_type=jnp.float32)
        + jnp.dot(key_gradient_block, full_key.T, preferred_element_type=jnp.float32)
        + jnp.dot(value_gradient_block, full_value.T, preferred_element_type=jnp.float32)
    )
    grad_attention = jnp.sum(d_normed * x_hat, axis=0)
    grad_n = d_normed * gain_attention.astype(jnp.float32)
    input_grad = d_hidden + root_x * (
        grad_n - x_hat * jnp.mean(grad_n * x_hat, axis=-1, keepdims=True)
    )
    (
        share_query,
        share_key,
        share_value,
        share_output,
        share_attention,
        share_feedforward,
        share_qgain,
        share_kgain,
    ) = (
        lax.psum_scatter(
            jnp.dot(normalized_input.T, d_query_b, preferred_element_type=jnp.float32).astype(
                jnp.bfloat16
            ),
            "wa",
            scatter_dimension=0,
            tiled=True,
        ).astype(jnp.float32),
        lax.psum_scatter(
            jnp.dot(
                normalized_input.T, key_gradient_block, preferred_element_type=jnp.float32
            ).astype(jnp.bfloat16),
            "wa",
            scatter_dimension=0,
            tiled=True,
        ).astype(jnp.float32),
        lax.psum_scatter(
            jnp.dot(
                normalized_input.T, value_gradient_block, preferred_element_type=jnp.float32
            ).astype(jnp.bfloat16),
            "wa",
            scatter_dimension=0,
            tiled=True,
        ).astype(jnp.float32),
        lax.psum_scatter(
            jnp.dot(attended_output.T, d_out, preferred_element_type=jnp.float32).astype(
                jnp.bfloat16
            ),
            "wa",
            scatter_dimension=0,
            tiled=True,
        ).astype(jnp.float32),
        lax.psum_scatter(
            grad_attention.astype(jnp.bfloat16), "wa", scatter_dimension=0, tiled=True
        ).astype(jnp.float32),
        lax.psum_scatter(
            grad_feedforward.astype(jnp.bfloat16), "wa", scatter_dimension=0, tiled=True
        ).astype(jnp.float32),
        lax.psum_scatter(
            grad_qgain.astype(jnp.bfloat16), "wa", scatter_dimension=0, tiled=True
        ).astype(jnp.float32),
        lax.psum_scatter(
            grad_kgain.astype(jnp.bfloat16), "wa", scatter_dimension=0, tiled=True
        ).astype(jnp.float32),
    )
    (
        total_query,
        total_key,
        total_value,
        total_output,
        total_attention,
        total_feedforward,
        total_qgain,
        total_kgain,
    ) = (
        lax.psum(share_query.astype(jnp.bfloat16), "ctx").astype(jnp.float32),
        lax.psum(share_key.astype(jnp.bfloat16), "ctx").astype(jnp.float32),
        lax.psum(share_value.astype(jnp.bfloat16), "ctx").astype(jnp.float32),
        lax.psum(share_output.astype(jnp.bfloat16), "ctx").astype(jnp.float32),
        lax.psum(share_attention.astype(jnp.bfloat16), "ctx").astype(jnp.float32),
        lax.psum(share_feedforward.astype(jnp.bfloat16), "ctx").astype(jnp.float32),
        lax.psum(share_qgain.astype(jnp.bfloat16), "ctx").astype(jnp.float32),
        lax.psum(share_kgain.astype(jnp.bfloat16), "ctx").astype(jnp.float32),
    )
    return (
        block_output[None],
        input_grad[None],
        total_query,
        total_key,
        total_value,
        total_output,
        total_attention,
        total_feedforward,
        total_qgain,
        total_kgain,
        grad_gate[None],
        grad_up[None],
        grad_down[None],
    )


def solution(mesh):
    in_specs = (
        P("wa", "ctx", None),
        P("wa", None),
        P("wa", None),
        P("wa", None),
        P("wa", None),
        P("wa"),
        P("wa"),
        P("wa"),
        P("wa"),
        P(("ctx", "wa"), None, None),
        P(("ctx", "wa"), None, None),
        P(("ctx", "wa"), None, None),
        P("wa", "ctx", None),
        P("wa", "ctx", None),
        P("wa", "ctx", None),
    )
    out_specs = (
        P("wa", "ctx", None),
        P("wa", "ctx", None),
        P("wa", None),
        P("wa", None),
        P("wa", None),
        P("wa", None),
        P("wa"),
        P("wa"),
        P("wa"),
        P("wa"),
        P(("ctx", "wa"), None, None),
        P(("ctx", "wa"), None, None),
        P(("ctx", "wa"), None, None),
    )
    return jax.shard_map(
        on_device, mesh=mesh, in_specs=in_specs, out_specs=out_specs, check_vma=False
    )
```

profile of v0, /device:TPU:0, one launch (start us, length us, event | category | flops | bytes accessed | tf_op | source)
XLA Modules:
  0.0 1845.6 jit_solution(10903760184316445211)
XLA Ops:
  12.3 18.5 %all-reduce.7 = (bf16[128]{0:T(256)(128)(2,1)S(1)}, bf16[128]{0:T(256)(128)(2,1)S(1)}) all-reduce(bf16[128]{0:T(256)(128)(2,1)S(1)} %dynamic-update-slice, bf16[128]{0:T(256)(128)(2,1)S(1)} %dynamic-update-slice.1), channel_id=1, replica_groups=mesh['ctx'=4,'wa'=8] {'wa'}, use_global_device_ids=true, to_apply=%add | all-reduce | flops 256 | bytes 1024
  31.8 8.5 all-gather.1
  40.4 10.8 all-gather
  51.2 9.0 reduce-window.6
  63.9 2.2 multiply_convert_fusion.6
  66.1 2.4 convolution_convert_fusion.6
  68.6 3.4 all-gather.7.cloned.1.call-done
  72.0 3.9 copy.64
  75.9 11.5 all_gather.39
  87.4 2.5 multiply_reduce_fusion.10
  90.8 10.1 all_gather.35
  100.9 123.4 %all-gather.9.cloned.1.call-done = bf16[2048,4096]{1,0:T(8,128)(2,1)} async-done(((bf16[256,4096]{1,0:T(8,128)(2,1)}), bf16[2048,4096]{1,0:T(8,128)(2,1)}) %all-gather.9.cloned.1.call-update) | async-done | bytes 16777232 | tf_op jit(solution)/shard_map/all_gather | solution.py:80
  224.2 21.8 %copy.65 = bf16[4096,2048]{1,0:T(8,128)(2,1)} copy(bf16[4096,2048]{0,1:T(8,128)(2,1)} %bitcast.245) | data formatting | bytes 33554432 | tf_op jit(solution)/shard_map/dot_general | solution.py:95
  246.1 8.5 multiply_reduce_fusion.2
  257.6 2.4 copy.67
  260.0 2.4 copy.66
  262.4 3.7 fusion.6
  269.3 3.5 fusion.36
  272.8 102.3 %all-gather.13.cloned.1.call-done = bf16[4096,2048]{1,0:T(8,128)(2,1)} async-done(((bf16[512,2048]{1,0:T(8,128)(2,1)}), bf16[4096,2048]{1,0:T(8,128)(2,1)}) %all-gather.13.cloned.1.call-update) | async-done | bytes 16777232 | tf_op jit(solution)/shard_map/all_gather | solution.py:83
  375.1 8.7 multiply_reduce_fusion.7
  385.7 12.1 scatter_custom_fusion
  397.8 3.8 all-to-all-start
  401.9 12.2 scatter_custom_fusion.1
  414.1 172.5 %all-to-all-done = bf16[32,64,2048]{2,1,0:T(8,128)(2,1)} async-done(((bf16[32,64,2048]{2,1,0:T(8,128)(2,1)}), bf16[32,64,2048]{2,1,0:T(8,128)(2,1)}, u32[]{:S(2)}, u32[]{:S(2)}) %all-to-all-start) | async-done | bytes 8388640 | tf_op jit(solution)/shard_map/all_to_all | solution.py:165
  586.6 3.7 all-to-all-start.2
  590.3 11.8 fusion.29
  602.1 10.7 fusion.33
  612.8 162.3 %all-to-all-done.2 = bf16[32,64,2048]{2,1,0:T(8,128)(2,1)} async-done(((bf16[32,64,2048]{2,1,0:T(8,128)(2,1)}), bf16[32,64,2048]{2,1,0:T(8,128)(2,1)}, u32[]{:S(2)}, u32[]{:S(2)}) %all-to-all-start.2) | async-done | bytes 8388640 | tf_op jit(solution)/shard_map/all_to_all | solution.py:191
  775.2 15.8 multiply_convert_fusion
  791.0 13.4 fusion.31
  804.4 12.6 add_convert_fusion
  817.0 3.7 all-to-all-start.3
  820.7 10.8 convolution_convert_fusion.2
  831.5 174.1 %all-to-all-done.3 = bf16[32,64,2048]{2,1,0:T(8,128)(2,1)} async-done(((bf16[32,64,2048]{2,1,0:T(8,128)(2,1)}), bf16[32,64,2048]{2,1,0:T(8,128)(2,1)}, u32[]{:S(2)}, u32[]{:S(2)}) %all-to-all-start.3) | async-done | bytes 8388640 | tf_op jit(solution)/shard_map/all_to_all | solution.py:209
  1005.6 3.7 all-to-all-start.1
  1009.5 25.4 %gather_fusion.1 = bf16[1024,2048]{1,0:T(8,128)(2,1)} fusion(bf16[32,64,2048]{2,1,0:T(8,128)(2,1)} %all-to-all-done.3, s32[1024]{0:T(1024)S(1)} %bitcast.242), kind=kCustom, calls=%fused_computation.1 | custom fusion | bytes 8396800 | tf_op jit(solution)/shard_map/gather | solution.py:211
  1034.8 5.1 convert_reduce_fusion
  1040.3 153.9 %all-to-all-done.1 = bf16[32,64,2048]{2,1,0:T(8,128)(2,1)} async-done(((bf16[32,64,2048]{2,1,0:T(8,128)(2,1)}), bf16[32,64,2048]{2,1,0:T(8,128)(2,1)}, u32[]{:S(2)}, u32[]{:S(2)}) %all-to-all-start.1) | async-done | bytes 8388640 | tf_op jit(solution)/shard_map/all_to_all | solution.py:172
  1194.2 25.8 %gather_fusion = bf16[1024,2048]{1,0:T(8,128)(2,1)} fusion(bf16[32,64,2048]{2,1,0:T(8,128)(2,1)} %all-to-all-done.1, s32[1024]{0:T(1024)S(1)} %bitcast.243), kind=kCustom, calls=%fused_computation | custom fusion | bytes 8396800 | tf_op jit(solution)/shard_map/gather | solution.py:175
  1220.0 6.6 fusion
  1228.0 11.7 convolution_convert_fusion.3
  1242.4 5.1 fusion.42
  1248.7 5.6 fusion.2
  1256.3 2.4 fusion.45
  1258.7 2.1 copy.106
  1260.8 10.2 reduce-scatter.21.cloned.1.call-done
  1271.1 3.0 convolution_convert_fusion.4
  1274.1 25.3 %reduce-scatter.19.cloned.1.call-done = bf16[128,512]{1,0:T(8,128)(2,1)} async-done(((bf16[512,512]{1,0:T(8,128)(2,1)}), bf16[128,512]{1,0:T(8,128)(2,1)}) %reduce-scatter.19.cloned.1.call-update) | async-done | bytes 131088
  1303.0 8.2 convolution_convert_fusion
  1312.2 3.0 convolution_multiply_fusion
  1318.0 9.4 convolution_convert_fusion.1
  1329.3 11.3 convolution_bitcast_fusion
  1340.6 11.0 convolution_bitcast_fusion.1
  1351.6 22.6 %reduce-scatter.13.cloned.1.call-done = bf16[256,512]{1,0:T(8,128)(2,1)} async-done(((bf16[2048,512]{1,0:T(8,128)(2,1)}), bf16[256,512]{1,0:T(8,128)(2,1)}) %reduce-scatter.13.cloned.1.call-update) | async-done | bytes 262160 | tf_op jit(solution)/shard_map/reduce_scatter | solution.py:317
  1374.2 169.4 %reduce-scatter.17.cloned.1.call-done = bf16[512,2048]{1,0:T(8,128)(2,1)} async-done(((bf16[4096,2048]{1,0:T(8,128)(2,1)}), bf16[512,2048]{1,0:T(8,128)(2,1)}) %reduce-scatter.17.cloned.1.call-update) | async-done | bytes 2097168 | tf_op jit(solution)/shard_map/reduce_scatter | solution.py:333
  1543.6 168.9 %reduce-scatter.11.cloned.1.call-done = bf16[256,4096]{1,0:T(8,128)(2,1)} async-done(((bf16[2048,4096]{1,0:T(8,128)(2,1)}), bf16[256,4096]{1,0:T(8,128)(2,1)}) %reduce-scatter.11.cloned.1.call-update) | async-done | bytes 2097168 | tf_op jit(solution)/shard_map/reduce_scatter | solution.py:309
  1712.5 12.1 convolution_bitcast_fusion.2
  1724.6 12.0 fusion.75
  1736.6 2.6 convolution_add_fusion.1
  1740.2 14.3 all-reduce.6
  1754.8 10.1 all-reduce.8
  1768.3 59.9 %all-reduce.12.cloned.1.call-done = (bf16[256,4096]{1,0:T(8,128)(2,1)}, bf16[256,512]{1,0:T(8,128)(2,1)}, bf16[256,512]{1,0:T(8,128)(2,1)}, bf16[512,2048]{1,0:T(8,128)(2,1)}) async-done(((bf16[256,4096]{1,0:T(8,128)(2,1)}, bf16[256,512]{1,0:T(8,128)(2,1)}, bf16[256,512]{1,0:T(8,128)(2,1)}, bf16[512,2048]{1,0:T(8,128)(2,1)}), (bf16[256,4096]{1,0:T(8,128)(2,1)}, bf16[256,512]{1,0:T(8,128)(2,1)}, ...) | async-done | bytes 4718608 | tf_op jit(solution)/shard_map/psum | solution.py:364
  1832.0 4.2 convert_element_type.285
  1836.2 2.5 convert_element_type.291
  (221 shorter events, 42.1 us)
Async XLA Ops:
  7.2 768.0 %copy-start = (bf16[1,768,2048]{2,1,0:T(8,128)(2,1)S(1)}, bf16[1,768,2048]{2,1,0:T(8,128)(2,1)}, u32[]{:S(2)}) copy-start(bf16[1,768,2048]{2,1,0:T(8,128)(2,1)} %param.26) | copy-start | bytes 9437188
  7.2 3.3 copy-start.45
  7.2 54.2 %copy-start.47 = (s32[2]{0:T(128)S(1)}, s32[2]{0:T(128)}, u32[]{:S(2)}) copy-start(s32[2]{0:T(128)} %constant.67) | copy-start | bytes 28
  7.2 54.3 %copy-start.46 = (s32[2]{0:T(128)S(1)}, s32[2]{0:T(128)}, u32[]{:S(2)}) copy-start(s32[2]{0:T(128)} %constant.70) | copy-start | bytes 28
  7.2 2.9 copy-start.44
  7.2 4.5 copy-start.51
  7.3 4.8 copy-start.52
  7.3 24.6 %copy-start.53 = (bf16[256]{0:T(256)(128)(2,1)S(1)}, bf16[256]{0:T(256)(128)(2,1)}, u32[]{:S(2)}) copy-start(bf16[256]{0:T(256)(128)(2,1)} %param.20) | copy-start | bytes 1540
  7.3 24.6 %copy-start.54 = (bf16[256]{0:T(256)(128)(2,1)S(1)}, bf16[256]{0:T(256)(128)(2,1)}, u32[]{:S(2)}) copy-start(bf16[256]{0:T(256)(128)(2,1)} %param.21) | copy-start | bytes 1540
  7.3 58.8 %all-gather.11.cloned.1.call-start = ((), (), s32[]{:S(2)}) async-start(), calls=%async_computation.12 | async-start | bytes 2359296 | tf_op jit(solution)/shard_map/all_gather | solution.py:82
  8.0 64.0 %all-gather.7.cloned.1.call-start = ((), (), s32[]{:S(2)}) async-start(), calls=%async_computation.10 | async-start | bytes 2359296 | tf_op jit(solution)/shard_map/all_gather | solution.py:81
  8.8 215.5 %all-gather.9.cloned.1.call-start = ((), (), s32[]{:S(2)}) async-start(), calls=%async_computation.11 | async-start | bytes 18874368 | tf_op jit(solution)/shard_map/all_gather | solution.py:80
  9.5 365.6 %all-gather.13.cloned.1.call-start = ((), (), s32[]{:S(2)}) async-start(), calls=%async_computation.13 | async-start | bytes 18874368 | tf_op jit(solution)/shard_map/all_gather | solution.py:83
  51.2 24.7 %copy-start.33 = (f32[8,1,256]{2,1,0:T(1,128)}, f32[8,1,256]{2,1,0:T(1,128)S(1)}, u32[]{:S(2)}) copy-start(f32[8,1,256]{2,1,0:T(1,128)S(1)} %convert_element_type.305) | copy-start | bytes 24580
  63.0 3.1 copy-start.38
  63.6 204.5 %copy-start.23 = (pred[128,512]{0,1:T(8,128)(4,1)}, pred[128,512]{0,1:T(8,128)(4,1)S(1)}, u32[]{:S(2)}) copy-start(pred[128,512]{0,1:T(8,128)(4,1)S(1)} %iota_compare_fusion) | copy-start | bytes 196612
  63.8 192.5 %copy-start.25 = (f32[128,64]{0,1:T(8,128)}, f32[128,64]{0,1:T(8,128)S(1)}, u32[]{:S(2)}) copy-start(f32[128,64]{0,1:T(8,128)S(1)} %get-tuple-element.51) | copy-start | bytes 98308
  63.9 192.5 %copy-start.27 = (f32[128,64]{0,1:T(8,128)}, f32[128,64]{0,1:T(8,128)S(1)}, u32[]{:S(2)}) copy-start(f32[128,64]{0,1:T(8,128)S(1)} %get-tuple-element.52) | copy-start | bytes 98308
  68.6 22.0 %copy-start.40 = (f32[128]{0:T(128)S(1)}, f32[128]{0:T(128)}, u32[]{:S(2)}) copy-start(f32[128]{0:T(128)} %convert_element_type.241) | copy-start | bytes 1540
  89.9 156.1 %copy-start.35 = (f32[128,4]{0,1:T(4,128)}, f32[128,4]{0,1:T(4,128)S(1)}, u32[]{:S(2)}) copy-start(f32[128,4]{0,1:T(4,128)S(1)} %add_rsqrt_fusion.1) | copy-start | bytes 6148
  246.1 9.9 copy-start.42
  254.6 3.0 copy-start.31
  266.0 3.2 copy-start.3
  266.1 3.2 copy-start.29
  397.8 3.8 copy-start.37
  397.8 188.7 %all-to-all-start = ((bf16[32,64,2048]{2,1,0:T(8,128)(2,1)}), bf16[32,64,2048]{2,1,0:T(8,128)(2,1)}, u32[]{:S(2)}, u32[]{:S(2)}) async-start(bf16[32,64,2048]{2,1,0:T(8,128)(2,1)} %bitcast.247), calls=%async_computation | async-start | bytes 16777216 | tf_op jit(solution)/shard_map/all_to_all | solution.py:165
  586.6 188.6 %all-to-all-start.2 = ((bf16[32,64,2048]{2,1,0:T(8,128)(2,1)}), bf16[32,64,2048]{2,1,0:T(8,128)(2,1)}, u32[]{:S(2)}, u32[]{:S(2)}) async-start(bf16[32,64,2048]{2,1,0:T(8,128)(2,1)} %bitcast.246), calls=%async_computation.2 | async-start | bytes 16777216 | tf_op jit(solution)/shard_map/all_to_all | solution.py:191
  590.3 11.8 copy-start.48
  775.2 15.8 copy-start.49
  791.0 13.4 copy-start.55
  791.0 13.4 copy-start.50
  817.0 188.6 %all-to-all-start.3 = ((bf16[32,64,2048]{2,1,0:T(8,128)(2,1)}), bf16[32,64,2048]{2,1,0:T(8,128)(2,1)}, u32[]{:S(2)}, u32[]{:S(2)}) async-start(bf16[32,64,2048]{2,1,0:T(8,128)(2,1)} %add_convert_fusion), calls=%async_computation.3 | async-start | bytes 16777216 | tf_op jit(solution)/shard_map/all_to_all | solution.py:209
  831.5 178.0 %copy-start.2 = (s32[1024,1]{0,1:T(1,128)S(1)}, s32[1024,1]{0,1:T(1,128)}, u32[]{:S(2)}) copy-start(s32[1024,1]{0,1:T(1,128)} %get-tuple-element.48) | copy-start | bytes 12292
  1005.6 188.6 %all-to-all-start.1 = ((bf16[32,64,2048]{2,1,0:T(8,128)(2,1)}), bf16[32,64,2048]{2,1,0:T(8,128)(2,1)}, u32[]{:S(2)}, u32[]{:S(2)}) async-start(bf16[32,64,2048]{2,1,0:T(8,128)(2,1)} %convolution_convert_fusion.2), calls=%async_computation.1 | async-start | bytes 16777216 | tf_op jit(solution)/shard_map/all_to_all | solution.py:172
  1009.3 261.8 %reduce-scatter.21.cloned.1.call-start = ((), (), s32[]{:S(2)}) async-start(), calls=%async_computation.19 | async-start | bytes 655360 | tf_op jit(solution)/shard_map/convert_element_type | solution.py:288
  1034.8 5.1 copy-start.11
  1219.9 6.6 copy-start.21
  1228.0 75.0 %copy-start.8 = (f32[128,2048]{1,0:T(8,128)}, f32[128,2048]{1,0:T(8,128)S(1)}, u32[]{:S(2)}) copy-start(f32[128,2048]{1,0:T(8,128)S(1)} %get-tuple-element.42) | copy-start | bytes 3145732
  1239.7 2.7 copy-start.24
  1248.6 7.7 copy-start.14
  1248.6 50.8 %reduce-scatter.19.cloned.1.call-start = ((), (), s32[]{:S(2)}) async-start(), calls=%async_computation.18 | async-start | bytes 655360
  1248.7 7.6 copy-start.15
  1256.3 14.8 copy-start.7
  1258.7 41.8 %copy-start.26 = (f32[128,64]{0,1:T(8,128)S(1)}, f32[128,64]{0,1:T(8,128)}, u32[]{:S(2)}) copy-start(f32[128,64]{0,1:T(8,128)} %copy-done.25) | copy-start | bytes 98308
  1258.7 41.8 %copy-start.28 = (f32[128,64]{0,1:T(8,128)S(1)}, f32[128,64]{0,1:T(8,128)}, u32[]{:S(2)}) copy-start(f32[128,64]{0,1:T(8,128)} %copy-done.27) | copy-start | bytes 98308
  1258.7 41.8 %copy-start.20 = (f32[128,4,128]{0,2,1:T(8,128)S(1)}, f32[128,4,128]{0,2,1:T(8,128)}, u32[]{:S(2)}) copy-start(f32[128,4,128]{0,2,1:T(8,128)} %copy-done.19) | copy-start | bytes 786436
  1258.7 41.9 %copy-start.36 = (f32[128,4]{0,1:T(4,128)S(1)}, f32[128,4]{0,1:T(4,128)}, u32[]{:S(2)}) copy-start(f32[128,4]{0,1:T(4,128)} %copy-done.35) | copy-start | bytes 6148
  1258.7 41.9 %copy-start.41 = (f32[128]{0:T(128)S(1)}, f32[128]{0:T(128)}, u32[]{:S(2)}) copy-start(f32[128]{0:T(128)} %convert_element_type.241) | copy-start | bytes 1540
  1260.8 90.8 %reduce-scatter.15.cloned.1.call-start = ((), (), s32[]{:S(2)}) async-start(), calls=%async_computation.16 | async-start | bytes 2359296 | tf_op jit(solution)/shard_map/reduce_scatter | solution.py:325
  1274.0 28.9 %copy-start.17 = (bf16[128,4,8,128]{0,3,2,1:T(8,128)(2,1)S(1)}, bf16[128,4,8,128]{0,3,2,1:T(8,128)(2,1)}, u32[]{:S(2)}) copy-start(bf16[128,4,8,128]{0,3,2,1:T(8,128)(2,1)} %get-tuple-element.61) | copy-start | bytes 3145732
  1274.1 100.2 %reduce-scatter.13.cloned.1.call-start = ((), (), s32[]{:S(2)}) async-start(), calls=%async_computation.15 | async-start | bytes 2359296 | tf_op jit(solution)/shard_map/reduce_scatter | solution.py:317
  1302.9 240.7 %reduce-scatter.17.cloned.1.call-start = ((), (), s32[]{:S(2)}) async-start(), calls=%async_computation.17 | async-start | bytes 18874368 | tf_op jit(solution)/shard_map/reduce_scatter | solution.py:333
  1311.2 4.3 copy-start.5
  1311.2 4.3 copy-start.32
  1311.2 4.3 copy-start.43
  1311.2 401.2 %reduce-scatter.11.cloned.1.call-start = ((), (), s32[]{:S(2)}) async-start(), calls=%async_computation.14 | async-start | bytes 18874368 | tf_op jit(solution)/shard_map/reduce_scatter | solution.py:309
  1327.4 500.8 %all-reduce.12.cloned.1.call-start = ((), (), s32[]{:S(2)}) async-start(), calls=%async_computation.20 | async-start | bytes 9437184 | tf_op jit(solution)/shard_map/psum | solution.py:364
  1329.3 11.3 copy-start.57
  1712.4 12.1 copy-start.13
  1724.6 14.6 copy-start.34
  1724.6 14.6 copy-start.39
  1736.6 30.5 %copy-start.9 = (f32[128,2048]{1,0:T(8,128)S(1)}, f32[128,2048]{1,0:T(8,128)}, u32[]{:S(2)}) copy-start(f32[128,2048]{1,0:T(8,128)} %copy-done.8) | copy-start | bytes 3145732
  1828.2 8.0 copy-start.22
  1832.0 6.8 copy-start.1
  (9 other events, 16.0 us)
Sparse Core Ops, SparseCore 0:
  9.7 31.9 all-gather.10
  43.3 28.6 all-gather.6
  73.6 150.5 all-gather.8
  225.7 149.3 all-gather.12
  1248.7 22.3 reduce-scatter.20
  1274.6 24.7 reduce-scatter.18
  1301.7 35.7 reduce-scatter.14
  1339.7 34.4 reduce-scatter.12
  1376.6 166.9 reduce-scatter.16
  1545.8 166.6 reduce-scatter.10
  1716.2 111.9 all-reduce.11
where the time goes:
time: 1850 us
  waiting for transfers between devices  1350 us (73%)
  matrix products  205 us (11%)
  local copies, waits for them, and re-layouts  109 us (6%)
  blocking collectives  83.8 us (5%)
  other arithmetic  65 us (4%)
    all_to_all x1, waiting for transfers between devices, on_device(): lax.all_to_all(d_rows, ('ctx', 'wa'), split_axis=0, concat_axis=0, tiled=...  174 us
    all_to_all x1, waiting for transfers between devices, on_device(): lax.all_to_all(outgoing, ('ctx', 'wa'), split_axis=0, concat_axis=0, tile...  172 us
    reduce_scatter x1, waiting for transfers between devices, on_device(): lax.psum_scatter(jnp.dot(attended_output.T, d_out, preferred_element_type...  169 us
    reduce_scatter x1, waiting for transfers between devices, on_device(): lax.psum_scatter(jnp.dot(normalized_input.T, d_query_b, preferred_element...  169 us
    all_to_all x1, waiting for transfers between devices, on_device(): lax.all_to_all(outgoing_grad, ('ctx', 'wa'), split_axis=0, concat_axis=0,...  162 us
    all_to_all x1, waiting for transfers between devices, on_device(): lax.all_to_all(produced, ('ctx', 'wa'), split_axis=0, concat_axis=0, tile...  154 us
    all_gather x1, waiting for transfers between devices, on_device(): lax.all_gather(query_weight, 'wa', axis=0, tiled=True)  123 us
    all_gather x1, waiting for transfers between devices, on_device(): lax.all_gather(output_weight, 'wa', axis=0, tiled=True)  102 us
  transfers between devices with their start and end apart: 15, of which 13 were waited for; matrix products, arithmetic and copies ran while one was open for 13% of the time, Pallas kernels for 0%

commit v1 on v0

v1 whole, which is shorter than its diff:
```python
import jax
import jax.numpy as jnp
from jax import lax
from jax.sharding import PartitionSpec as P

MODEL_WIDTH = 2048
QUERY_HEADS = 32
KEY_VALUE_HEADS = 4
HEAD_SIZE = 128
TOP = 8

EPSILON = 1e-06
ROPE_BASE = 1000000.0
VERY_NEGATIVE = -1e30
EVERY = ("ctx", "wa")


def inv_root(values):
    return lax.rsqrt(jnp.mean(values * values, axis=-1, keepdims=True) + EPSILON)


def rope_tables(positions):
    half_width = HEAD_SIZE // 2
    frequency = ROPE_BASE ** (-(jnp.arange(half_width).astype(positions.dtype) * 2.0 / HEAD_SIZE))
    angles = positions[:, None] * frequency[None, :]
    cosine, sine = jnp.cos(angles), jnp.sin(angles)
    return (
        jnp.concatenate([cosine, cosine], axis=-1),
        jnp.concatenate([-sine, sine], axis=-1),
    )


def swap_halves(values):
    half_width = values.shape[-1] // 2
    return jnp.concatenate([values[..., half_width:], values[..., :half_width]], axis=-1)


def rotate(values, cosine, sine):
    return values * cosine + swap_halves(values) * sine


def unrotate(values, cosine, sine):
    return values * cosine - swap_halves(values) * sine


def dot(a, b, contract):
    return lax.dot_general(a, b, (contract, ((), ())), preferred_element_type=jnp.float32)


def on_device(
    block_input,
    query_weight,
    key_projection_matrix,
    value_projection_matrix,
    output_weight,
    attention_gain,
    feedforward_gain,
    query_gain,
    key_gain,
    expert_gate,
    expert_up,
    expert_down,
    expert_ids,
    route_gates,
    cotangent,
):
    bf16, f32 = jnp.bfloat16, jnp.float32
    n_ctx, n_wa = lax.axis_size("ctx"), lax.axis_size("wa")
    my_ctx, my_wa = lax.axis_index("ctx"), lax.axis_index("wa")
    experts = n_ctx * n_wa
    block_rows = block_input[0]
    rows = block_rows.shape[0]
    length = rows * n_ctx
    capacity = 2 * rows * TOP // experts
    heads = QUERY_HEADS // n_ctx
    per_group = QUERY_HEADS // KEY_VALUE_HEADS
    sharers = per_group // heads
    head_columns = heads * HEAD_SIZE
    out_columns = MODEL_WIDTH // n_ctx
    score_scale = HEAD_SIZE ** (-0.5)

    gains = [attention_gain, feedforward_gain, query_gain, key_gain]
    small = jnp.concatenate(
        [expert_ids[0].astype(bf16).reshape(-1), route_gates[0].reshape(-1)] + gains
    )
    small = lax.all_gather(small, EVERY, axis=0)
    ids_all = small[:, : rows * TOP].reshape(experts, rows, TOP)
    gates_all = small[:, rows * TOP : 2 * rows * TOP].reshape(experts, rows, TOP)
    at = 2 * rows * TOP
    full_gains = []
    for g in gains:
        width = g.shape[0]
        full_gains.append(small[:n_wa, at : at + width].reshape(-1).astype(f32))
        at += width
    gain_attention, gain_feedforward, gain_query, gain_key = full_gains

    group = my_ctx * heads // per_group
    my_query = lax.dynamic_slice_in_dim(query_weight, my_ctx * head_columns, head_columns, 1)
    my_key = lax.dynamic_slice_in_dim(key_projection_matrix, group * HEAD_SIZE, HEAD_SIZE, 1)
    my_value = lax.dynamic_slice_in_dim(value_projection_matrix, group * HEAD_SIZE, HEAD_SIZE, 1)
    my_out = lax.dynamic_slice_in_dim(output_weight, my_ctx * out_columns, out_columns, 1)
    full_qkv = lax.all_gather(
        jnp.concatenate([my_query, my_key, my_value], axis=1), "wa", axis=0, tiled=True
    )
    full_out = lax.all_gather(my_out, "wa", axis=0, tiled=True)

    out_cotangent = cotangent[0]
    cot_all = lax.all_gather(out_cotangent.astype(bf16), EVERY, axis=0)

    root_x = inv_root(block_rows)
    x_hat = block_rows * root_x
    normed = (x_hat * gain_attention).astype(bf16)
    normed_all = lax.all_gather(normed, "ctx", axis=0, tiled=True)
    cosine, sine = rope_tables(jnp.arange(length, dtype=jnp.int32).astype(f32))
    qkv = dot(normed_all, full_qkv, ((1,), (0,)))
    query = qkv[:, :head_columns].reshape(length, heads, HEAD_SIZE).transpose(1, 0, 2)
    key_raw = qkv[:, head_columns : head_columns + HEAD_SIZE]
    value = qkv[:, head_columns + HEAD_SIZE :].astype(bf16)
    root_q = inv_root(query)
    q_hat = query * root_q
    root_k = inv_root(key_raw)
    k_hat = key_raw * root_k
    q_rot = rotate(q_hat * gain_query, cosine, sine).astype(bf16)
    k_rot = rotate(k_hat * gain_key, cosine, sine).astype(bf16)
    positions = jnp.arange(length, dtype=jnp.int32)
    allowed = positions[:, None] >= positions[None, :]
    scores = jnp.einsum("hqd,kd->hqk", q_rot, k_rot, preferred_element_type=f32) * score_scale
    masked = jnp.where(allowed, scores, VERY_NEGATIVE)
    top = jnp.max(masked, axis=-1, keepdims=True)
    weights = jnp.exp(masked - top)
    total = jnp.sum(weights, axis=-1, keepdims=True)
    attended = (
        jnp.einsum("hqk,kd->hqd", weights.astype(bf16), value, preferred_element_type=f32) / total
    ).astype(bf16)
    lse = top + jnp.log(total)
    attended_rows = attended.transpose(1, 0, 2).reshape(length, head_columns)
    attended_all = lax.all_gather(attended_rows, "ctx", axis=0)
    out_part = jnp.einsum(
        "ctk,ckn->tn",
        attended_all,
        full_out.reshape(n_ctx, head_columns, out_columns),
        preferred_element_type=f32,
    ).astype(bf16)
    out_rows = lax.all_to_all(
        out_part.reshape(n_ctx, rows, out_columns), "ctx", split_axis=0, concat_axis=0, tiled=True
    )
    hidden = block_rows + out_rows.transpose(1, 0, 2).reshape(rows, MODEL_WIDTH).astype(f32)

    root_h = inv_root(hidden)
    h_hat = hidden * root_h
    ffn_in = (h_hat * gain_feedforward).astype(bf16)
    ffn_all = lax.all_gather(ffn_in, EVERY, axis=0)
    me = (my_ctx * n_wa + my_wa).astype(bf16)
    mine = ids_all == me
    hit = jnp.any(mine, axis=-1)
    gate_of = jnp.sum(jnp.where(mine, gates_all.astype(f32), 0.0), axis=-1)
    token = jnp.arange(rows, dtype=jnp.int32)
    before = (token[:, None] < token[None, :]).astype(bf16)
    rank = dot(hit.astype(bf16), before, ((1,), (0,))).astype(jnp.int32)
    slot = jnp.arange(capacity, dtype=jnp.int32)
    chosen = (rank[:, None, :] == slot[None, :, None]) & hit[:, None, :]
    pick = chosen.astype(bf16)
    pick_gate = jnp.where(chosen, gate_of[:, None, :], 0.0).astype(bf16)
    gate_w, up_w, down_w = expert_gate[0], expert_up[0], expert_down[0]

    def to_slots(one_hot, values):
        return (
            jnp.einsum("bst,btd->bsd", one_hot, values, preferred_element_type=f32)
            .astype(bf16)
            .reshape(experts * capacity, MODEL_WIDTH)
        )

    def to_tokens(one_hot, values):
        return (
            jnp.einsum(
                "bst,bsd->btd",
                one_hot,
                values.reshape(experts, capacity, MODEL_WIDTH),
                preferred_element_type=f32,
            )
            .astype(bf16)
            .reshape(experts * rows, MODEL_WIDTH)
        )

    down_grad = to_slots(pick_gate, cot_all)
    arrived = to_slots(pick, ffn_all)
    gate_pre = dot(arrived, gate_w, ((1,), (0,)))
    up_pre = dot(arrived, up_w, ((1,), (0,)))
    sigmoid_gate = jax.nn.sigmoid(gate_pre)
    activated = gate_pre * sigmoid_gate
    middle = (activated * up_pre).astype(bf16)
    d_middle = dot(down_grad, down_w, ((1,), (1,)))
    d_gate_pre = (
        d_middle * up_pre * sigmoid_gate * (1.0 + gate_pre * (1.0 - sigmoid_gate))
    ).astype(bf16)
    d_up_pre = (d_middle * activated).astype(bf16)
    d_rows = (
        dot(d_gate_pre, gate_w, ((1,), (1,))) + dot(d_up_pre, up_w, ((1,), (1,)))
    ).astype(bf16)
    d_ffn = lax.psum_scatter(
        to_tokens(pick, d_rows), EVERY, scatter_dimension=0, tiled=True
    ).astype(f32)
    produced = dot(middle, down_w, ((1,), (0,))).astype(bf16)
    mixture = lax.psum_scatter(
        to_tokens(pick_gate, produced), EVERY, scatter_dimension=0, tiled=True
    ).astype(f32)
    block_output = hidden + mixture
    grad_down = dot(middle, down_grad, ((0,), (0,)))
    grad_gate = dot(arrived, d_gate_pre, ((0,), (0,)))
    grad_up = dot(arrived, d_up_pre, ((0,), (0,)))

    grad_feedforward = jnp.sum(d_ffn * h_hat, axis=0)
    grad_hat = d_ffn * gain_feedforward
    d_hidden = out_cotangent + root_h * (
        grad_hat - h_hat * jnp.mean(grad_hat * h_hat, axis=-1, keepdims=True)
    )
    d_out = lax.all_gather(d_hidden.astype(bf16), "ctx", axis=0, tiled=True)
    out_by_rows = lax.all_to_all(
        full_out.reshape(n_ctx, head_columns, out_columns),
        "ctx",
        split_axis=0,
        concat_axis=0,
        tiled=True,
    )
    d_attended = jnp.einsum(
        "tcn,ckn->tk",
        d_out.reshape(length, n_ctx, out_columns),
        out_by_rows,
        preferred_element_type=f32,
    ).astype(bf16)
    d_attended = d_attended.reshape(length, heads, HEAD_SIZE).transpose(1, 0, 2)
    delta = jnp.sum(d_attended.astype(f32) * attended.astype(f32), axis=-1, keepdims=True)
    scores = jnp.einsum("hqd,kd->hqk", q_rot, k_rot, preferred_element_type=f32) * score_scale
    probs = jnp.where(allowed, jnp.exp(scores - lse), 0.0)
    d_prob = jnp.einsum("hqd,kd->hqk", d_attended, value, preferred_element_type=f32)
    d_round = (probs * (d_prob - delta)).astype(bf16)
    d_value = jnp.einsum("hqk,hqd->kd", probs.astype(bf16), d_attended, preferred_element_type=f32)
    d_krot = jnp.einsum("hqk,hqd->kd", d_round, q_rot, preferred_element_type=f32) * score_scale
    d_qrot = jnp.einsum("hqk,kd->hqd", d_round, k_rot, preferred_element_type=f32) * score_scale
    d_qn = unrotate(d_qrot, cosine, sine)
    d_kn = unrotate(d_krot, cosine, sine)
    grad_qgain = jnp.sum(d_qn * q_hat, axis=(0, 1))
    grad_kgain = jnp.sum(d_kn * k_hat, axis=0)
    grad_q = d_qn * gain_query
    d_query = root_q * (grad_q - q_hat * jnp.mean(grad_q * q_hat, axis=-1, keepdims=True))
    grad_k = d_kn * gain_key
    d_key = root_k * (grad_k - k_hat * jnp.mean(grad_k * k_hat, axis=-1, keepdims=True))
    d_query = d_query.astype(bf16).transpose(1, 0, 2).reshape(length, head_columns)
    d_qkv = jnp.concatenate([d_query, d_key.astype(bf16), d_value.astype(bf16)], axis=1)
    d_normed = lax.psum_scatter(
        dot(d_qkv, full_qkv, ((1,), (1,))).astype(bf16), "ctx", scatter_dimension=0, tiled=True
    ).astype(f32)
    grad_attention = jnp.sum(d_normed * x_hat, axis=0)
    grad_n = d_normed * gain_attention
    input_grad = d_hidden + root_x * (
        grad_n - x_hat * jnp.mean(grad_n * x_hat, axis=-1, keepdims=True)
    )

    my_d_out = lax.dynamic_slice_in_dim(d_out, my_ctx * out_columns, out_columns, 1)
    grad_out = jnp.einsum("ctk,tn->ckn", attended_all, my_d_out, preferred_element_type=f32)
    grad_out = lax.psum_scatter(
        grad_out.astype(bf16).reshape(-1, out_columns), "wa", scatter_dimension=0, tiled=True
    )
    grad_out = lax.all_gather(grad_out, "ctx", axis=0)
    grad_out = grad_out.transpose(1, 0, 2).reshape(-1, MODEL_WIDTH).astype(f32)
    grad_qkv = dot(normed_all, d_qkv, ((0,), (0,))).astype(bf16)
    grad_qkv = lax.psum_scatter(grad_qkv, "wa", scatter_dimension=0, tiled=True)
    grad_qkv = lax.all_gather(grad_qkv, "ctx", axis=0).astype(f32)
    share = grad_qkv.shape[1]
    grad_query = (
        grad_qkv[:, :, :head_columns].transpose(1, 0, 2).reshape(share, QUERY_HEADS * HEAD_SIZE)
    )
    by_group = grad_qkv[:, :, head_columns:].reshape(
        KEY_VALUE_HEADS, sharers, share, 2, HEAD_SIZE
    )
    by_group = jnp.sum(by_group, axis=1)
    grad_key = by_group[:, :, 0].transpose(1, 0, 2).reshape(share, KEY_VALUE_HEADS * HEAD_SIZE)
    grad_value = by_group[:, :, 1].transpose(1, 0, 2).reshape(share, KEY_VALUE_HEADS * HEAD_SIZE)
    sums = lax.psum(
        jnp.concatenate([grad_attention, grad_feedforward, grad_qgain, grad_kgain]), EVERY
    )
    gain_grads, at = [], 0
    for g in gains:
        width = g.shape[0]
        gain_grads.append(lax.dynamic_slice_in_dim(sums, at + my_wa * width, width, 0))
        at += width * n_wa
    return (
        block_output[None],
        input_grad[None],
        grad_query,
        grad_key,
        grad_value,
        grad_out,
        *gain_grads,
        grad_gate[None],
        grad_up[None],
        grad_down[None],
    )


def solution(mesh):
    by_row, by_expert = P("wa", None), P(EVERY, None, None)
    tokens = P("wa", "ctx", None)
    gain = P("wa")
    in_specs = (
        (tokens,)
        + (by_row,) * 4
        + (gain,) * 4
        + (by_expert,) * 3
        + (tokens,) * 3
    )
    out_specs = (tokens,) * 2 + (by_row,) * 4 + (gain,) * 4 + (by_expert,) * 3
    return jax.shard_map(
        on_device, mesh=mesh, in_specs=in_specs, out_specs=out_specs, check_vma=False
    )
```

time: 1850 us -> 1380 us (0.75)
  waiting for transfers between devices: 1350 us -> 962 us
  blocking collectives: 83.8 us -> 41.9 us
  local copies, waits for them, and re-layouts: 109 us -> 70.7 us
    all_to_all x4 -> x2, waiting for transfers between devices: 663 us -> 12 us  [the longest x1 12 us: on_device(): lax.all_to_all(out_part.reshape(n_ctx, rows, out_columns), 'ctx', split_a...]
    all_gather x4 -> x9, waiting for transfers between devices: 229 us -> 461 us  [the longest x1 105 us: on_device(): ffn_all = lax.all_gather(ffn_in, EVERY, axis=0)]
    unnamed x12 -> x16, waiting for transfers between devices: 28 us -> 125 us
    psum x1 -> x0, waiting for transfers between devices: 59.9 us -> none  [on_device(): lax.psum(share_query.astype(jnp.bfloat16), 'ctx').astype(jnp.float32)]
    gather x2 -> x0, local copies, waits for them, and re-layouts: 51.1 us -> none  [the longest x1 25.8 us: on_device(): picked = returned[routes, slot_index].astype(jnp.float32)]
    all_gather x4 -> x0, blocking collectives: 40.9 us -> none  [the longest x1 11.5 us: on_device(): value_piece = lax.all_gather(value_matrix_rows, 'ctx', axis=0, tiled=True)]
    unnamed x2 -> x0, blocking collectives: 32.8 us -> none
    psum x1, blocking collectives: 10.1 us -> 41.9 us  [on_device(): lax.psum(jnp.concatenate([grad_attention, grad_feedforward, grad_qgain, g...]
  transfers between devices with their start and end apart: 15 -> 17, of which waited for: 13 -> 15; matrix products, arithmetic and copies ran while one was open for 13% -> 15% of each run, Pallas kernels for 0% -> 0%
where the time goes in v1:
time: 1380 us; the launch traced here: 1370 us
  waiting for transfers between devices  962 us (70%)
  matrix products  213 us (15%)
  local copies, waits for them, and re-layouts  70.7 us (5%)
  other arithmetic  52.6 us (4%)
  blocking collectives  41.9 us (3%)
  between operations  15.3 us (1%)
    reduce_scatter x1, waiting for transfers between devices, on_device(): lax.psum_scatter(to_tokens(pick, d_rows), EVERY, scatter_dimension=0, til...  185 us
    reduce_scatter x1, waiting for transfers between devices, on_device(): lax.psum_scatter(to_tokens(pick_gate, produced), EVERY, scatter_dimension...  145 us
    unnamed x16, waiting for transfers between devices  125 us
    dot_general x13, matrix products, dot(): lax.dot_general(a, b, (contract, ((), ())), preferred_element_type=jnp.fl...  125 us
    all_gather x1, waiting for transfers between devices, on_device(): ffn_all = lax.all_gather(ffn_in, EVERY, axis=0)  105 us
    all_gather x1, waiting for transfers between devices, on_device(): cot_all = lax.all_gather(out_cotangent.astype(bf16), EVERY, axis=0)  75.8 us
    all_gather x1, waiting for transfers between devices, on_device(): d_out = lax.all_gather(d_hidden.astype(bf16), 'ctx', axis=0, tiled=True)  60.7 us
    all_gather x1, waiting for transfers between devices, on_device(): lax.all_gather(jnp.concatenate([my_query, my_key, my_value], axis=1), 'wa...  58.3 us
  transfers between devices with their start and end apart: 17, of which 15 were waited for; matrix products, arithmetic and copies ran while one was open for 15% of the time, Pallas kernels for 0%

profile of v1, /device:TPU:0, one launch (start us, length us, event | category | flops | bytes accessed | tf_op | source)
XLA Modules:
  0.0 1365.4 jit_solution(2763674591959409322)
XLA Ops:
  9.2 2.8 concatenate.30
  14.5 124.3 %all-reduce.3.cloned.1.call-done = bf16[82944]{0:T(1024)(128)(2,1)} async-done(((bf16[82944]{0:T(1024)(128)(2,1)}), bf16[82944]{0:T(1024)(128)(2,1)}) %all-reduce.3.cloned.1.call-update) | async-done | bytes 165904
  141.2 2.2 multiply_convert_fusion.6
  151.3 29.5 %all-gather.13.cloned.1.call-done = bf16[512,2048]{1,0:T(8,128)(2,1)} async-done(((bf16[128,2048]{1,0:T(8,128)(2,1)}), bf16[512,2048]{1,0:T(8,128)(2,1)}) %all-gather.13.cloned.1.call-update) | async-done | bytes 2097168 | tf_op jit(solution)/shard_map/all_gather | solution.py:113
  180.8 58.3 %all-gather.15.cloned.1.call-done = bf16[2048,1280]{1,0:T(8,128)(2,1)} async-done(((bf16[256,1280]{1,0:T(8,128)(2,1)}), bf16[2048,1280]{1,0:T(8,128)(2,1)}) %all-gather.15.cloned.1.call-update) | async-done | bytes 5242896 | tf_op jit(solution)/shard_map/all_gather | solution.py:102
  239.1 6.0 fusion.92
  252.1 3.0 copy.156
  255.1 2.1 multiply_reduce_fusion.3
  264.6 4.8 fusion.23
  269.4 2.3 copy.120
  272.2 2.1 convert_element_type.261
  274.4 12.7 all-gather.19.cloned.1.call-done
  287.1 53.7 %all-gather.17.cloned.1.call-done = bf16[4,512,1024]{2,1,0:T(8,128)(2,1)} async-done(((bf16[1,512,1024]{2,1,0:T(8,128)(2,1)}), bf16[4,512,1024]{2,1,0:T(8,128)(2,1)}) %all-gather.17.cloned.1.call-update) | async-done | bytes 4194320 | tf_op jit(solution)/shard_map/all_gather | solution.py:137
  340.8 6.6 fusion.24
  347.4 4.1 all-to-all-start
  351.6 12.0 all-to-all-done
  363.6 2.3 convert_bitcast_fusion.1
  367.6 2.9 reshape.246
  371.9 2.3 multiply_reduce_fusion.4
  380.9 1.9 copy.124
  386.4 75.8 %all-gather.23.cloned.1.call-done = bf16[32,128,2048]{2,1,0:T(8,128)(2,1)} async-done(((bf16[1,128,2048]{2,1,0:T(8,128)(2,1)}), bf16[32,128,2048]{2,1,0:T(8,128)(2,1)}) %all-gather.23.cloned.1.call-update) | async-done | bytes 16777232 | tf_op jit(solution)/shard_map/all_gather | solution.py:108
  462.3 11.4 convolution_convert_fusion.4
  473.7 105.3 %all-gather.21.cloned.1.call-done = bf16[32,128,2048]{2,1,0:T(8,128)(2,1)} async-done(((bf16[1,128,2048]{2,1,0:T(8,128)(2,1)}), bf16[32,128,2048]{2,1,0:T(8,128)(2,1)}) %all-gather.21.cloned.1.call-update) | async-done | bytes 16777232 | tf_op jit(solution)/shard_map/all_gather | solution.py:152
  579.0 11.5 convolution_convert_fusion.5
  590.5 12.0 fusion.14
  602.5 8.5 fusion.18
  611.0 13.9 %multiply_convert_fusion.1 = (bf16[2048,768]{1,0:T(8,128)(2,1)}, bf16[2048,768]{1,0:T(8,128)(2,1)}, bf16[2048,768]{1,0:T(8,128)(2,1)}) fusion(f32[2048,768]{1,0:T(8,128)} %fusion.18, f32[2048,768]{1,0:T(8,128)} %fusion.14, bf16[2048,2048]{1,0:T(8,128)(2,1)S(1)} %bitcast.194, bf16[1,768,2048]{2,1,0:T(8,128)(2,1)S(1)} %copy-done), kind=kOutput, calls=%fused_computation.12 | convolution fusion | flops 6466043904 | bytes 33554432 | tf_op jit(solution)/shard_map/dot_general | solution.py:47
  624.9 12.7 fusion.16
  637.6 12.7 add_convert_fusion
  650.3 13.7 %convolution_convert_fusion = bf16[32,128,2048]{2,1,0:T(8,128)(2,1)} fusion(bf16[32,64,2048]{2,1,0:T(8,128)(2,1)} %bitcast.190, s32[32,128]{1,0:T(8,128)S(1)} %convolution_convert_fusion.8, pred[32,128]{1,0:T(8,128)(4,1)S(1)} %copy.123), kind=kOutput, calls=%fused_computation.1 | convolution fusion | flops 1082654720 | bytes 25186304 | tf_op jit(solution)/shard_map/bst,bsd->btd/dot_general | solution.py:175
  664.1 184.9 %reduce-scatter.8.cloned.1.call-done = bf16[128,2048]{1,0:T(8,128)(2,1)} async-done(((bf16[4096,2048]{1,0:T(8,128)(2,1)}), bf16[128,2048]{1,0:T(8,128)(2,1)}) %reduce-scatter.8.cloned.1.call-update) | async-done | bytes 524304 | tf_op jit(solution)/shard_map/reduce_scatter | solution.py:200
  849.0 2.4 fusion.43
  851.4 2.8 fusion.82
  854.3 4.9 all-to-all-start.1
  859.2 60.7 %all-gather.25.cloned.1.call-done = bf16[512,2048]{1,0:T(8,128)(2,1)} async-done(((bf16[128,2048]{1,0:T(8,128)(2,1)}), bf16[512,2048]{1,0:T(8,128)(2,1)}) %all-gather.25.cloned.1.call-update) | async-done | bytes 2097168 | tf_op jit(solution)/shard_map/all_gather | solution.py:217
  920.0 6.7 convolution_convert_fusion.7
  928.6 4.3 copy.127
  932.9 6.2 bitcast_convert_fusion
  939.1 2.3 copy.129
  941.4 2.3 multiply_reduce_fusion.2
  943.7 5.1 multiply_convert_fusion
  956.2 3.3 broadcast_multiply_fusion
  964.5 1.9 fusion.33
  967.1 4.8 convolution_convert_fusion.2
  972.9 7.1 convolution_convert_fusion.6
  980.1 10.9 convolution_convert_fusion.3
  991.0 13.8 %convolution_convert_fusion.1 = bf16[32,128,2048]{2,1,0:T(8,128)(2,1)} fusion(bf16[32,64,2048]{2,1,0:T(8,128)(2,1)} %bitcast.189, bf16[32,128]{1,0:T(8,128)(2,1)S(1)} %copy-done.33, s32[32,128]{1,0:T(8,128)S(1)} %convolution_convert_fusion.8, pred[32,128]{1,0:T(8,128)(4,1)S(1)} %copy-done.29), kind=kOutput, calls=%fused_computation.2 | convolution fusion | flops 1082916864 | bytes 25194496 | tf_op jit(solution)/shard_map/bst,bsd->btd/dot_general | solution.py:175
  1005.5 12.2 convolution_bitcast_fusion.1
  1017.7 20.0 %reduce-scatter.12.cloned.1.call-done = bf16[256,1280]{1,0:T(8,128)(2,1)} async-done(((bf16[2048,1280]{1,0:T(8,128)(2,1)}), bf16[256,1280]{1,0:T(8,128)(2,1)}) %reduce-scatter.12.cloned.1.call-update) | async-done | bytes 655376 | tf_op jit(solution)/shard_map/reduce_scatter | solution.py:267
  1037.7 11.9 convolution_bitcast_fusion
  1049.7 11.2 convolution_bitcast_fusion.2
  1060.8 13.8 %reduce-scatter.10.cloned.1.call-done = bf16[128,2048]{1,0:T(8,128)(2,1)} async-done(((bf16[512,2048]{1,0:T(8,128)(2,1)}), bf16[128,2048]{1,0:T(8,128)(2,1)}) %reduce-scatter.10.cloned.1.call-update) | async-done | bytes 524304 | tf_op jit(solution)/shard_map/reduce_scatter | solution.py:250
  1076.5 41.9 %psum.7 = f32[4352]{0:T(1024)S(1)} all-reduce(f32[4352]{0:T(1024)S(1)} %pad_maximum_fusion.6), channel_id=1, replica_groups=mesh['ctx'=4,'wa'=8] {'ctx','wa'}, use_global_device_ids=true, to_apply=%region_22.23 | all-reduce | flops 4352 | bytes 34816 | tf_op jit(solution)/shard_map/psum | solution.py:279
  1119.5 145.2 %reduce-scatter.6.cloned.1.call-done = bf16[128,2048]{1,0:T(8,128)(2,1)} async-done(((bf16[4096,2048]{1,0:T(8,128)(2,1)}), bf16[128,2048]{1,0:T(8,128)(2,1)}) %reduce-scatter.6.cloned.1.call-update) | async-done | bytes 524304 | tf_op jit(solution)/shard_map/reduce_scatter | solution.py:204
  1264.7 4.1 fusion.39
  1268.8 30.8 %all-gather.29.cloned.1.call-done = bf16[2048,512]{1,0:T(8,128)(2,1)} async-done(((bf16[512,512]{1,0:T(8,128)(2,1)}), bf16[2048,512]{1,0:T(8,128)(2,1)}) %all-gather.29.cloned.1.call-update) | async-done | bytes 2097168 | tf_op jit(solution)/shard_map/all_gather | solution.py:264
  1299.6 3.2 copy.143
  1302.8 4.0 copy.168
  1306.8 34.3 %all-gather.27.cloned.1.call-done = bf16[1024,1280]{1,0:T(8,128)(2,1)} async-done(((bf16[256,1280]{1,0:T(8,128)(2,1)}), bf16[1024,1280]{1,0:T(8,128)(2,1)}) %all-gather.27.cloned.1.call-update) | async-done | bytes 2621456 | tf_op jit(solution)/shard_map/all_gather | solution.py:268
  1341.1 2.1 slice.103
  1343.2 4.5 convert.15
  1347.8 2.7 reduce_sum.152
  1350.5 2.6 fusion.87
  1356.1 2.3 copy.163
  (253 shorter events, 65.4 us)
Async XLA Ops:
  7.2 603.8 %copy-start = (bf16[1,768,2048]{2,1,0:T(8,128)(2,1)S(1)}, bf16[1,768,2048]{2,1,0:T(8,128)(2,1)}, u32[]{:S(2)}) copy-start(bf16[1,768,2048]{2,1,0:T(8,128)(2,1)} %param.26) | copy-start | bytes 9437188
  7.2 131.5 %all-reduce.3.cloned.1.call-start = ((), (), s32[]{:S(2)}) async-start(), calls=%async_computation.21 | async-start | bytes 331776
  13.0 167.8 %all-gather.13.cloned.1.call-start = ((), (), s32[]{:S(2)}) async-start(), calls=%async_computation.7 | async-start | bytes 2621440 | tf_op jit(solution)/shard_map/all_gather | solution.py:113
  14.4 133.8 %copy-start.55 = (f32[128]{0:T(128)}, f32[128]{0:T(128)S(1)}, u32[]{:S(2)}) copy-start(f32[128]{0:T(128)S(1)} %add_rsqrt_fusion.3) | copy-start | bytes 1540
  139.9 8.3 copy-start.27
  143.3 95.8 %all-gather.15.cloned.1.call-start = ((), (), s32[]{:S(2)}) async-start(), calls=%async_computation.8 | async-start | bytes 5898240 | tf_op jit(solution)/shard_map/all_gather | solution.py:102
  146.3 140.8 %all-gather.19.cloned.1.call-start = ((), (), s32[]{:S(2)}) async-start(), calls=%async_computation.10 | async-start | bytes 4718592 | tf_op jit(solution)/shard_map/all_gather | solution.py:105
  148.3 192.5 %all-gather.17.cloned.1.call-start = ((), (), s32[]{:S(2)}) async-start(), calls=%async_computation.9 | async-start | bytes 5242880 | tf_op jit(solution)/shard_map/all_gather | solution.py:137
  151.2 106.9 %copy-start.51 = (f32[128]{0:T(128)}, f32[128]{0:T(128)S(1)}, u32[]{:S(2)}) copy-start(f32[128]{0:T(128)S(1)} %reshape.242) | copy-start | bytes 1540
  151.3 95.9 %copy-start.49 = (f32[128]{0:T(128)}, f32[128]{0:T(128)S(1)}, u32[]{:S(2)}) copy-start(f32[128]{0:T(128)S(1)} %reshape.243) | copy-start | bytes 1540
  245.1 3.4 copy-start.10
  245.1 2.1 copy-start.17
  248.5 11.2 copy-start.19
  255.1 2.3 copy-start.1
  261.2 3.3 copy-start.4
  261.2 3.3 copy-start.38
  263.0 6.4 copy-start.36
  271.7 190.5 %all-gather.23.cloned.1.call-start = ((), (), s32[]{:S(2)}) async-start(), calls=%async_computation.13 | async-start | bytes 17301504 | tf_op jit(solution)/shard_map/all_gather | solution.py:108
  340.8 10.8 copy-start.46
  347.4 16.2 %all-to-all-start = ((bf16[4,128,512]{2,1,0:T(8,128)(2,1)}), bf16[4,128,512]{2,1,0:T(8,128)(2,1)}, u32[]{:S(2)}, u32[]{:S(2)}) async-start(bf16[4,128,512]{2,1,0:T(8,128)(2,1)} %bitcast.219), calls=%async_computation | async-start | bytes 1048576 | tf_op jit(solution)/shard_map/all_to_all | solution.py:144
  351.5 227.4 %all-gather.21.cloned.1.call-start = ((), (), s32[]{:S(2)}) async-start(), calls=%async_computation.11 | async-start | bytes 17301504 | tf_op jit(solution)/shard_map/all_gather | solution.py:152
  351.6 499.8 %copy-start.34 = (f32[1,2,8,128]{3,1,2,0:T(2,128)}, f32[1,2,8,128]{3,1,2,0:T(2,128)S(1)}, u32[]{:S(2)}) copy-start(f32[1,2,8,128]{3,1,2,0:T(2,128)S(1)} %copy.165) | copy-start | bytes 24580
  370.5 3.8 copy-start.3
  370.5 3.8 copy-start.13
  374.3 477.1 %copy-start.53 = (f32[128]{0:T(128)}, f32[128]{0:T(128)S(1)}, u32[]{:S(2)}) copy-start(f32[128]{0:T(128)S(1)} %add_rsqrt_fusion.2) | copy-start | bytes 1540
  375.3 473.8 %reduce-scatter.8.cloned.1.call-start = ((), (), s32[]{:S(2)}) async-start(), calls=%async_computation.14 | async-start | bytes 17301504 | tf_op jit(solution)/shard_map/reduce_scatter | solution.py:200
  379.4 270.9 %copy-start.28 = (pred[32,128]{1,0:T(8,128)(4,1)}, pred[32,128]{1,0:T(8,128)(4,1)S(1)}, u32[]{:S(2)}) copy-start(pred[32,128]{1,0:T(8,128)(4,1)S(1)} %copy.123) | copy-start | bytes 12292
  385.5 88.2 %copy-start.32 = (bf16[32,128]{1,0:T(8,128)(2,1)}, bf16[32,128]{1,0:T(8,128)(2,1)S(1)}, u32[]{:S(2)}) copy-start(bf16[32,128]{1,0:T(8,128)(2,1)S(1)} %copy.125) | copy-start | bytes 24580
  579.0 11.5 copy-start.62
  590.5 12.0 copy-start.5
  590.5 12.0 copy-start.61
  590.5 20.5 %slice-start.2 = ((s8[8388608]{0:T(1024)(128)(4,1)}), s8[4194304]{0:T(1024)(128)(4,1)S(1)}, s32[]{:S(2)}) async-start(s8[8388608]{0:T(1024)(128)(4,1)} %bitcast.192), calls=%async_computation.24 | async-start | bytes 8388608
  602.5 8.5 slice-start.3
  624.9 12.7 copy-start.63
  624.9 12.7 copy-start.66
  664.1 255.9 %all-gather.25.cloned.1.call-start = ((), (), s32[]{:S(2)}) async-start(), calls=%async_computation.15 | async-start | bytes 2621440 | tf_op jit(solution)/shard_map/all_gather | solution.py:217
  851.4 2.8 copy-start.57
  854.3 78.6 %all-to-all-start.1 = ((bf16[4,1024,512]{2,1,0:T(8,128)(2,1)}), bf16[4,1024,512]{2,1,0:T(8,128)(2,1)}, u32[]{:S(2)}, u32[]{:S(2)}) async-start(bf16[4,1024,512]{2,1,0:T(8,128)(2,1)} %bitcast.205), calls=%async_computation.3 | async-start | bytes 8388608 | tf_op jit(solution)/shard_map/all_to_all | solution.py:218
  859.2 145.8 %reduce-scatter.14.cloned.1.call-start = ((), (), s32[]{:S(2)}) async-start(), calls=%async_computation.18 | async-start | bytes 4718592 | tf_op jit(solution)/shard_map/reduce_scatter | solution.py:261
  926.7 110.9 %reduce-scatter.12.cloned.1.call-start = ((), (), s32[]{:S(2)}) async-start(), calls=%async_computation.17 | async-start | bytes 5898240 | tf_op jit(solution)/shard_map/reduce_scatter | solution.py:267
  928.5 15.2 %copy-start.47 = (f32[8,512]{1,0:T(8,128)}, f32[8,512]{1,0:T(8,128)S(1)}, u32[]{:S(2)}) copy-start(f32[8,512]{1,0:T(8,128)S(1)} %log_add_fusion) | copy-start | bytes 49156
  941.4 2.4 copy-start.11
  943.7 5.1 copy-start.9
  950.1 6.1 copy-start.20
  959.8 3.9 slice-start
  961.2 2.8 slice-start.1
  964.5 2.6 copy-start.42
  964.5 2.6 copy-start.64
  972.0 102.6 %reduce-scatter.10.cloned.1.call-start = ((), (), s32[]{:S(2)}) async-start(), calls=%async_computation.16 | async-start | bytes 2621440 | tf_op jit(solution)/shard_map/reduce_scatter | solution.py:250
  980.0 284.7 %reduce-scatter.6.cloned.1.call-start = ((), (), s32[]{:S(2)}) async-start(), calls=%async_computation.12 | async-start | bytes 17301504 | tf_op jit(solution)/shard_map/reduce_scatter | solution.py:204
  980.1 10.9 copy-start.29
  980.1 10.9 copy-start.33
  1004.9 294.8 %all-gather.29.cloned.1.call-start = ((), (), s32[]{:S(2)}) async-start(), calls=%async_computation.20 | async-start | bytes 2621440 | tf_op jit(solution)/shard_map/all_gather | solution.py:264
  1005.4 335.7 %all-gather.27.cloned.1.call-start = ((), (), s32[]{:S(2)}) async-start(), calls=%async_computation.19 | async-start | bytes 3276800 | tf_op jit(solution)/shard_map/all_gather | solution.py:268
  1037.7 11.9 copy-start.65
  1049.6 25.0 %copy-start.41 = (f32[1,2,8,128]{3,1,2,0:T(2,128)S(1)}, f32[1,2,8,128]{3,1,2,0:T(2,128)}, u32[]{:S(2)}) copy-start(f32[1,2,8,128]{3,1,2,0:T(2,128)} %copy-done.40) | copy-start | bytes 24580
  1049.6 25.0 %copy-start.56 = (f32[128]{0:T(128)S(1)}, f32[128]{0:T(128)}, u32[]{:S(2)}) copy-start(f32[128]{0:T(128)} %copy-done.55) | copy-start | bytes 1540
  1049.6 26.8 %copy-start.45 = (f32[2048]{0:T(1024)S(1)}, f32[2048]{0:T(1024)}, u32[]{:S(2)}) copy-start(f32[2048]{0:T(1024)} %get-tuple-element.19) | copy-start | bytes 24580
  1049.6 26.8 %copy-start.59 = (f32[128]{0:T(128)S(1)}, f32[128]{0:T(128)}, u32[]{:S(2)}) copy-start(f32[128]{0:T(128)} %get-tuple-element.13) | copy-start | bytes 1540
  1049.6 26.8 %copy-start.60 = (f32[128]{0:T(128)S(1)}, f32[128]{0:T(128)}, u32[]{:S(2)}) copy-start(f32[128]{0:T(128)} %get-tuple-element.15) | copy-start | bytes 1540
  1049.6 215.1 %copy-start.35 = (f32[1,2,8,128]{3,1,2,0:T(2,128)S(1)}, f32[1,2,8,128]{3,1,2,0:T(2,128)}, u32[]{:S(2)}) copy-start(f32[1,2,8,128]{3,1,2,0:T(2,128)} %copy-done.34) | copy-start | bytes 24580
  1049.7 215.1 %copy-start.54 = (f32[128]{0:T(128)S(1)}, f32[128]{0:T(128)}, u32[]{:S(2)}) copy-start(f32[128]{0:T(128)} %copy-done.53) | copy-start | bytes 1540
  1049.7 215.1 %copy-start.58 = (f32[128]{0:T(128)S(1)}, f32[128]{0:T(128)}, u32[]{:S(2)}) copy-start(f32[128]{0:T(128)} %copy-done.57) | copy-start | bytes 1540
  1350.5 5.0 copy-start.6
  (26 other events, 39.7 us)
Sparse Core Ops, SparseCore 0:
  14.1 124.5 all-reduce.2
  143.5 37.2 all-gather.12
  183.0 56.0 all-gather.14
  241.1 45.9 all-gather.18
  289.4 51.3 all-gather.16
  344.2 117.9 all-gather.22
  465.8 113.0 all-gather.20
  664.2 184.8 reduce-scatter.7
  854.4 65.5 all-gather.24
  926.8 49.7 reduce-scatter.13
  979.5 58.0 reduce-scatter.11
  1041.0 33.5 reduce-scatter.9
  1077.0 187.6 reduce-scatter.5
  1266.6 33.0 all-gather.28
  1301.5 39.6 all-gather.26

commit v2 on v1

v2 whole, which is shorter than its diff:
```python
import functools

import jax
import jax.numpy as jnp
from jax import lax
from jax.experimental import pallas as pl
from jax.experimental.pallas import tpu as pltpu
from jax.sharding import PartitionSpec as P

MODEL_WIDTH = 2048
QUERY_HEADS = 32
KEY_VALUE_HEADS = 4
HEAD_SIZE = 128
TOP = 8

EPSILON = 1e-06
ROPE_BASE = 1000000.0
VERY_NEGATIVE = -1e30
EVERY = ("ctx", "wa")
GROUPS = ((1, 3), (0, 2))


def inv_root(values):
    return lax.rsqrt(jnp.mean(values * values, axis=-1, keepdims=True) + EPSILON)


def rope_tables(positions):
    half_width = HEAD_SIZE // 2
    frequency = ROPE_BASE ** (-(jnp.arange(half_width).astype(positions.dtype) * 2.0 / HEAD_SIZE))
    angles = positions[:, None] * frequency[None, :]
    cosine, sine = jnp.cos(angles), jnp.sin(angles)
    return (
        jnp.concatenate([cosine, cosine], axis=-1),
        jnp.concatenate([-sine, sine], axis=-1),
    )


def dot(a, b, contract):
    return lax.dot_general(a, b, (contract, ((), ())), preferred_element_type=jnp.float32)


def add(*terms):
    total = terms[0].astype(jnp.float32)
    for t in terms[1:]:
        total = total + t.astype(jnp.float32)
    return total


def send(values, move):
    n_ctx, n_z = lax.axis_size("ctx"), lax.axis_size("wa") // 2
    pairs = []
    for c in range(n_ctx):
        for z in range(n_z):
            for k in range(2):
                c2, z2, k2 = move(c, z, k)
                pairs.append(((c * n_z + z) * 2 + k, (c2 * n_z + z2 % n_z) * 2 + k2))
    return lax.ppermute(values, EVERY, pairs)


def to_x(values):
    return send(values, lambda c, z, k: (c ^ 1, z, k))


def to_y(values):
    return send(values, lambda c, z, k: (c ^ 2, z, k))


def to_diagonal(values):
    return send(values, lambda c, z, k: (c ^ 3, z, k))


def to_core(values):
    return send(values, lambda c, z, k: (c, z, 1 - k))


def along_z(values, step):
    return send(values, lambda c, z, k: (c, z + step, k))


def after(values, other):
    return values + lax.slice(other, (0,) * other.ndim, (1,) * other.ndim).reshape(()) * 0.0


def hold(values, *others):
    place = pl.BlockSpec(memory_space=pl.ANY)
    return pl.pallas_call(
        lambda *refs: None,
        out_shape=jax.ShapeDtypeStruct(values.shape, values.dtype),
        in_specs=[place] * (1 + len(others)),
        out_specs=place,
        input_output_aliases={0: 0},
        cost_estimate=pl.CostEstimate(flops=0, bytes_accessed=0, transcendentals=0),
        name="hold",
    )(values, *others)


def by_permutes():
    return lax.axis_size("ctx") == 4 and lax.axis_size("wa") == 8


def ctx_order():
    n_ctx = lax.axis_size("ctx")
    if by_permutes():
        return [lax.axis_index("ctx") ^ i for i in range(n_ctx)]
    return [jnp.int32(i) for i in range(n_ctx)]


def ctx_gather(block):
    if not by_permutes():
        return list(lax.all_gather(block, "ctx", axis=0))
    half = block.shape[0] // 2
    x, y = to_x(block), to_y(block)
    first, second = to_y(x[:half]), to_x(y[half:])
    return [block, x, y, jnp.concatenate([first, second])]


def ctx_scatter(blocks):
    if not by_permutes():
        return lax.psum_scatter(
            jnp.concatenate(blocks), "ctx", scatter_dimension=0, tiled=True
        ).astype(jnp.float32)
    o, x, y, d = blocks
    half, kind = o.shape[0] // 2, o.dtype
    from_x = to_x(jnp.concatenate([d[:half], x[:half]]))
    from_y = to_y(jnp.concatenate([d[half:], y[half:]]))
    late_x = to_x(add(x[half:], from_y[:half]).astype(kind))
    late_y = to_y(add(y[:half], from_x[:half]).astype(kind))
    return jnp.concatenate(
        [add(o[:half], from_x[half:], late_y), add(o[half:], from_y[half:], late_x)]
    )


def ctx_exchange(blocks):
    if not by_permutes():
        return list(
            lax.all_to_all(jnp.stack(blocks), "ctx", split_axis=0, concat_axis=0, tiled=True)
        )
    o, x, y, d = blocks
    return [o, to_x(x), to_y(y), to_diagonal(d)]


def scatter_near(mine, other):
    mine = add(mine, to_core(other)).astype(mine.dtype)
    return ctx_scatter(list(mine.reshape(4, -1, mine.shape[2])))


def scatter_far(parts, kind):
    total = None
    for steps, part in zip(GROUPS, parts):
        rows = part.shape[0] // len(steps)
        for i, step in enumerate(steps):
            piece = part[i * rows : (i + 1) * rows]
            if step:
                piece = along_z(piece.astype(kind), -step)
            total = piece if total is None else add(total, piece)
    return total


def scatter_whole(blocks):
    return lax.psum_scatter(
        blocks.reshape(-1, blocks.shape[-1]), EVERY, scatter_dimension=0, tiled=True
    ).astype(jnp.float32)


def block_order():
    n_wa = lax.axis_size("wa")
    if not by_permutes():
        return [(i, w) for i in range(lax.axis_size("ctx")) for w in range(n_wa)]
    w = lax.axis_index("wa")
    z, k = w // 2, w % 2
    return [
        (i, 2 * ((z - step) % 4) + (k ^ b))
        for steps in GROUPS
        for b in range(2)
        for i in range(4)
        for step in steps
    ]


def sum_all(values):
    if not by_permutes():
        return lax.psum(values, EVERY)
    for move in (
        to_core,
        to_x,
        to_y,
        lambda v: send(v, lambda c, z, k: (c, z ^ 1, k)),
        lambda v: send(v, lambda c, z, k: (c, z ^ 2, k)),
    ):
        values = values + move(values)
    return values


def place(parts, order, axis):
    width = parts[0].shape[axis]
    shape = list(parts[0].shape)
    shape[axis] = width * len(parts)
    whole = jnp.zeros(shape, parts[0].dtype)
    for part, where in zip(parts, order):
        whole = lax.dynamic_update_slice_in_dim(whole, part, where * width, axis)
    return whole


def normed_rotated(raw, gain, cosine, sine):
    root = lax.rsqrt(jnp.mean(raw * raw, axis=-1, keepdims=True) + EPSILON)
    hat = raw * root
    scaled = hat * gain
    turned = scaled * cosine + pltpu.roll(scaled, HEAD_SIZE // 2, 1) * sine
    return root, hat, turned.astype(jnp.bfloat16)


def norm_back(d_turned, root, hat, gain, cosine, sine):
    d_scaled = d_turned * cosine - pltpu.roll(d_turned, HEAD_SIZE // 2, 1) * sine
    d_gain = jnp.sum(d_scaled * hat, axis=0, keepdims=True)
    d_hat = d_scaled * gain
    return root * (d_hat - hat * jnp.mean(d_hat * hat, axis=-1, keepdims=True)), d_gain


def softmax_parts(q_rot, k_rot, row_at, column_at):
    scores = dot(q_rot, k_rot, ((1,), (1,))) * HEAD_SIZE ** (-0.5)
    scores = jnp.where(row_at >= column_at, scores, VERY_NEGATIVE)
    weights = jnp.exp(scores - jnp.max(scores, axis=-1, keepdims=True))
    return weights, jnp.sum(weights, axis=-1, keepdims=True)


def attention_kernel(
    q_ref, k_ref, v_ref, gq_ref, gk_ref, cos_ref, sin_ref, row_ref, col_ref, out_ref, k_scratch
):
    @pl.when(pl.program_id(0) == 0)
    def _():
        k_scratch[...] = normed_rotated(k_ref[...], gk_ref[...], cos_ref[...], sin_ref[...])[2]

    _, _, q_rot = normed_rotated(q_ref[...], gq_ref[...], cos_ref[...], sin_ref[...])
    weights, total = softmax_parts(q_rot, k_scratch[...], row_ref[...], col_ref[...])
    value = v_ref[...].astype(jnp.bfloat16)
    mixed = jnp.dot(weights.astype(jnp.bfloat16), value, preferred_element_type=jnp.float32)
    out_ref[...] = (mixed / total).astype(jnp.bfloat16)


def attention_back_kernel(
    q_ref,
    k_ref,
    v_ref,
    gq_ref,
    gk_ref,
    cos_ref,
    sin_ref,
    row_ref,
    col_ref,
    out_ref,
    d_out_ref,
    d_qkv_ref,
    d_gain_ref,
    k_scratch,
    dk_scratch,
    dv_scratch,
):
    bf16 = jnp.bfloat16
    head, heads = pl.program_id(0), pl.num_programs(0)
    scale = HEAD_SIZE ** (-0.5)
    cosine, sine = cos_ref[...], sin_ref[...]

    @pl.when(head == 0)
    def _():
        k_scratch[...] = normed_rotated(k_ref[...], gk_ref[...], cosine, sine)[2]
        dk_scratch[...] = jnp.zeros_like(dk_scratch)
        dv_scratch[...] = jnp.zeros_like(dv_scratch)
        d_gain_ref[...] = jnp.zeros_like(d_gain_ref)

    root, hat, q_rot = normed_rotated(q_ref[...], gq_ref[...], cosine, sine)
    k_rot = k_scratch[...]
    weights, total = softmax_parts(q_rot, k_rot, row_ref[...], col_ref[...])
    probs = weights * (1.0 / total)
    d_out = d_out_ref[...]
    delta = jnp.sum(
        d_out.astype(jnp.float32) * out_ref[...].astype(jnp.float32), axis=-1, keepdims=True
    )
    d_probs = dot(d_out, v_ref[...].astype(bf16), ((1,), (1,)))
    d_scores = (probs * (d_probs - delta)).astype(bf16)
    dv_scratch[...] += dot(probs.astype(bf16), d_out, ((0,), (0,)))
    dk_scratch[...] += dot(d_scores, q_rot, ((0,), (0,))) * scale
    d_turned = jnp.dot(d_scores, k_rot, preferred_element_type=jnp.float32) * scale
    d_raw, d_gain = norm_back(d_turned, root, hat, gq_ref[...], cosine, sine)
    d_qkv_ref[:, pl.ds(pl.multiple_of(head * HEAD_SIZE, HEAD_SIZE), HEAD_SIZE)] = d_raw.astype(bf16)
    d_gain_ref[0:1] += d_gain

    @pl.when(head == heads - 1)
    def _():
        root, hat, _ = normed_rotated(k_ref[...], gk_ref[...], cosine, sine)
        d_raw, d_gain = norm_back(dk_scratch[...], root, hat, gk_ref[...], cosine, sine)
        last = d_qkv_ref.shape[1] - 2 * HEAD_SIZE
        d_qkv_ref[:, last : last + HEAD_SIZE] = d_raw.astype(bf16)
        d_qkv_ref[:, last + HEAD_SIZE :] = dv_scratch[...].astype(bf16)
        d_gain_ref[1:2] = d_gain


def attention_specs(qkv, gain_query, gain_key, cosine, sine, positions):
    length, heads = qkv.shape[0], qkv.shape[1] // HEAD_SIZE - 2

    def column(which):
        return pl.BlockSpec((length, HEAD_SIZE), lambda h: (0, which(h)))

    def whole(array):
        return pl.BlockSpec(array.shape, lambda h: (0, 0))

    tables = (
        gain_query[None, :],
        gain_key[None, :],
        cosine,
        sine,
        positions[:, None],
        positions[None, :],
    )
    specs = [column(lambda h: h), column(lambda h: heads), column(lambda h: heads + 1)]
    return heads, (qkv, qkv, qkv) + tables, specs + [whole(t) for t in tables], column(lambda h: h)


def attend(*arguments):
    heads, arrays, specs, column = attention_specs(*arguments)
    length = arrays[0].shape[0]
    return pl.pallas_call(
        attention_kernel,
        out_shape=jax.ShapeDtypeStruct((length, heads * HEAD_SIZE), jnp.bfloat16),
        grid=(heads,),
        in_specs=specs,
        out_specs=column,
        scratch_shapes=[pltpu.VMEM((length, HEAD_SIZE), jnp.bfloat16)],
        compiler_params=pltpu.CompilerParams(vmem_limit_bytes=40 * 2**20),
        name="attention",
    )(*arrays)


def attend_back(attended, d_attended, *arguments):
    heads, arrays, specs, column = attention_specs(*arguments)
    length = arrays[0].shape[0]
    shared = pltpu.VMEM((length, HEAD_SIZE), jnp.float32)
    return pl.pallas_call(
        attention_back_kernel,
        out_shape=(
            jax.ShapeDtypeStruct(arrays[0].shape, jnp.bfloat16),
            jax.ShapeDtypeStruct((8, HEAD_SIZE), jnp.float32),
        ),
        grid=(heads,),
        in_specs=specs + [column, column],
        out_specs=(
            pl.BlockSpec(arrays[0].shape, lambda h: (0, 0)),
            pl.BlockSpec((8, HEAD_SIZE), lambda h: (0, 0)),
        ),
        scratch_shapes=[pltpu.VMEM((length, HEAD_SIZE), jnp.bfloat16), shared, shared],
        compiler_params=pltpu.CompilerParams(vmem_limit_bytes=48 * 2**20),
        name="attention_back",
    )(*arrays, attended, d_attended)


def picks(place_ref, gate_ref, blocks, capacity, rows):
    slot = lax.broadcasted_iota(jnp.int32, (capacity, rows), 0)
    chosen = [place_ref[i] == slot for i in range(blocks)]
    return (
        [jnp.where(c, 1.0, 0.0).astype(jnp.bfloat16) for c in chosen],
        [jnp.where(c, gate_ref[i], 0.0).astype(jnp.bfloat16) for i, c in enumerate(chosen)],
    )


def forward_kernel(where_ref, *refs, blocks):
    bf16, f32 = jnp.bfloat16, jnp.float32
    tokens, refs = refs[:blocks], refs[blocks:]
    place_ref, gate_ref, gate_w_ref, up_w_ref, down_w_ref = refs[:5]
    arrived_ref, gate_pre_ref, up_pre_ref, middle_ref, back_ref = refs[-5:]
    rows = tokens[0].shape[1]
    capacity = arrived_ref.shape[0] // blocks
    plain, gated = picks(place_ref, gate_ref, blocks, capacity, rows)
    for i in range(blocks):
        arrived_ref[i * capacity : (i + 1) * capacity] = jnp.dot(
            plain[i], tokens[i][0], preferred_element_type=f32
        ).astype(bf16)
    arrived = arrived_ref[...]
    gate_pre = jnp.dot(arrived, gate_w_ref[...], preferred_element_type=f32)
    up_pre = jnp.dot(arrived, up_w_ref[...], preferred_element_type=f32)
    gate_pre_ref[...] = gate_pre
    up_pre_ref[...] = up_pre
    middle = (gate_pre * jax.nn.sigmoid(gate_pre) * up_pre).astype(bf16)
    middle_ref[...] = middle
    produced = jnp.dot(middle, down_w_ref[...], preferred_element_type=f32).astype(bf16)
    for i in range(blocks):
        mine = produced[i * capacity : (i + 1) * capacity]
        back_ref[i] = dot(gated[i], mine, ((0,), (0,))).astype(bf16)


def backward_kernel(where_ref, *refs, blocks):
    bf16, f32 = jnp.bfloat16, jnp.float32
    cots, refs = refs[:blocks], refs[blocks:]
    place_ref, gate_ref, gate_w_ref, up_w_ref, down_w_ref, gate_pre_ref, up_pre_ref = refs[:7]
    down_grad_ref, d_gate_ref, d_up_ref, back_ref = refs[-4:]
    rows = cots[0].shape[1]
    capacity = down_grad_ref.shape[0] // blocks
    plain, gated = picks(place_ref, gate_ref, blocks, capacity, rows)
    for i in range(blocks):
        down_grad_ref[i * capacity : (i + 1) * capacity] = jnp.dot(
            gated[i], cots[i][0], preferred_element_type=f32
        ).astype(bf16)
    d_middle = dot(down_grad_ref[...], down_w_ref[...], ((1,), (1,)))
    gate_pre = gate_pre_ref[...]
    sigmoid_gate = jax.nn.sigmoid(gate_pre)
    d_gate = d_middle * up_pre_ref[...] * sigmoid_gate * (1.0 + gate_pre * (1.0 - sigmoid_gate))
    d_gate = d_gate.astype(bf16)
    d_up = (d_middle * (gate_pre * sigmoid_gate)).astype(bf16)
    d_gate_ref[...] = d_gate
    d_up_ref[...] = d_up
    d_rows = dot(d_gate, gate_w_ref[...], ((1,), (1,))) + dot(d_up, up_w_ref[...], ((1,), (1,)))
    d_rows = d_rows.astype(bf16)
    for i in range(blocks):
        mine = d_rows[i * capacity : (i + 1) * capacity]
        back_ref[i] = dot(plain[i], mine, ((0,), (0,))).astype(bf16)


def over_blocks(kernel, name, blocks, where, place, gate, weights, by_row, widths, waits):
    bf16, f32 = jnp.bfloat16, jnp.float32
    rows, columns = blocks.shape[1:]
    count, step = where.shape[0], 4
    experts, hidden = blocks.shape[0], weights[0].shape[1]
    tall = step * (2 * rows * TOP // experts)
    place_spec = pl.BlockSpec((step, 1, rows), lambda i, w: (i, 0, 0))

    def row_spec(width):
        return pl.BlockSpec((tall, width), lambda i, w: (i, 0))

    results = [jax.ShapeDtypeStruct((count // step * tall, width), t) for width, t in widths]
    return pl.pallas_call(
        functools.partial(kernel, blocks=step),
        out_shape=(*results, jax.ShapeDtypeStruct((count, rows, columns), bf16)),
        grid_spec=pltpu.PrefetchScalarGridSpec(
            num_scalar_prefetch=1,
            grid=(count // step,),
            in_specs=[
                pl.BlockSpec((1, rows, columns), lambda i, w, j=j: (w[i * step + j], 0, 0))
                for j in range(step)
            ]
            + [place_spec, place_spec]
            + [
                pl.BlockSpec(w.shape, lambda i, w: (0, 0), pipeline_mode=pl.Buffered(1))
                for w in weights
            ]
            + [row_spec(r.shape[1]) for r in by_row]
            + [pl.BlockSpec(memory_space=pl.ANY)] * len(waits),
            out_specs=(
                *(row_spec(width) for width, _ in widths),
                pl.BlockSpec((step, rows, columns), lambda i, w: (i, 0, 0)),
            ),
        ),
        compiler_params=pltpu.CompilerParams(vmem_limit_bytes=52 * 2**20),
        cost_estimate=pl.CostEstimate(flops=0, bytes_accessed=0, transcendentals=0),
        name=name,
    )(
        where,
        *([blocks] * step),
        place[:, None, :],
        gate[:, None, :],
        *weights,
        *by_row,
        *waits,
    )


def on_device(
    block_input,
    query_weight,
    key_projection_matrix,
    value_projection_matrix,
    output_weight,
    attention_gain,
    feedforward_gain,
    query_gain,
    key_gain,
    expert_gate,
    expert_up,
    expert_down,
    expert_ids,
    route_gates,
    cotangent,
):
    bf16, f32 = jnp.bfloat16, jnp.float32
    n_ctx, n_wa = lax.axis_size("ctx"), lax.axis_size("wa")
    my_ctx, my_wa = lax.axis_index("ctx"), lax.axis_index("wa")
    experts = n_ctx * n_wa
    block_rows = block_input[0]
    rows = block_rows.shape[0]
    length = rows * n_ctx
    capacity = 2 * rows * TOP // experts
    heads = QUERY_HEADS // n_ctx
    per_group = QUERY_HEADS // KEY_VALUE_HEADS
    sharers = per_group // heads
    head_columns = heads * HEAD_SIZE
    out_columns = MODEL_WIDTH // n_ctx

    order = ctx_order()
    share = query_weight.shape[0]
    gain_rows = attention_gain.astype(f32)[:, None]
    group = my_ctx * heads // per_group

    def tall(values):
        return jnp.pad(values, ((0, share - values.shape[0]), (0, 0)))

    extras = [
        tall(expert_ids[0].astype(bf16)),
        tall(route_gates[0]),
        feedforward_gain[:, None],
        tall(query_gain[:, None]),
        tall(key_gain[:, None]),
    ]
    extras = jnp.concatenate(extras, axis=1)
    extras = jnp.pad(extras, ((0, 0), (0, HEAD_SIZE - extras.shape[1])))
    my_qkv = jnp.concatenate(
        [
            lax.dynamic_slice_in_dim(query_weight, my_ctx * head_columns, head_columns, 1),
            lax.dynamic_slice_in_dim(key_projection_matrix, group * HEAD_SIZE, HEAD_SIZE, 1),
            lax.dynamic_slice_in_dim(value_projection_matrix, group * HEAD_SIZE, HEAD_SIZE, 1),
        ],
        axis=1,
    )
    scaled_qkv = (my_qkv.astype(f32) * gain_rows).astype(bf16)
    packed = lax.all_gather(
        jnp.concatenate([scaled_qkv, extras], axis=1), "wa", axis=0, tiled=True
    )
    full_qkv = packed[:, : head_columns + 2 * HEAD_SIZE]
    extras = packed[:, head_columns + 2 * HEAD_SIZE :].reshape(n_wa, share, HEAD_SIZE)
    at = 2 * TOP
    gain_feedforward, gain_query, gain_key = (
        extras[:, : g.shape[0], at + i].reshape(-1).astype(f32)
        for i, g in enumerate((feedforward_gain, query_gain, key_gain))
    )
    my_out = lax.dynamic_slice_in_dim(output_weight, my_ctx * out_columns, out_columns, 1)
    full_out = lax.all_gather(
        after(my_out.astype(f32), scaled_qkv.astype(f32)).astype(bf16), "wa", axis=0, tiled=True
    )
    root_x = inv_root(block_rows)
    x_hat = block_rows * root_x
    x_all = jnp.concatenate(ctx_gather(x_hat.astype(bf16)))
    out_cotangent = cotangent[0]
    positions = jnp.concatenate([i * rows + jnp.arange(rows, dtype=jnp.int32) for i in order])
    cosine, sine = rope_tables(positions.astype(f32))
    qkv = dot(x_all, full_qkv, ((1,), (0,)))
    arguments = (qkv, gain_query, gain_key, cosine, sine, positions)
    attended_rows = attend(*arguments)
    others = ctx_gather(attended_rows)
    products = [
        dot(
            theirs,
            lax.dynamic_slice_in_dim(full_out, i * head_columns, head_columns, 0),
            ((1,), (0,)),
        ).reshape(n_ctx, rows, out_columns)
        for theirs, i in zip(others, order)
    ]
    seen = [[m ^ i if by_permutes() else m for m in range(n_ctx)] for i in range(n_ctx)]
    out_blocks = ctx_exchange(
        [add(*(p[seen[i][m]] for i, p in enumerate(products))).astype(bf16) for m in range(n_ctx)]
    )
    hidden = block_rows + place(out_blocks, order, 1).astype(f32)
    others = [
        jnp.concatenate([theirs[m * rows : (m + 1) * rows] for m in seen[i]])
        for i, theirs in enumerate(others)
    ]
    attended_all = place(others, order, 1)

    root_h = inv_root(hidden)
    h_hat = hidden * root_h
    ffn_in = (h_hat * gain_feedforward).astype(bf16)
    ffn_all = lax.all_gather(ffn_in, EVERY, axis=0)
    cot_all = lax.all_gather(after(out_cotangent, hidden).astype(bf16), EVERY, axis=0)
    routing = extras[:, :rows].reshape(n_wa * rows, HEAD_SIZE)
    routing = jnp.concatenate(ctx_exchange([routing] * n_ctx)).reshape(experts, rows, HEAD_SIZE)
    places = block_order()
    in_routing = jnp.stack([jnp.int32(i * n_wa + w) for i, w in places])
    in_all = jnp.stack([order[i] * n_wa + w for i, w in places])
    mine = routing[:, :, :TOP] == (my_ctx * n_wa + my_wa).astype(bf16)
    hit = jnp.any(mine, axis=-1)
    gate_of = jnp.sum(jnp.where(mine, routing[:, :, TOP : 2 * TOP].astype(f32), 0.0), axis=-1)
    token = jnp.arange(rows, dtype=jnp.int32)
    before = (token[:, None] < token[None, :]).astype(bf16)
    rank = dot(hit.astype(bf16), before, ((1,), (0,)))
    place_of = jnp.where(hit, rank, -1.0)[in_routing].astype(jnp.int32)
    gate_of = gate_of[in_routing]
    gate_w, up_w, down_w = expert_gate[0], expert_up[0], expert_down[0]

    out_by_rows = lax.all_to_all(
        full_out.reshape(n_ctx, head_columns, out_columns),
        "ctx",
        split_axis=0,
        concat_axis=0,
        tiled=True,
    )
    weights = (gate_w, up_w, down_w)
    hidden_units = gate_w.shape[1]
    sizes = [8 * len(steps) for steps in GROUPS] if by_permutes() else [experts]
    cuts = [slice(sum(sizes[:g]), sum(sizes[: g + 1])) for g in range(len(sizes))]
    forward, produced_parts = [], []
    for cut in cuts:
        *results, back = over_blocks(
            forward_kernel,
            "experts_forward",
            ffn_all,
            in_all[cut],
            place_of[cut],
            gate_of[cut],
            weights,
            (),
            [(MODEL_WIDTH, bf16), (hidden_units, f32), (hidden_units, f32), (hidden_units, bf16)],
            [],
        )
        forward.append(results)
        produced_parts.append(
            scatter_near(*jnp.split(back, 2)) if by_permutes() else scatter_whole(back)
        )
    backward, back_parts = [], []
    for cut, (_, gate_pre, up_pre, _), wait in zip(cuts, forward, produced_parts):
        *results, back = over_blocks(
            backward_kernel,
            "experts_backward",
            cot_all,
            in_all[cut],
            place_of[cut],
            gate_of[cut],
            weights,
            (gate_pre, up_pre),
            [(MODEL_WIDTH, bf16), (hidden_units, bf16), (hidden_units, bf16)],
            [wait, out_by_rows],
        )
        backward.append(results)
        back_parts.append(
            scatter_near(*jnp.split(back, 2)) if by_permutes() else scatter_whole(back)
        )
    if by_permutes():
        mixture, d_ffn = scatter_far(produced_parts, bf16), scatter_far(back_parts, bf16)
    else:
        [mixture], [d_ffn] = produced_parts, back_parts
    block_output = hidden + mixture
    arrived, _, _, middle = (jnp.concatenate(parts) for parts in zip(*forward))
    down_grad, d_gate_pre, d_up_pre = (jnp.concatenate(parts) for parts in zip(*backward))
    grad_down = dot(middle, down_grad, ((0,), (0,)))
    grad_gate = dot(arrived, d_gate_pre, ((0,), (0,)))
    grad_up = dot(arrived, d_up_pre, ((0,), (0,)))

    grad_feedforward = jnp.sum(d_ffn * h_hat, axis=0)
    grad_hat = d_ffn * gain_feedforward
    d_hidden = out_cotangent + root_h * (
        grad_hat - h_hat * jnp.mean(grad_hat * h_hat, axis=-1, keepdims=True)
    )
    d_out = jnp.concatenate(ctx_gather(d_hidden.astype(bf16)))
    d_attended = jnp.einsum(
        "tcn,ckn->tk",
        d_out.reshape(length, n_ctx, out_columns),
        out_by_rows,
        preferred_element_type=f32,
    ).astype(bf16)
    my_d_out = lax.dynamic_slice_in_dim(d_out, my_ctx * out_columns, out_columns, 1)
    grad_out = dot(attended_all, my_d_out, ((0,), (0,))).astype(bf16)
    grad_out = lax.psum_scatter(grad_out, "wa", scatter_dimension=0, tiled=True)
    d_qkv, d_gains = attend_back(attended_rows, d_attended, *arguments)
    grad_qkv = dot(x_all, d_qkv, ((0,), (0,))).astype(bf16)
    grad_qkv = lax.psum_scatter(grad_qkv, "wa", scatter_dimension=0, tiled=True)
    grad_n = dot(d_qkv, full_qkv, ((1,), (1,))).astype(bf16)
    grad_n = ctx_scatter([grad_n[i * rows : (i + 1) * rows] for i in range(n_ctx)])
    input_grad = d_hidden + root_x * (
        grad_n - x_hat * jnp.mean(grad_n * x_hat, axis=-1, keepdims=True)
    )

    grad_out = place(ctx_gather(grad_out), order, 1).astype(f32)
    sums = sum_all(jnp.concatenate([grad_feedforward, d_gains[0], d_gains[1]]))
    parts = ctx_gather(hold(grad_qkv, grad_out, sums, grad_n))
    raw_query = place([p[:, :head_columns] for p in parts], order, 1).astype(f32)
    raw_key, raw_value = (
        jnp.sum(
            place([p[:, a : a + HEAD_SIZE] for p in parts], order, 1)
            .astype(f32)
            .reshape(share, KEY_VALUE_HEADS, sharers, HEAD_SIZE),
            axis=2,
        ).reshape(share, KEY_VALUE_HEADS * HEAD_SIZE)
        for a in (head_columns, head_columns + HEAD_SIZE)
    )
    grad_attention = sum(
        jnp.sum(w.astype(f32) * raw, axis=1)
        for w, raw in (
            (query_weight, raw_query),
            (key_projection_matrix, raw_key),
            (value_projection_matrix, raw_value),
        )
    )
    gain_grads, at = [grad_attention], 0
    for g in (feedforward_gain, query_gain, key_gain):
        width = g.shape[0]
        gain_grads.append(lax.dynamic_slice_in_dim(sums, at + my_wa * width, width, 0))
        at += width * n_wa
    return (
        block_output[None],
        input_grad[None],
        gain_rows * raw_query,
        gain_rows * raw_key,
        gain_rows * raw_value,
        grad_out,
        *gain_grads,
        grad_gate[None],
        grad_up[None],
        grad_down[None],
    )


def solution(mesh):
    by_row, by_expert = P("wa", None), P(EVERY, None, None)
    tokens = P("wa", "ctx", None)
    gain = P("wa")
    in_specs = (
        (tokens,)
        + (by_row,) * 4
        + (gain,) * 4
        + (by_expert,) * 3
        + (tokens,) * 3
    )
    out_specs = (tokens,) * 2 + (by_row,) * 4 + (gain,) * 4 + (by_expert,) * 3
    return jax.shard_map(
        on_device, mesh=mesh, in_specs=in_specs, out_specs=out_specs, check_vma=False
    )
```

time: 1380 us -> 893 us (0.65)
  waiting for transfers between devices: 962 us -> 481 us
  matrix products: 213 us -> 62.1 us
  Pallas kernels: 0 us -> 123 us
  starting transfers between devices: 10.1 us -> 90.5 us
  blocking collectives: 41.9 us -> 0 us
  local copies, waits for them, and re-layouts: 70.7 us -> 53.5 us
    reduce_scatter x4 -> x1, waiting for transfers between devices: 344 us -> 0.01 us  [on_device(): grad_out = lax.psum_scatter(grad_out, 'wa', scatter_dimension=0, tiled=True)]
    ppermute x0 -> x61, waiting for transfers between devices: none -> 332 us  [send(): return lax.ppermute(values, EVERY, pairs)]
    all_gather x8 -> x3, waiting for transfers between devices: 356 us -> 54.8 us  [the longest x1 34.3 us: on_device(): lax.all_gather(jnp.concatenate([scaled_qkv, extras], axis=1), 'wa', axis=...]
    unnamed x16 -> x6, waiting for transfers between devices: 125 us -> 0.1 us
    pallas_call x0 -> x7, Pallas kernels: none -> 123 us  [the longest x4 89.2 us: over_blocks(): pl.pallas_call(functools.partial(kernel, blocks=step), out_shape=(*result...]
    ppermute x0 -> x61, starting transfers between devices: none -> 84.8 us  [send(): return lax.ppermute(values, EVERY, pairs)]
    dot_general x12 -> x0, matrix products: 81.7 us -> none  [the longest x2 27.5 us: to_tokens(): jnp.einsum('bst,bsd->btd', one_hot, values.reshape(experts, capacity, MOD...]
    dot_general x13 -> x12, matrix products: 125 us -> 57 us  [dot(): lax.dot_general(a, b, (contract, ((), ())), preferred_element_type=jnp.fl...]
  transfers between devices with their start and end apart: 17 -> 68, of which waited for: 15 -> 39; matrix products, arithmetic and copies ran while one was open for 15% -> 17% of each run, Pallas kernels for 0% -> 14%
where the time goes in v2:
time: 893 us; the launch traced here: 884 us
  waiting for transfers between devices  481 us (54%)
  Pallas kernels  123 us (14%)
  starting transfers between devices  90.5 us (10%)
  matrix products  62.1 us (7%)
  other arithmetic  57.7 us (6%)
  local copies, waits for them, and re-layouts  53.5 us (6%)
  between operations  17.1 us (2%)
    ppermute x61, waiting for transfers between devices, send(): return lax.ppermute(values, EVERY, pairs)  332 us
    all_gather x1, waiting for transfers between devices, on_device(): ffn_all = lax.all_gather(ffn_in, EVERY, axis=0)  93.9 us
    pallas_call x4, Pallas kernels, over_blocks(): pl.pallas_call(functools.partial(kernel, blocks=step), out_shape=(*result...  89.2 us
    ppermute x61, starting transfers between devices, send(): return lax.ppermute(values, EVERY, pairs)  84.8 us
    dot_general x12, matrix products, dot(): lax.dot_general(a, b, (contract, ((), ())), preferred_element_type=jnp.fl...  57 us
    all_gather x1, waiting for transfers between devices, on_device(): lax.all_gather(jnp.concatenate([scaled_qkv, extras], axis=1), 'wa', axis=...  34.3 us
    split x4, local copies, waits for them, and re-layouts, on_device(): jnp.split(back, 2)  20.9 us
    all_gather x1, waiting for transfers between devices, on_device(): lax.all_gather(after(my_out.astype(f32), scaled_qkv.astype(f32)).astype(b...  20.5 us
  transfers between devices with their start and end apart: 68, of which 39 were waited for; matrix products, arithmetic and copies ran while one was open for 17% of the time, Pallas kernels for 14%

profile of v2, /device:TPU:0, one launch (start us, length us, event | category | flops | bytes accessed | tf_op | source)
XLA Modules:
  0.0 884.2 jit_solution(2439736876671655454)
XLA Ops:
  18.9 2.9 collective-permute-start
  24.9 8.9 %collective-permute-done = bf16[128,2048]{1,0:T(8,128)(2,1)S(1)} collective-permute-done((bf16[128,2048]{1,0:T(8,128)(2,1)S(1)}, bf16[128,2048]{1,0:T(8,128)(2,1)S(1)}, u32[]{:S(2)}, u32[]{:S(2)}) %collective-permute-start) | collective-permute-done | bytes 524320 | tf_op jit(solution)/shard_map/ppermute | solution.py:57
  39.0 2.5 collective-permute-done.2
  43.5 34.3 %all-gather.6.cloned.1.call-done = bf16[2048,1408]{1,0:T(8,128)(2,1)} async-done(((bf16[256,1408]{1,0:T(8,128)(2,1)}), bf16[2048,1408]{1,0:T(8,128)(2,1)}) %all-gather.6.cloned.1.call-update) | async-done | bytes 5767184 | tf_op jit(solution)/shard_map/all_gather | solution.py:521
  79.4 6.0 fusion.6.q_ref.k_ref.v_ref
  85.5 14.6 %attention.1.out_ref = bf16[512,1024]{1,0:T(8,128)(2,1)S(1)} custom-call(f32[512,1280]{1,0:T(8,128)S(1)} %fusion.6.q_ref.k_ref.v_ref, f32[512,1280]{1,0:T(8,128)S(1)} %fusion.6.q_ref.k_ref.v_ref, f32[512,1280]{1,0:T(8,128)S(1)} %fusion.6.q_ref.k_ref.v_ref, f32[1,128]{1,0:T(1,128)S(1)} %reshape.1512.gq_ref, f32[1,128]{1,0:T(1,128)S(1)} %reshape.1513.gk_ref, ...), custom_call_target="tpu_custom_call" | custom-call | tf_op jit(solution)/shard_map/attention/pallas_call | solution.py:321
  105.4 20.5 %all-gather.8.cloned.1.call-done = bf16[4096,512]{1,0:T(8,128)(2,1)} async-done(((bf16[512,512]{1,0:T(8,128)(2,1)}), bf16[4096,512]{1,0:T(8,128)(2,1)}) %all-gather.8.cloned.1.call-update) | async-done | bytes 4194320 | tf_op jit(solution)/shard_map/all_gather | solution.py:532
  125.9 2.1 fusion.61
  128.0 2.1 fusion.97
  138.0 6.1 collective-permute-done.7
  144.1 2.3 collective-permute-done.6
  151.4 2.5 collective-permute-done.8
  163.8 9.0 %collective-permute-done.13 = bf16[1024,128]{1,0:T(8,128)(2,1)S(1)} collective-permute-done((bf16[1024,128]{1,0:T(8,128)(2,1)S(1)}, bf16[1024,128]{1,0:T(8,128)(2,1)S(1)}, u32[]{:S(2)}, u32[]{:S(2)}) %collective-permute-start.13) | collective-permute-done | bytes 262176 | tf_op jit(solution)/shard_map/ppermute | solution.py:57
  172.8 4.0 collective-permute-done.12
  179.7 93.9 %all-gather.12.cloned.1.call-done = bf16[4096,2048]{1,0:T(8,128)(2,1)} async-done(((bf16[128,2048]{1,0:T(8,128)(2,1)}), bf16[4096,2048]{1,0:T(8,128)(2,1)}) %all-gather.12.cloned.1.call-update) | async-done | bytes 16777232 | tf_op jit(solution)/shard_map/all_gather | solution.py:567
  273.5 20.5 %experts_forward.2 = (bf16[1024,2048]{1,0:T(8,128)(2,1)}, f32[1024,768]{1,0:T(8,128)}, f32[1024,768]{1,0:T(8,128)}, bf16[1024,768]{1,0:T(8,128)(2,1)S(1)}, bf16[16,128,2048]{2,1,0:T(8,128)(2,1)}) custom-call(s32[16]{0:T(128)S(1)} %stack.217.where_ref, bf16[32,128,2048]{2,1,0:T(8,128)(2,1)} %bitcast.277, bf16[32,128,2048]{2,1,0:T(8,128)(2,1)} %bitcast.278, ...), custom_call_target="tpu_custom_call" | custom-call | tf_op jit(solution)/shard_map/experts_forward/pallas_call | solution.py:428
  294.0 4.8 split.25
  299.2 20.5 %experts_forward.3 = (bf16[1024,2048]{1,0:T(8,128)(2,1)}, f32[1024,768]{1,0:T(8,128)}, f32[1024,768]{1,0:T(8,128)}, bf16[1024,768]{1,0:T(8,128)(2,1)S(1)}, bf16[16,128,2048]{2,1,0:T(8,128)(2,1)}) custom-call(s32[16]{0:T(128)S(1)} %stack.267.where_ref, bf16[32,128,2048]{2,1,0:T(8,128)(2,1)} %bitcast.281, bf16[32,128,2048]{2,1,0:T(8,128)(2,1)} %bitcast.282, ...), custom_call_target="tpu_custom_call" | custom-call | tf_op jit(solution)/shard_map/experts_forward/pallas_call | solution.py:428
  319.6 5.4 split.27
  325.4 4.9 all-to-all-start
  330.7 5.4 add_convert_fusion.3
  338.4 5.4 add_convert_fusion.2
  346.9 84.5 %collective-permute-done.15 = bf16[256,2048]{1,0:T(8,128)(2,1)S(1)} collective-permute-done((bf16[256,2048]{1,0:T(8,128)(2,1)S(1)}, bf16[256,2048]{1,0:T(8,128)(2,1)S(1)}, u32[]{:S(2)}, u32[]{:S(2)}) %collective-permute-start.15) | collective-permute-done | bytes 1048608 | tf_op jit(solution)/shard_map/ppermute | solution.py:57
  433.8 12.7 %collective-permute-done.16 = bf16[128,2048]{1,0:T(8,128)(2,1)S(1)} collective-permute-done((bf16[128,2048]{1,0:T(8,128)(2,1)S(1)}, bf16[128,2048]{1,0:T(8,128)(2,1)S(1)}, u32[]{:S(2)}, u32[]{:S(2)}) %collective-permute-start.16) | collective-permute-done | bytes 524320 | tf_op jit(solution)/shard_map/ppermute | solution.py:57
  447.7 6.1 collective-permute-done.22
  453.9 12.7 %collective-permute-done.24 = bf16[256,2048]{1,0:T(8,128)(2,1)S(1)} collective-permute-done((bf16[256,2048]{1,0:T(8,128)(2,1)S(1)}, bf16[256,2048]{1,0:T(8,128)(2,1)S(1)}, u32[]{:S(2)}, u32[]{:S(2)}) %collective-permute-start.24) | collective-permute-done | bytes 1048608 | tf_op jit(solution)/shard_map/ppermute | solution.py:57
  472.5 24.1 %experts_backward.2 = (bf16[1024,2048]{1,0:T(8,128)(2,1)}, bf16[1024,768]{1,0:T(8,128)(2,1)S(1)}, bf16[1024,768]{1,0:T(8,128)(2,1)}, bf16[16,128,2048]{2,1,0:T(8,128)(2,1)}) custom-call(s32[16]{0:T(128)S(1)} %stack.217.where_ref, bf16[32,128,2048]{2,1,0:T(8,128)(2,1)} %all-gather.10.cloned.1.call-done.refs_0_.refs_1_.refs_2_.refs_3_, ...), custom_call_target="tpu_custom_call" | custom-call | tf_op jit(solution)/shard_map/experts_backward/pallas_call | solution.py:428
  496.6 5.4 split.29
  507.4 23.3 %collective-permute-done.26 = bf16[128,2048]{1,0:T(8,128)(2,1)S(1)} collective-permute-done((bf16[128,2048]{1,0:T(8,128)(2,1)S(1)}, bf16[128,2048]{1,0:T(8,128)(2,1)S(1)}, u32[]{:S(2)}, u32[]{:S(2)}) %collective-permute-start.26) | collective-permute-done | bytes 524320 | tf_op jit(solution)/shard_map/ppermute | solution.py:57
  530.7 10.8 %collective-permute-done.17 = bf16[128,2048]{1,0:T(8,128)(2,1)S(1)} collective-permute-done((bf16[128,2048]{1,0:T(8,128)(2,1)S(1)}, bf16[128,2048]{1,0:T(8,128)(2,1)S(1)}, u32[]{:S(2)}, u32[]{:S(2)}) %collective-permute-start.17) | collective-permute-done | bytes 524320 | tf_op jit(solution)/shard_map/ppermute | solution.py:57
  541.6 2.7 add_bitcast_fusion.1
  545.8 24.1 %experts_backward.3 = (bf16[1024,2048]{1,0:T(8,128)(2,1)}, bf16[1024,768]{1,0:T(8,128)(2,1)S(1)}, bf16[1024,768]{1,0:T(8,128)(2,1)}, bf16[16,128,2048]{2,1,0:T(8,128)(2,1)}) custom-call(s32[16]{0:T(128)S(1)} %stack.267.where_ref, bf16[32,128,2048]{2,1,0:T(8,128)(2,1)} %all-gather.10.cloned.1.call-done.refs_0_.refs_1_.refs_2_.refs_3_, ...), custom_call_target="tpu_custom_call" | custom-call | tf_op jit(solution)/shard_map/experts_backward/pallas_call | solution.py:428
  569.9 5.4 split.31
  575.3 4.1 add_convert_fusion.1
  582.7 4.1 add_convert_fusion
  591.1 14.7 %collective-permute-done.28 = bf16[256,2048]{1,0:T(8,128)(2,1)S(1)} collective-permute-done((bf16[256,2048]{1,0:T(8,128)(2,1)S(1)}, bf16[256,2048]{1,0:T(8,128)(2,1)S(1)}, u32[]{:S(2)}, u32[]{:S(2)}) %collective-permute-start.28) | collective-permute-done | bytes 1048608 | tf_op jit(solution)/shard_map/ppermute | solution.py:57
  606.7 21.2 %collective-permute-done.35 = bf16[256,2048]{1,0:T(8,128)(2,1)S(1)} collective-permute-done((bf16[256,2048]{1,0:T(8,128)(2,1)S(1)}, bf16[256,2048]{1,0:T(8,128)(2,1)S(1)}, u32[]{:S(2)}, u32[]{:S(2)}) %collective-permute-start.35) | collective-permute-done | bytes 1048608 | tf_op jit(solution)/shard_map/ppermute | solution.py:57
  629.8 7.6 collective-permute-done.31
  637.4 10.1 %collective-permute-done.29 = bf16[128,2048]{1,0:T(8,128)(2,1)S(1)} collective-permute-done((bf16[128,2048]{1,0:T(8,128)(2,1)S(1)}, bf16[128,2048]{1,0:T(8,128)(2,1)S(1)}, u32[]{:S(2)}, u32[]{:S(2)}) %collective-permute-start.29) | collective-permute-done | bytes 524320 | tf_op jit(solution)/shard_map/ppermute | solution.py:57
  652.0 11.2 %collective-permute-start.39 = (bf16[128,2048]{1,0:T(8,128)(2,1)S(1)}, bf16[128,2048]{1,0:T(8,128)(2,1)S(1)}, u32[]{:S(2)}, u32[]{:S(2)}) collective-permute-start(bf16[128,2048]{1,0:T(8,128)(2,1)S(1)} %fusion.36), channel_id=1, source_target_pairs={{0,4},{1,5},{2,6},{3,7},{4,0},{5,1},{6,2},{7,3},{8,12},{9,13},{10,... | collective-permute-start | bytes 1572872 | tf_op jit(solution)/shard_map/ppermute | solution.py:57
  663.5 9.6 %collective-permute-start.33 = (bf16[128,2048]{1,0:T(8,128)(2,1)S(1)}, bf16[128,2048]{1,0:T(8,128)(2,1)S(1)}, u32[]{:S(2)}, u32[]{:S(2)}) collective-permute-start(bf16[128,2048]{1,0:T(8,128)(2,1)S(1)} %fusion.43), channel_id=1, source_target_pairs={{0,2},{1,3},{2,4},{3,5},{4,6},{5,7},{6,0},{7,1},{8,10},{9,11},{10,... | collective-permute-start | bytes 1572872 | tf_op jit(solution)/shard_map/ppermute | solution.py:57
  674.7 32.4 %collective-permute-done.39 = bf16[128,2048]{1,0:T(8,128)(2,1)S(1)} collective-permute-done((bf16[128,2048]{1,0:T(8,128)(2,1)S(1)}, bf16[128,2048]{1,0:T(8,128)(2,1)S(1)}, u32[]{:S(2)}, u32[]{:S(2)}) %collective-permute-start.39) | collective-permute-done | bytes 524320 | tf_op jit(solution)/shard_map/ppermute | solution.py:57
  712.0 8.8 collective-permute-done.40
  724.3 3.0 collective-permute-done.42
  730.2 4.5 convolution_convert_fusion.1
  734.8 5.2 bitcast_convert_fusion.d_out_ref
  739.9 19.0 %attention_back.1 = (bf16[512,1280]{1,0:T(8,128)(2,1)S(1)}, f32[8,128]{1,0:T(8,128)S(1)}) custom-call(f32[512,1280]{1,0:T(8,128)} %copy-done, f32[512,1280]{1,0:T(8,128)} %copy-done, f32[512,1280]{1,0:T(8,128)} %copy-done, f32[1,128]{1,0:T(1,128)S(1)} %reshape.1512.gq_ref, f32[1,128]{1,0:T(1,128)S(1)} %reshape.1513.gk_ref, ...), custom_call_target="tpu_custom_call" | custom-call | tf_op jit(solution)/shard_map/attention_back/pallas_call | solution.py:337
  760.0 6.9 convolution_convert_fusion
  767.0 2.7 constant_dynamic-update-slice_fusion.13
  771.9 5.7 fusion.21
  779.9 9.1 %convolution_bitcast_fusion.1 = f32[1,2048,768]{2,1,0:T(8,128)} fusion(bf16[2048,2048]{1,0:T(8,128)(2,1)S(1)} %constant_dynamic-update-slice_fusion.12, bf16[1024,768]{1,0:T(8,128)(2,1)S(1)} %copy-done.8, bf16[1024,768]{1,0:T(8,128)(2,1)S(1)} %copy-done.6), kind=kOutput, calls=%fused_computation.21 | convolution fusion | flops 6448742400 | bytes 17825792 | tf_op jit(solution)/shard_map/dot_general | solution.py:39
  789.0 2.8 collective-permute-done.53
  797.3 9.2 %convolution_bitcast_fusion = f32[1,2048,768]{2,1,0:T(8,128)} fusion(bf16[2048,2048]{1,0:T(8,128)(2,1)S(1)} %constant_dynamic-update-slice_fusion.12, bf16[1024,768]{1,0:T(8,128)(2,1)S(1)} %copy-done.47, bf16[1024,768]{1,0:T(8,128)(2,1)S(1)} %copy-done.46), kind=kOutput, calls=%fused_computation.20 | convolution fusion | flops 6448742400 | bytes 17825792 | tf_op jit(solution)/shard_map/dot_general | solution.py:39
  808.2 3.5 collective-permute-done.45
  813.6 8.8 fusion.9
  825.9 2.3 add_bitcast_fusion
  828.2 8.8 collective-permute-done.49
  840.1 3.3 collective-permute-done.51
  843.4 2.1 collective-permute-done.50
  845.6 2.5 convert_element_type.583.refs_1_
  850.8 11.3 %collective-permute-done.57 = bf16[256,1280]{1,0:T(8,128)(2,1)S(1)} collective-permute-done((bf16[256,1280]{1,0:T(8,128)(2,1)}, bf16[256,1280]{1,0:T(8,128)(2,1)S(1)}, u32[]{:S(2)}, u32[]{:S(2)}) %collective-permute-start.57) | collective-permute-done | bytes 655392 | tf_op jit(solution)/shard_map/ppermute | solution.py:57
  865.4 3.9 collective-permute-done.59
  869.3 2.1 collective-permute-done.60
  871.5 3.1 fusion.8
  (362 shorter events, 133.3 us)
Async XLA Ops:
  7.2 70.6 %all-gather.6.cloned.1.call-start = ((), (), s32[]{:S(2)}) async-start(), calls=%async_computation.3 | async-start | bytes 6488064 | tf_op jit(solution)/shard_map/all_gather | solution.py:521
  14.6 111.3 %all-gather.8.cloned.1.call-start = ((), (), s32[]{:S(2)}) async-start(), calls=%async_computation.4 | async-start | bytes 4718592 | tf_op jit(solution)/shard_map/all_gather | solution.py:532
  17.7 255.8 %all-gather.12.cloned.1.call-start = ((), (), s32[]{:S(2)}) async-start(), calls=%async_computation.8 | async-start | bytes 17301504 | tf_op jit(solution)/shard_map/all_gather | solution.py:567
  18.9 14.9 %collective-permute-start = (bf16[128,2048]{1,0:T(8,128)(2,1)S(1)}, bf16[128,2048]{1,0:T(8,128)(2,1)S(1)}, u32[]{:S(2)}, u32[]{:S(2)}) collective-permute-start(bf16[128,2048]{1,0:T(8,128)(2,1)S(1)} %get-tuple-element.70), channel_id=1, source_target_pairs={{0,8},{1,9},{2,10},{3,11},{4,12},{5,13},{6,14},{7,15},{8,0},{9,1},... | collective-permute-start | bytes 1572872 | tf_op jit(solution)/shard_map/ppermute | solution.py:57
  21.9 13.8 %collective-permute-start.1 = (bf16[128,2048]{1,0:T(8,128)(2,1)S(1)}, bf16[128,2048]{1,0:T(8,128)(2,1)S(1)}, u32[]{:S(2)}, u32[]{:S(2)}) collective-permute-start(bf16[128,2048]{1,0:T(8,128)(2,1)S(1)} %get-tuple-element.70), channel_id=1, source_target_pairs={{0,16},{1,17},{2,18},{3,19},{4,20},{5,21},{6,22},{7,23},{8,24},{9,... | collective-permute-start | bytes 1572872 | tf_op jit(solution)/shard_map/ppermute | solution.py:57
  33.8 7.7 collective-permute-start.2
  35.7 7.1 collective-permute-start.3
  100.1 27.9 %collective-permute-start.5 = (bf16[512,1024]{1,0:T(8,128)(2,1)S(1)}, bf16[512,1024]{1,0:T(8,128)(2,1)}, u32[]{:S(2)}, u32[]{:S(2)}) collective-permute-start(bf16[512,1024]{1,0:T(8,128)(2,1)S(1)} %attention.1.out_ref), channel_id=1, source_target_pairs={{0,16},{1,17},{2,18},{3,19},{4,20},{5,21},{6,22},{7,23},{8,24},{9,... | collective-permute-start | bytes 3145736 | tf_op jit(solution)/shard_map/ppermute | solution.py:57
  101.7 29.9 %collective-permute-start.4 = (bf16[512,1024]{1,0:T(8,128)(2,1)S(1)}, bf16[512,1024]{1,0:T(8,128)(2,1)}, u32[]{:S(2)}, u32[]{:S(2)}) collective-permute-start(bf16[512,1024]{1,0:T(8,128)(2,1)S(1)} %attention.1.out_ref), channel_id=1, source_target_pairs={{0,8},{1,9},{2,10},{3,11},{4,12},{5,13},{6,14},{7,15},{8,0},{9,1},... | collective-permute-start | bytes 3145736 | tf_op jit(solution)/shard_map/ppermute | solution.py:57
  130.1 14.1 %collective-permute-start.7 = (bf16[256,1024]{1,0:T(8,128)(2,1)S(1)}, bf16[256,1024]{1,0:T(8,128)(2,1)S(1)}, u32[]{:S(2)}, u32[]{:S(2)}) collective-permute-start(bf16[256,1024]{1,0:T(8,128)(2,1)S(1)} %get-tuple-element.108), channel_id=1, source_target_pairs={{0,8},{1,9},{2,10},{3,11},{4,12},{5,13},{6,14},{7,15},{8,0},{9,1},... | collective-permute-start | bytes 1572872 | tf_op jit(solution)/shard_map/ppermute | solution.py:57
  132.6 13.8 %collective-permute-start.6 = (bf16[256,1024]{1,0:T(8,128)(2,1)S(1)}, bf16[256,1024]{1,0:T(8,128)(2,1)S(1)}, u32[]{:S(2)}, u32[]{:S(2)}) collective-permute-start(bf16[256,1024]{1,0:T(8,128)(2,1)S(1)} %slice.680), channel_id=1, source_target_pairs={{0,16},{1,17},{2,18},{3,19},{4,20},{5,21},{6,22},{7,23},{8,24},{9,... | collective-permute-start | bytes 1572872 | tf_op jit(solution)/shard_map/ppermute | solution.py:57
  157.5 315.0 %all-gather.10.cloned.1.call-start = ((), (), s32[]{:S(2)}) async-start(), calls=%async_computation.5 | async-start | bytes 17301504 | tf_op jit(solution)/shard_map/all_gather | solution.py:568
  160.2 12.5 %collective-permute-start.13 = (bf16[1024,128]{1,0:T(8,128)(2,1)S(1)}, bf16[1024,128]{1,0:T(8,128)(2,1)S(1)}, u32[]{:S(2)}, u32[]{:S(2)}) collective-permute-start(bf16[1024,128]{1,0:T(8,128)(2,1)S(1)} %bitcast.303), channel_id=1, source_target_pairs={{0,24},{1,25},{2,26},{3,27},{4,28},{5,29},{6,30},{7,31},{8,16},{9,... | collective-permute-start | bytes 786440 | tf_op jit(solution)/shard_map/ppermute | solution.py:57
  162.2 14.7 %collective-permute-start.12 = (bf16[1024,128]{1,0:T(8,128)(2,1)S(1)}, bf16[1024,128]{1,0:T(8,128)(2,1)S(1)}, u32[]{:S(2)}, u32[]{:S(2)}) collective-permute-start(bf16[1024,128]{1,0:T(8,128)(2,1)S(1)} %bitcast.304), channel_id=1, source_target_pairs={{0,16},{1,17},{2,18},{3,19},{4,20},{5,21},{6,22},{7,23},{8,24},{9,... | collective-permute-start | bytes 786440 | tf_op jit(solution)/shard_map/ppermute | solution.py:57
  163.1 13.7 %collective-permute-start.11 = (bf16[1024,128]{1,0:T(8,128)(2,1)S(1)}, bf16[1024,128]{1,0:T(8,128)(2,1)S(1)}, u32[]{:S(2)}, u32[]{:S(2)}) collective-permute-start(bf16[1024,128]{1,0:T(8,128)(2,1)S(1)} %bitcast.305), channel_id=1, source_target_pairs={{0,8},{1,9},{2,10},{3,11},{4,12},{5,13},{6,14},{7,15},{8,0},{9,1},... | collective-permute-start | bytes 786440 | tf_op jit(solution)/shard_map/ppermute | solution.py:57
  298.8 31.9 %collective-permute-start.14 = (bf16[8,128,2048]{2,1,0:T(8,128)(2,1)}, bf16[8,128,2048]{2,1,0:T(8,128)(2,1)}, u32[]{:S(2)}, u32[]{:S(2)}) collective-permute-start(bf16[8,128,2048]{2,1,0:T(8,128)(2,1)} %split.25), channel_id=1, source_target_pairs={{0,1},{1,0},{2,3},{3,2},{4,5},{5,4},{6,7},{7,6},{8,9},{9,8},{10,11... | collective-permute-start | bytes 12582920 | tf_op jit(solution)/shard_map/ppermute | solution.py:57
  325.0 13.4 %collective-permute-start.21 = (bf16[8,128,2048]{2,1,0:T(8,128)(2,1)}, bf16[8,128,2048]{2,1,0:T(8,128)(2,1)}, u32[]{:S(2)}, u32[]{:S(2)}) collective-permute-start(bf16[8,128,2048]{2,1,0:T(8,128)(2,1)} %split.27), channel_id=1, source_target_pairs={{0,1},{1,0},{2,3},{3,2},{4,5},{5,4},{6,7},{7,6},{8,9},{9,8},{10,11... | collective-permute-start | bytes 12582920 | tf_op jit(solution)/shard_map/ppermute | solution.py:57
  325.4 147.1 %all-to-all-start = ((bf16[4,1024,512]{2,1,0:T(8,128)(2,1)}), bf16[4,1024,512]{2,1,0:T(8,128)(2,1)}, u32[]{:S(2)}, u32[]{:S(2)}) async-start(bf16[4,1024,512]{2,1,0:T(8,128)(2,1)} %bitcast.299), calls=%async_computation | async-start | bytes 8388608 | tf_op jit(solution)/shard_map/all_to_all | solution.py:584
  330.2 494.7 %reduce-scatter.5.cloned.1.call-start = ((), (), s32[]{:S(2)}) async-start(), calls=%async_computation.7 | async-start | bytes 4718592 | tf_op jit(solution)/shard_map/reduce_scatter | solution.py:656
  336.4 94.9 %collective-permute-start.15 = (bf16[256,2048]{1,0:T(8,128)(2,1)S(1)}, bf16[256,2048]{1,0:T(8,128)(2,1)S(1)}, u32[]{:S(2)}, u32[]{:S(2)}) collective-permute-start(bf16[256,2048]{1,0:T(8,128)(2,1)S(1)} %pad_maximum_fusion.3), channel_id=1, source_target_pairs={{0,8},{1,9},{2,10},{3,11},{4,12},{5,13},{6,14},{7,15},{8,0},{9,1},... | collective-permute-start | bytes 3145736 | tf_op jit(solution)/shard_map/ppermute | solution.py:57
  344.2 109.6 %collective-permute-start.22 = (bf16[256,2048]{1,0:T(8,128)(2,1)S(1)}, bf16[256,2048]{1,0:T(8,128)(2,1)S(1)}, u32[]{:S(2)}, u32[]{:S(2)}) collective-permute-start(bf16[256,2048]{1,0:T(8,128)(2,1)S(1)} %pad_maximum_fusion.5), channel_id=1, source_target_pairs={{0,8},{1,9},{2,10},{3,11},{4,12},{5,13},{6,14},{7,15},{8,0},{9,1},... | collective-permute-start | bytes 3145736 | tf_op jit(solution)/shard_map/ppermute | solution.py:57
  345.4 88.4 %collective-permute-start.18 = (bf16[256,2048]{1,0:T(8,128)(2,1)S(1)}, bf16[256,2048]{1,0:T(8,128)(2,1)S(1)}, u32[]{:S(2)}, u32[]{:S(2)}) collective-permute-start(bf16[256,2048]{1,0:T(8,128)(2,1)S(1)} %pad_maximum_fusion.4), channel_id=1, source_target_pairs={{0,16},{1,17},{2,18},{3,19},{4,20},{5,21},{6,22},{7,23},{8,24},{9,... | collective-permute-start | bytes 3145736 | tf_op jit(solution)/shard_map/ppermute | solution.py:57
  431.5 14.9 %collective-permute-start.16 = (bf16[128,2048]{1,0:T(8,128)(2,1)S(1)}, bf16[128,2048]{1,0:T(8,128)(2,1)S(1)}, u32[]{:S(2)}, u32[]{:S(2)}) collective-permute-start(bf16[128,2048]{1,0:T(8,128)(2,1)S(1)} %fusion.53), channel_id=1, source_target_pairs={{0,16},{1,17},{2,18},{3,19},{4,20},{5,21},{6,22},{7,23},{8,24},{9,... | collective-permute-start | bytes 1572872 | tf_op jit(solution)/shard_map/ppermute | solution.py:57
  433.2 33.4 %collective-permute-start.24 = (bf16[256,2048]{1,0:T(8,128)(2,1)S(1)}, bf16[256,2048]{1,0:T(8,128)(2,1)S(1)}, u32[]{:S(2)}, u32[]{:S(2)}) collective-permute-start(bf16[256,2048]{1,0:T(8,128)(2,1)S(1)} %pad_maximum_fusion.6), channel_id=1, source_target_pairs={{0,16},{1,17},{2,18},{3,19},{4,20},{5,21},{6,22},{7,23},{8,24},{9,... | collective-permute-start | bytes 3145736 | tf_op jit(solution)/shard_map/ppermute | solution.py:57
  447.7 22.2 %collective-permute-start.19 = (bf16[128,2048]{1,0:T(8,128)(2,1)S(1)}, bf16[128,2048]{1,0:T(8,128)(2,1)S(1)}, u32[]{:S(2)}, u32[]{:S(2)}) collective-permute-start(bf16[128,2048]{1,0:T(8,128)(2,1)S(1)} %get-tuple-element.89), channel_id=1, source_target_pairs={{0,8},{1,9},{2,10},{3,11},{4,12},{5,13},{6,14},{7,15},{8,0},{9,1},... | collective-permute-start | bytes 1572872 | tf_op jit(solution)/shard_map/ppermute | solution.py:57
  467.9 34.1 %collective-permute-start.25 = (bf16[128,2048]{1,0:T(8,128)(2,1)}, bf16[128,2048]{1,0:T(8,128)(2,1)}, u32[]{:S(2)}, u32[]{:S(2)}) collective-permute-start(bf16[128,2048]{1,0:T(8,128)(2,1)} %get-tuple-element.84), channel_id=1, source_target_pairs={{0,8},{1,9},{2,10},{3,11},{4,12},{5,13},{6,14},{7,15},{8,0},{9,1},... | collective-permute-start | bytes 1572872 | tf_op jit(solution)/shard_map/ppermute | solution.py:57
  468.5 38.9 %collective-permute-start.23 = (bf16[128,2048]{1,0:T(8,128)(2,1)}, bf16[128,2048]{1,0:T(8,128)(2,1)}, u32[]{:S(2)}, u32[]{:S(2)}) collective-permute-start(bf16[128,2048]{1,0:T(8,128)(2,1)} %get-tuple-element.83), channel_id=1, source_target_pairs={{0,16},{1,17},{2,18},{3,19},{4,20},{5,21},{6,22},{7,23},{8,24},{9,... | collective-permute-start | bytes 1572872 | tf_op jit(solution)/shard_map/ppermute | solution.py:57
  502.0 73.3 %collective-permute-start.27 = (bf16[8,128,2048]{2,1,0:T(8,128)(2,1)}, bf16[8,128,2048]{2,1,0:T(8,128)(2,1)S(1)}, u32[]{:S(2)}, u32[]{:S(2)}) collective-permute-start(bf16[8,128,2048]{2,1,0:T(8,128)(2,1)} %split.29), channel_id=1, source_target_pairs={{0,1},{1,0},{2,3},{3,2},{4,5},{5,4},{6,7},{7,6},{8,9},{9,8},{10,11... | collective-permute-start | bytes 12582920 | tf_op jit(solution)/shard_map/ppermute | solution.py:57
  503.7 27.0 %collective-permute-start.26 = (bf16[128,2048]{1,0:T(8,128)(2,1)S(1)}, bf16[128,2048]{1,0:T(8,128)(2,1)S(1)}, u32[]{:S(2)}, u32[]{:S(2)}) collective-permute-start(bf16[128,2048]{1,0:T(8,128)(2,1)S(1)} %get-tuple-element.65), channel_id=1, source_target_pairs={{0,4},{1,5},{2,6},{3,7},{4,0},{5,1},{6,2},{7,3},{8,12},{9,13},{10,... | collective-permute-start | bytes 1572872 | tf_op jit(solution)/shard_map/ppermute | solution.py:57
  505.2 36.3 %collective-permute-start.17 = (bf16[128,2048]{1,0:T(8,128)(2,1)S(1)}, bf16[128,2048]{1,0:T(8,128)(2,1)S(1)}, u32[]{:S(2)}, u32[]{:S(2)}) collective-permute-start(bf16[128,2048]{1,0:T(8,128)(2,1)S(1)} %copy-done.29), channel_id=1, source_target_pairs={{0,6},{1,7},{2,0},{3,1},{4,2},{5,3},{6,4},{7,5},{8,14},{9,15},{10,... | collective-permute-start | bytes 1572872 | tf_op jit(solution)/shard_map/ppermute | solution.py:57
  506.7 34.9 %collective-permute-start.20 = (bf16[128,2048]{1,0:T(8,128)(2,1)S(1)}, bf16[128,2048]{1,0:T(8,128)(2,1)S(1)}, u32[]{:S(2)}, u32[]{:S(2)}) collective-permute-start(bf16[128,2048]{1,0:T(8,128)(2,1)S(1)} %copy-done.35), channel_id=1, source_target_pairs={{0,2},{1,3},{2,4},{3,5},{4,6},{5,7},{6,0},{7,1},{8,10},{9,11},{10,... | collective-permute-start | bytes 1572872 | tf_op jit(solution)/shard_map/ppermute | solution.py:57
  575.3 7.4 collective-permute-start.34
  579.8 26.0 %collective-permute-start.28 = (bf16[256,2048]{1,0:T(8,128)(2,1)S(1)}, bf16[256,2048]{1,0:T(8,128)(2,1)S(1)}, u32[]{:S(2)}, u32[]{:S(2)}) collective-permute-start(bf16[256,2048]{1,0:T(8,128)(2,1)S(1)} %pad_maximum_fusion.7), channel_id=1, source_target_pairs={{0,8},{1,9},{2,10},{3,11},{4,12},{5,13},{6,14},{7,15},{8,0},{9,1},... | collective-permute-start | bytes 3145736 | tf_op jit(solution)/shard_map/ppermute | solution.py:57
  587.1 40.7 %collective-permute-start.35 = (bf16[256,2048]{1,0:T(8,128)(2,1)S(1)}, bf16[256,2048]{1,0:T(8,128)(2,1)S(1)}, u32[]{:S(2)}, u32[]{:S(2)}) collective-permute-start(bf16[256,2048]{1,0:T(8,128)(2,1)S(1)} %pad_maximum_fusion.9), channel_id=1, source_target_pairs={{0,8},{1,9},{2,10},{3,11},{4,12},{5,13},{6,14},{7,15},{8,0},{9,1},... | collective-permute-start | bytes 3145736 | tf_op jit(solution)/shard_map/ppermute | solution.py:57
  588.8 39.1 %collective-permute-start.37 = (bf16[256,2048]{1,0:T(8,128)(2,1)S(1)}, bf16[256,2048]{1,0:T(8,128)(2,1)S(1)}, u32[]{:S(2)}, u32[]{:S(2)}) collective-permute-start(bf16[256,2048]{1,0:T(8,128)(2,1)S(1)} %pad_maximum_fusion.10), channel_id=1, source_target_pairs={{0,16},{1,17},{2,18},{3,19},{4,20},{5,21},{6,22},{7,23},{8,24},{9,... | collective-permute-start | bytes 3145736 | tf_op jit(solution)/shard_map/ppermute | solution.py:57
  589.6 47.8 %collective-permute-start.31 = (bf16[256,2048]{1,0:T(8,128)(2,1)S(1)}, bf16[256,2048]{1,0:T(8,128)(2,1)S(1)}, u32[]{:S(2)}, u32[]{:S(2)}) collective-permute-start(bf16[256,2048]{1,0:T(8,128)(2,1)S(1)} %pad_maximum_fusion.8), channel_id=1, source_target_pairs={{0,16},{1,17},{2,18},{3,19},{4,20},{5,21},{6,22},{7,23},{8,24},{9,... | collective-permute-start | bytes 3145736 | tf_op jit(solution)/shard_map/ppermute | solution.py:57
  605.9 41.6 %collective-permute-start.29 = (bf16[128,2048]{1,0:T(8,128)(2,1)S(1)}, bf16[128,2048]{1,0:T(8,128)(2,1)S(1)}, u32[]{:S(2)}, u32[]{:S(2)}) collective-permute-start(bf16[128,2048]{1,0:T(8,128)(2,1)S(1)} %fusion.44), channel_id=1, source_target_pairs={{0,16},{1,17},{2,18},{3,19},{4,20},{5,21},{6,22},{7,23},{8,24},{9,... | collective-permute-start | bytes 1572872 | tf_op jit(solution)/shard_map/ppermute | solution.py:57
  628.2 23.6 %collective-permute-start.38 = (bf16[128,2048]{1,0:T(8,128)(2,1)S(1)}, bf16[128,2048]{1,0:T(8,128)(2,1)S(1)}, u32[]{:S(2)}, u32[]{:S(2)}) collective-permute-start(bf16[128,2048]{1,0:T(8,128)(2,1)S(1)} %get-tuple-element.78), channel_id=1, source_target_pairs={{0,8},{1,9},{2,10},{3,11},{4,12},{5,13},{6,14},{7,15},{8,0},{9,1},... | collective-permute-start | bytes 1572872 | tf_op jit(solution)/shard_map/ppermute | solution.py:57
  647.9 15.3 %collective-permute-start.32 = (bf16[128,2048]{1,0:T(8,128)(2,1)S(1)}, bf16[128,2048]{1,0:T(8,128)(2,1)S(1)}, u32[]{:S(2)}, u32[]{:S(2)}) collective-permute-start(bf16[128,2048]{1,0:T(8,128)(2,1)S(1)} %get-tuple-element.72), channel_id=1, source_target_pairs={{0,8},{1,9},{2,10},{3,11},{4,12},{5,13},{6,14},{7,15},{8,0},{9,1},... | collective-permute-start | bytes 1572872 | tf_op jit(solution)/shard_map/ppermute | solution.py:57
  649.3 25.4 %collective-permute-start.36 = (bf16[128,2048]{1,0:T(8,128)(2,1)S(1)}, bf16[128,2048]{1,0:T(8,128)(2,1)S(1)}, u32[]{:S(2)}, u32[]{:S(2)}) collective-permute-start(bf16[128,2048]{1,0:T(8,128)(2,1)S(1)} %get-tuple-element.77), channel_id=1, source_target_pairs={{0,16},{1,17},{2,18},{3,19},{4,20},{5,21},{6,22},{7,23},{8,24},{9,... | collective-permute-start | bytes 1572872 | tf_op jit(solution)/shard_map/ppermute | solution.py:57
  650.0 24.7 %collective-permute-start.30 = (bf16[128,2048]{1,0:T(8,128)(2,1)S(1)}, bf16[128,2048]{1,0:T(8,128)(2,1)S(1)}, u32[]{:S(2)}, u32[]{:S(2)}) collective-permute-start(bf16[128,2048]{1,0:T(8,128)(2,1)S(1)} %get-tuple-element.71), channel_id=1, source_target_pairs={{0,6},{1,7},{2,0},{3,1},{4,2},{5,3},{6,4},{7,5},{8,14},{9,15},{10,... | collective-permute-start | bytes 1572872 | tf_op jit(solution)/shard_map/ppermute | solution.py:57
  652.0 55.1 %collective-permute-start.39 = (bf16[128,2048]{1,0:T(8,128)(2,1)S(1)}, bf16[128,2048]{1,0:T(8,128)(2,1)S(1)}, u32[]{:S(2)}, u32[]{:S(2)}) collective-permute-start(bf16[128,2048]{1,0:T(8,128)(2,1)S(1)} %fusion.36), channel_id=1, source_target_pairs={{0,4},{1,5},{2,6},{3,7},{4,0},{5,1},{6,2},{7,3},{8,12},{9,13},{10,... | collective-permute-start | bytes 1572872 | tf_op jit(solution)/shard_map/ppermute | solution.py:57
  663.5 43.6 %collective-permute-start.33 = (bf16[128,2048]{1,0:T(8,128)(2,1)S(1)}, bf16[128,2048]{1,0:T(8,128)(2,1)S(1)}, u32[]{:S(2)}, u32[]{:S(2)}) collective-permute-start(bf16[128,2048]{1,0:T(8,128)(2,1)S(1)} %fusion.43), channel_id=1, source_target_pairs={{0,2},{1,3},{2,4},{3,5},{4,6},{5,7},{6,0},{7,1},{8,10},{9,11},{10,... | collective-permute-start | bytes 1572872 | tf_op jit(solution)/shard_map/ppermute | solution.py:57
  709.2 11.6 %collective-permute-start.40 = (bf16[128,2048]{1,0:T(8,128)(2,1)S(1)}, bf16[128,2048]{1,0:T(8,128)(2,1)S(1)}, u32[]{:S(2)}, u32[]{:S(2)}) collective-permute-start(bf16[128,2048]{1,0:T(8,128)(2,1)S(1)} %get-tuple-element.56), channel_id=1, source_target_pairs={{0,8},{1,9},{2,10},{3,11},{4,12},{5,13},{6,14},{7,15},{8,0},{9,1},... | collective-permute-start | bytes 1572872 | tf_op jit(solution)/shard_map/ppermute | solution.py:57
  710.3 12.1 %collective-permute-start.41 = (bf16[128,2048]{1,0:T(8,128)(2,1)S(1)}, bf16[128,2048]{1,0:T(8,128)(2,1)S(1)}, u32[]{:S(2)}, u32[]{:S(2)}) collective-permute-start(bf16[128,2048]{1,0:T(8,128)(2,1)S(1)} %get-tuple-element.56), channel_id=1, source_target_pairs={{0,16},{1,17},{2,18},{3,19},{4,20},{5,21},{6,22},{7,23},{8,24},{9,... | collective-permute-start | bytes 1572872 | tf_op jit(solution)/shard_map/ppermute | solution.py:57
  720.8 6.4 collective-permute-start.42
  722.4 6.4 collective-permute-start.43
  734.7 113.4 %reduce-scatter.3.cloned.1.call-start = ((), (), s32[]{:S(2)}) async-start(), calls=%async_computation.6 | async-start | bytes 5898240 | tf_op jit(solution)/shard_map/reduce_scatter | solution.py:659
  771.2 8.4 collective-permute-start.52
  777.7 17.8 %collective-permute-start.44 = (bf16[128,2048]{1,0:T(8,128)(2,1)S(1)}, bf16[128,2048]{1,0:T(8,128)(2,1)S(1)}, u32[]{:S(2)}, u32[]{:S(2)}) collective-permute-start(bf16[128,2048]{1,0:T(8,128)(2,1)S(1)} %pad_maximum_fusion.12), channel_id=1, source_target_pairs={{0,8},{1,9},{2,10},{3,11},{4,12},{5,13},{6,14},{7,15},{8,0},{9,1},... | collective-permute-start | bytes 1572872 | tf_op jit(solution)/shard_map/ppermute | solution.py:57
  779.5 12.2 %collective-permute-start.53 = (f32[2304]{0:T(1024)S(1)}, f32[2304]{0:T(1024)S(1)}, u32[]{:S(2)}, u32[]{:S(2)}) collective-permute-start(f32[2304]{0:T(1024)S(1)} %fusion.86), channel_id=1, source_target_pairs={{0,8},{1,9},{2,10},{3,11},{4,12},{5,13},{6,14},{7,15},{8,0},{9,1},... | collective-permute-start | bytes 27656 | tf_op jit(solution)/shard_map/ppermute | solution.py:57
  793.3 14.9 %collective-permute-start.46 = (bf16[128,2048]{1,0:T(8,128)(2,1)S(1)}, bf16[128,2048]{1,0:T(8,128)(2,1)S(1)}, u32[]{:S(2)}, u32[]{:S(2)}) collective-permute-start(bf16[128,2048]{1,0:T(8,128)(2,1)S(1)} %pad_maximum_fusion.13), channel_id=1, source_target_pairs={{0,16},{1,17},{2,18},{3,19},{4,20},{5,21},{6,22},{7,23},{8,24},{9,... | collective-permute-start | bytes 1572872 | tf_op jit(solution)/shard_map/ppermute | solution.py:57
  795.5 11.0 %collective-permute-start.55 = (f32[2304]{0:T(1024)S(1)}, f32[2304]{0:T(1024)S(1)}, u32[]{:S(2)}, u32[]{:S(2)}) collective-permute-start(f32[2304]{0:T(1024)S(1)} %add.770), channel_id=1, source_target_pairs={{0,2},{1,3},{2,0},{3,1},{4,6},{5,7},{6,4},{7,5},{8,10},{9,11},{10,... | collective-permute-start | bytes 27656 | tf_op jit(solution)/shard_map/ppermute | solution.py:57
  795.6 16.1 %collective-permute-start.45 = (bf16[64,2048]{1,0:T(8,128)(2,1)S(1)}, bf16[64,2048]{1,0:T(8,128)(2,1)S(1)}, u32[]{:S(2)}, u32[]{:S(2)}) collective-permute-start(bf16[64,2048]{1,0:T(8,128)(2,1)S(1)} %add_convert_fusion.7), channel_id=1, source_target_pairs={{0,16},{1,17},{2,18},{3,19},{4,20},{5,21},{6,22},{7,23},{8,24},{9,... | collective-permute-start | bytes 786440 | tf_op jit(solution)/shard_map/ppermute | solution.py:57
  806.5 15.9 %collective-permute-start.56 = (f32[2304]{0:T(1024)S(1)}, f32[2304]{0:T(1024)S(1)}, u32[]{:S(2)}, u32[]{:S(2)}) collective-permute-start(f32[2304]{0:T(1024)S(1)} %add.771), channel_id=1, source_target_pairs={{0,4},{1,5},{2,6},{3,7},{4,0},{5,1},{6,2},{7,3},{8,12},{9,13},{10,... | collective-permute-start | bytes 27656 | tf_op jit(solution)/shard_map/ppermute | solution.py:57
  811.9 11.8 %collective-permute-start.47 = (bf16[64,2048]{1,0:T(8,128)(2,1)S(1)}, bf16[64,2048]{1,0:T(8,128)(2,1)S(1)}, u32[]{:S(2)}, u32[]{:S(2)}) collective-permute-start(bf16[64,2048]{1,0:T(8,128)(2,1)S(1)} %get-tuple-element.100), channel_id=1, source_target_pairs={{0,8},{1,9},{2,10},{3,11},{4,12},{5,13},{6,14},{7,15},{8,0},{9,1},... | collective-permute-start | bytes 786440 | tf_op jit(solution)/shard_map/ppermute | solution.py:57
  825.0 14.1 %collective-permute-start.48 = (bf16[512,512]{1,0:T(8,128)(2,1)}, bf16[512,512]{1,0:T(8,128)(2,1)S(1)}, u32[]{:S(2)}, u32[]{:S(2)}) collective-permute-start(bf16[512,512]{1,0:T(8,128)(2,1)} %reduce-scatter.5.cloned.1.call-done), channel_id=1, source_target_pairs={{0,8},{1,9},{2,10},{3,11},{4,12},{5,13},{6,14},{7,15},{8,0},{9,1},... | collective-permute-start | bytes 1572872 | tf_op jit(solution)/shard_map/ppermute | solution.py:57
  825.4 11.6 %collective-permute-start.49 = (bf16[512,512]{1,0:T(8,128)(2,1)}, bf16[512,512]{1,0:T(8,128)(2,1)S(1)}, u32[]{:S(2)}, u32[]{:S(2)}) collective-permute-start(bf16[512,512]{1,0:T(8,128)(2,1)} %reduce-scatter.5.cloned.1.call-done), channel_id=1, source_target_pairs={{0,16},{1,17},{2,18},{3,19},{4,20},{5,21},{6,22},{7,23},{8,24},{9,... | collective-permute-start | bytes 1572872 | tf_op jit(solution)/shard_map/ppermute | solution.py:57
  837.0 6.4 collective-permute-start.51
  839.1 6.4 collective-permute-start.50
  848.1 14.0 %collective-permute-start.57 = (bf16[256,1280]{1,0:T(8,128)(2,1)}, bf16[256,1280]{1,0:T(8,128)(2,1)S(1)}, u32[]{:S(2)}, u32[]{:S(2)}) collective-permute-start(bf16[256,1280]{1,0:T(8,128)(2,1)} %hold.1), channel_id=1, source_target_pairs={{0,8},{1,9},{2,10},{3,11},{4,12},{5,13},{6,14},{7,15},{8,0},{9,1},... | collective-permute-start | bytes 1966088 | tf_op jit(solution)/shard_map/ppermute | solution.py:57
  848.1 16.1 %collective-permute-start.58 = (bf16[256,1280]{1,0:T(8,128)(2,1)}, bf16[256,1280]{1,0:T(8,128)(2,1)S(1)}, u32[]{:S(2)}, u32[]{:S(2)}) collective-permute-start(bf16[256,1280]{1,0:T(8,128)(2,1)} %hold.1), channel_id=1, source_target_pairs={{0,16},{1,17},{2,18},{3,19},{4,20},{5,21},{6,22},{7,23},{8,24},{9,... | collective-permute-start | bytes 1966088 | tf_op jit(solution)/shard_map/ppermute | solution.py:57
  862.1 7.1 collective-permute-start.59
  864.3 7.1 collective-permute-start.60
  (52 other events, 515.7 us)
Sparse Core Ops, SparseCore 0:
  14.7 63.1 all-gather.5
  80.0 45.8 all-gather.7
  157.6 115.9 all-gather.11
  276.4 160.4 all-gather.9
  734.8 48.4 reduce-scatter.4
  785.4 58.5 reduce-scatter.2

commit v3 on v2

--- a/solution.py
+++ b/solution.py
@@ -139,6 +139,33 @@
     return [o, to_x(x), to_y(y), to_diagonal(d)]
 
 
+def turn_weights(blocks, order):
+    if not by_permutes():
+        return list(lax.all_to_all(blocks, "ctx", split_axis=0, concat_axis=0, tiled=True))
+    k = lax.axis_index("wa") % 2
+    half = blocks.shape[1] // 2
+    shape = (1, half, blocks.shape[2])
+    mine = [lax.dynamic_slice(blocks, (i, k * half, 0), shape)[0] for i in order[1:]]
+    mine = jnp.stack([move(v) for move, v in zip((to_x, to_y, to_diagonal), mine)])
+    other = to_core(mine)
+    low, high = jnp.where(k == 0, mine, other), jnp.where(k == 0, other, mine)
+    own = lax.dynamic_index_in_dim(blocks, order[0], 0)
+    return list(jnp.concatenate([own, jnp.concatenate([low, high], axis=1)]))
+
+
+def gather_groups(block):
+    if not by_permutes():
+        whole = lax.all_gather(block, EVERY, axis=0)
+        return [jnp.split(part, 2) for part in jnp.split(whole, lax.axis_size("ctx"))]
+    rows, columns = block.shape
+    far = {step: along_z(block, step) if step else block for steps in GROUPS for step in steps}
+    groups = []
+    for steps in GROUPS:
+        mine = jnp.concatenate(ctx_gather(jnp.concatenate([far[step] for step in steps])))
+        groups.append([a.reshape(-1, rows, columns) for a in (mine, to_core(mine))])
+    return groups
+
+
 def scatter_near(mine, other):
     mine = add(mine, to_core(other)).astype(mine.dtype)
     return ctx_scatter(list(mine.reshape(4, -1, mine.shape[2])))
@@ -156,10 +183,15 @@
     return total
 
 
-def scatter_whole(blocks):
-    return lax.psum_scatter(
-        blocks.reshape(-1, blocks.shape[-1]), EVERY, scatter_dimension=0, tiled=True
-    ).astype(jnp.float32)
+def scatter_near_whole(*blocks):
+    blocks = jnp.concatenate(blocks)
+    blocks = blocks.reshape(-1, blocks.shape[-1])
+    return lax.psum_scatter(blocks, "wa", scatter_dimension=0, tiled=True)
+
+
+def scatter_far_whole(parts):
+    parts = jnp.concatenate(parts)
+    return lax.psum_scatter(parts, "ctx", scatter_dimension=0, tiled=True).astype(jnp.float32)
 
 
 def block_order():
@@ -361,104 +393,138 @@
     )
 
 
-def forward_kernel(where_ref, *refs, blocks):
+def experts_kernel(where_ref, *refs, blocks):
     bf16, f32 = jnp.bfloat16, jnp.float32
     tokens, refs = refs[:blocks], refs[blocks:]
-    place_ref, gate_ref, gate_w_ref, up_w_ref, down_w_ref = refs[:5]
-    arrived_ref, gate_pre_ref, up_pre_ref, middle_ref, back_ref = refs[-5:]
+    cot_ref, late_cot_ref, place_ref, gate_ref, gate_w_ref, up_w_ref, down_w_ref = refs[:7]
+    arrived_ref, down_grad_ref, middle_ref, d_gate_ref, d_up_ref = refs[-9:-4]
     rows = tokens[0].shape[1]
     capacity = arrived_ref.shape[0] // blocks
     plain, gated = picks(place_ref, gate_ref, blocks, capacity, rows)
+    those = [slice(i * capacity, (i + 1) * capacity) for i in range(blocks)]
+    step, steps = pl.program_id(0), pl.num_programs(0)
+
+    def take(cots):
+        for i in range(blocks):
+            down_grad_ref[those[i]] = jnp.dot(
+                gated[i], cots[i], preferred_element_type=f32
+            ).astype(bf16)
+
+    pl.when(step < steps // 2)(lambda: take(cot_ref))
+    pl.when(step >= steps // 2)(lambda: take(late_cot_ref))
     for i in range(blocks):
-        arrived_ref[i * capacity : (i + 1) * capacity] = jnp.dot(
+        arrived_ref[those[i]] = jnp.dot(
             plain[i], tokens[i][0], preferred_element_type=f32
         ).astype(bf16)
     arrived = arrived_ref[...]
     gate_pre = jnp.dot(arrived, gate_w_ref[...], preferred_element_type=f32)
     up_pre = jnp.dot(arrived, up_w_ref[...], preferred_element_type=f32)
-    gate_pre_ref[...] = gate_pre
-    up_pre_ref[...] = up_pre
-    middle = (gate_pre * jax.nn.sigmoid(gate_pre) * up_pre).astype(bf16)
+    d_middle = dot(down_grad_ref[...], down_w_ref[...], ((1,), (1,)))
+    sigmoid_gate = jax.nn.sigmoid(gate_pre)
+    activated = gate_pre * sigmoid_gate
+    middle = (activated * up_pre).astype(bf16)
     middle_ref[...] = middle
-    produced = jnp.dot(middle, down_w_ref[...], preferred_element_type=f32).astype(bf16)
-    for i in range(blocks):
-        mine = produced[i * capacity : (i + 1) * capacity]
-        back_ref[i] = dot(gated[i], mine, ((0,), (0,))).astype(bf16)
-
-
-def backward_kernel(where_ref, *refs, blocks):
-    bf16, f32 = jnp.bfloat16, jnp.float32
-    cots, refs = refs[:blocks], refs[blocks:]
-    place_ref, gate_ref, gate_w_ref, up_w_ref, down_w_ref, gate_pre_ref, up_pre_ref = refs[:7]
-    down_grad_ref, d_gate_ref, d_up_ref, back_ref = refs[-4:]
-    rows = cots[0].shape[1]
-    capacity = down_grad_ref.shape[0] // blocks
-    plain, gated = picks(place_ref, gate_ref, blocks, capacity, rows)
-    for i in range(blocks):
-        down_grad_ref[i * capacity : (i + 1) * capacity] = jnp.dot(
-            gated[i], cots[i][0], preferred_element_type=f32
-        ).astype(bf16)
-    d_middle = dot(down_grad_ref[...], down_w_ref[...], ((1,), (1,)))
-    gate_pre = gate_pre_ref[...]
-    sigmoid_gate = jax.nn.sigmoid(gate_pre)
-    d_gate = d_middle * up_pre_ref[...] * sigmoid_gate * (1.0 + gate_pre * (1.0 - sigmoid_gate))
+    d_gate = d_middle * up_pre * sigmoid_gate * (1.0 + gate_pre * (1.0 - sigmoid_gate))
     d_gate = d_gate.astype(bf16)
-    d_up = (d_middle * (gate_pre * sigmoid_gate)).astype(bf16)
+    d_up = (d_middle * activated).astype(bf16)
     d_gate_ref[...] = d_gate
     d_up_ref[...] = d_up
     d_rows = dot(d_gate, gate_w_ref[...], ((1,), (1,))) + dot(d_up, up_w_ref[...], ((1,), (1,)))
     d_rows = d_rows.astype(bf16)
-    for i in range(blocks):
-        mine = d_rows[i * capacity : (i + 1) * capacity]
-        back_ref[i] = dot(plain[i], mine, ((0,), (0,))).astype(bf16)
-
-
-def over_blocks(kernel, name, blocks, where, place, gate, weights, by_row, widths, waits):
-    bf16, f32 = jnp.bfloat16, jnp.float32
-    rows, columns = blocks.shape[1:]
+    produced = jnp.dot(middle, down_w_ref[...], preferred_element_type=f32).astype(bf16)
+
+    def leave(d_rows_ref, produced_ref):
+        for i in range(blocks):
+            d_rows_ref[i] = dot(plain[i], d_rows[those[i]], ((0,), (0,))).astype(bf16)
+            produced_ref[i] = dot(gated[i], produced[those[i]], ((0,), (0,))).astype(bf16)
+
+    pl.when(step < steps // 2)(lambda: leave(refs[-4], refs[-2]))
+    pl.when(step >= steps // 2)(lambda: leave(refs[-3], refs[-1]))
+
+
+def run_experts(tokens, where, cots, place, gate, weights, waits):
+    bf16 = jnp.bfloat16
+    rows, columns = tokens.shape[1:]
     count, step = where.shape[0], 4
-    experts, hidden = blocks.shape[0], weights[0].shape[1]
-    tall = step * (2 * rows * TOP // experts)
+    hidden = weights[0].shape[1]
+    tall = step * (2 * rows * TOP // tokens.shape[0])
+    steps = count // step
+    half = steps // 2
+
+    def block_spec(place):
+        return pl.BlockSpec((step, rows, columns), lambda i, w: (place(i), 0, 0))
+
     place_spec = pl.BlockSpec((step, 1, rows), lambda i, w: (i, 0, 0))
-
-    def row_spec(width):
-        return pl.BlockSpec((tall, width), lambda i, w: (i, 0))
-
-    results = [jax.ShapeDtypeStruct((count // step * tall, width), t) for width, t in widths]
+    early = block_spec(lambda i: jnp.minimum(i, half - 1))
+    late = block_spec(lambda i: jnp.maximum(i - half, 0))
+    widths = (columns, columns, hidden, hidden, hidden)
     return pl.pallas_call(
-        functools.partial(kernel, blocks=step),
-        out_shape=(*results, jax.ShapeDtypeStruct((count, rows, columns), bf16)),
+        functools.partial(experts_kernel, blocks=step),
+        out_shape=(
+            *(jax.ShapeDtypeStruct((steps * tall, width), bf16) for width in widths),
+            *([jax.ShapeDtypeStruct((count // 2, rows, columns), bf16)] * 4),
+        ),
         grid_spec=pltpu.PrefetchScalarGridSpec(
             num_scalar_prefetch=1,
-            grid=(count // step,),
+            grid=(steps,),
             in_specs=[
                 pl.BlockSpec((1, rows, columns), lambda i, w, j=j: (w[i * step + j], 0, 0))
                 for j in range(step)
             ]
-            + [place_spec, place_spec]
+            + [early, late, place_spec, place_spec]
             + [
                 pl.BlockSpec(w.shape, lambda i, w: (0, 0), pipeline_mode=pl.Buffered(1))
                 for w in weights
             ]
-            + [row_spec(r.shape[1]) for r in by_row]
             + [pl.BlockSpec(memory_space=pl.ANY)] * len(waits),
             out_specs=(
-                *(row_spec(width) for width, _ in widths),
-                pl.BlockSpec((step, rows, columns), lambda i, w: (i, 0, 0)),
+                *(pl.BlockSpec((tall, width), lambda i, w: (i, 0)) for width in widths),
+                early,
+                late,
+                early,
+                late,
             ),
         ),
-        compiler_params=pltpu.CompilerParams(vmem_limit_bytes=52 * 2**20),
+        compiler_params=pltpu.CompilerParams(vmem_limit_bytes=56 * 2**20),
         cost_estimate=pl.CostEstimate(flops=0, bytes_accessed=0, transcendentals=0),
-        name=name,
+        name="experts",
     )(
         where,
-        *([blocks] * step),
+        *([tokens] * step),
+        *cots,
         place[:, None, :],
         gate[:, None, :],
         *weights,
-        *by_row,
         *waits,
     )
+
+
+def product_kernel(*refs, parts):
+    out_ref = refs[-1]
+    out_ref[...] = sum(dot(refs[p][...], refs[parts + p][...], ((0,), (0,))) for p in range(parts))
+
+
+def sum_of_products(left, right, waits):
+    parts, tile = len(left), 256
+    height, width = left[0].shape[1], right[0].shape[1]
+    return pl.pallas_call(
+        functools.partial(product_kernel, parts=parts),
+        out_shape=jax.ShapeDtypeStruct((height, width), jnp.float32),
+        grid=(width // tile,),
+        in_specs=[
+            pl.BlockSpec(a.shape, lambda i: (0, 0), pipeline_mode=pl.Buffered(1)) for a in left
+        ]
+        + [pl.BlockSpec((b.shape[0], tile), lambda i: (0, i)) for b in right]
+        + [pl.BlockSpec(memory_space=pl.ANY)] * len(waits),
+        out_specs=pl.BlockSpec((height, tile), lambda i: (0, i)),
+        compiler_params=pltpu.CompilerParams(vmem_limit_bytes=48 * 2**20),
+        cost_estimate=pl.CostEstimate(
+            flops=2 * sum(a.shape[0] for a in left) * height * width,
+            bytes_accessed=4 * height * width,
+            transcendentals=0,
+        ),
+        name="sum_of_products",
+    )(*left, *right, *waits)
 
 
 def on_device(
@@ -565,7 +631,7 @@
     h_hat = hidden * root_h
     ffn_in = (h_hat * gain_feedforward).astype(bf16)
     ffn_all = lax.all_gather(ffn_in, EVERY, axis=0)
-    cot_all = lax.all_gather(after(out_cotangent, hidden).astype(bf16), EVERY, axis=0)
+    cot_groups = gather_groups(out_cotangent.astype(bf16))
     routing = extras[:, :rows].reshape(n_wa * rows, HEAD_SIZE)
     routing = jnp.concatenate(ctx_exchange([routing] * n_ctx)).reshape(experts, rows, HEAD_SIZE)
     places = block_order()
@@ -581,81 +647,59 @@
     gate_of = gate_of[in_routing]
     gate_w, up_w, down_w = expert_gate[0], expert_up[0], expert_down[0]
 
-    out_by_rows = lax.all_to_all(
-        full_out.reshape(n_ctx, head_columns, out_columns),
-        "ctx",
-        split_axis=0,
-        concat_axis=0,
-        tiled=True,
-    )
+    out_by_rows = jnp.stack(turn_weights(full_out.reshape(n_ctx, head_columns, out_columns), order))
     weights = (gate_w, up_w, down_w)
-    hidden_units = gate_w.shape[1]
-    sizes = [8 * len(steps) for steps in GROUPS] if by_permutes() else [experts]
-    cuts = [slice(sum(sizes[:g]), sum(sizes[: g + 1])) for g in range(len(sizes))]
-    forward, produced_parts = [], []
-    for cut in cuts:
-        *results, back = over_blocks(
-            forward_kernel,
-            "experts_forward",
+    kept, back_parts, produced, at = [], [], [], 0
+    for cots in cot_groups:
+        cut = slice(at, at + 2 * cots[0].shape[0])
+        at = cut.stop
+        *results, back, back_other, forth, forth_other = run_experts(
             ffn_all,
             in_all[cut],
+            cots,
             place_of[cut],
             gate_of[cut],
             weights,
-            (),
-            [(MODEL_WIDTH, bf16), (hidden_units, f32), (hidden_units, f32), (hidden_units, bf16)],
-            [],
+            kept[-1][:1] if kept else [],
         )
-        forward.append(results)
-        produced_parts.append(
-            scatter_near(*jnp.split(back, 2)) if by_permutes() else scatter_whole(back)
-        )
-    backward, back_parts = [], []
-    for cut, (_, gate_pre, up_pre, _), wait in zip(cuts, forward, produced_parts):
-        *results, back = over_blocks(
-            backward_kernel,
-            "experts_backward",
-            cot_all,
-            in_all[cut],
-            place_of[cut],
-            gate_of[cut],
-            weights,
-            (gate_pre, up_pre),
-            [(MODEL_WIDTH, bf16), (hidden_units, bf16), (hidden_units, bf16)],
-            [wait, out_by_rows],
-        )
-        backward.append(results)
-        back_parts.append(
-            scatter_near(*jnp.split(back, 2)) if by_permutes() else scatter_whole(back)
-        )
+        kept.append(results)
+        if by_permutes():
+            if cut.stop == experts:
+                back = hold(back, out_by_rows)
+            back_parts.append(scatter_near(back, back_other))
+        else:
+            back_parts.append(scatter_near_whole(back, back_other))
+            forth = scatter_near_whole(forth, forth_other)
+        produced.append((forth, forth_other))
     if by_permutes():
-        mixture, d_ffn = scatter_far(produced_parts, bf16), scatter_far(back_parts, bf16)
+        d_ffn = scatter_far(back_parts, bf16)
+        mixture = scatter_far([scatter_near(hold(a, d_ffn), b) for a, b in produced], bf16)
     else:
-        [mixture], [d_ffn] = produced_parts, back_parts
+        d_ffn = scatter_far_whole(back_parts)
+        mixture = scatter_far_whole([forth for forth, _ in produced])
     block_output = hidden + mixture
-    arrived, _, _, middle = (jnp.concatenate(parts) for parts in zip(*forward))
-    down_grad, d_gate_pre, d_up_pre = (jnp.concatenate(parts) for parts in zip(*backward))
-    grad_down = dot(middle, down_grad, ((0,), (0,)))
-    grad_gate = dot(arrived, d_gate_pre, ((0,), (0,)))
-    grad_up = dot(arrived, d_up_pre, ((0,), (0,)))
-
     grad_feedforward = jnp.sum(d_ffn * h_hat, axis=0)
     grad_hat = d_ffn * gain_feedforward
     d_hidden = out_cotangent + root_h * (
         grad_hat - h_hat * jnp.mean(grad_hat * h_hat, axis=-1, keepdims=True)
     )
     d_out = jnp.concatenate(ctx_gather(d_hidden.astype(bf16)))
-    d_attended = jnp.einsum(
-        "tcn,ckn->tk",
-        d_out.reshape(length, n_ctx, out_columns),
-        out_by_rows,
-        preferred_element_type=f32,
+    d_attended = add(
+        *(
+            dot(
+                lax.dynamic_slice_in_dim(d_out, where * out_columns, out_columns, 1),
+                out_by_rows[i],
+                ((1,), (1,)),
+            )
+            for i, where in enumerate(order)
+        )
     ).astype(bf16)
     my_d_out = lax.dynamic_slice_in_dim(d_out, my_ctx * out_columns, out_columns, 1)
     grad_out = dot(attended_all, my_d_out, ((0,), (0,))).astype(bf16)
     grad_out = lax.psum_scatter(grad_out, "wa", scatter_dimension=0, tiled=True)
     d_qkv, d_gains = attend_back(attended_rows, d_attended, *arguments)
     grad_qkv = dot(x_all, d_qkv, ((0,), (0,))).astype(bf16)
+    whole_qkv = grad_qkv
     grad_qkv = lax.psum_scatter(grad_qkv, "wa", scatter_dimension=0, tiled=True)
     grad_n = dot(d_qkv, full_qkv, ((1,), (1,))).astype(bf16)
     grad_n = ctx_scatter([grad_n[i * rows : (i + 1) * rows] for i in range(n_ctx)])
@@ -663,9 +707,14 @@
         grad_n - x_hat * jnp.mean(grad_n * x_hat, axis=-1, keepdims=True)
     )
 
-    grad_out = place(ctx_gather(grad_out), order, 1).astype(f32)
+    parts = ctx_gather(grad_out)
+    arrived, down_grad, middle, d_gate_pre, d_up_pre = zip(*kept)
+    grad_down = sum_of_products(middle, down_grad, [whole_qkv])
+    grad_gate = sum_of_products(arrived, d_gate_pre, [whole_qkv])
+    grad_up = sum_of_products(arrived, d_up_pre, [whole_qkv])
+    grad_out = place(parts, order, 1).astype(f32)
     sums = sum_all(jnp.concatenate([grad_feedforward, d_gains[0], d_gains[1]]))
-    parts = ctx_gather(hold(grad_qkv, grad_out, sums, grad_n))
+    parts = ctx_gather(grad_qkv)
     raw_query = place([p[:, :head_columns] for p in parts], order, 1).astype(f32)
     raw_key, raw_value = (
         jnp.sum(

time: 893 us -> 852 us (0.954)
  waiting for transfers between devices: 481 us -> 431 us
  Pallas kernels: 123 us -> 156 us
  matrix products: 62.1 us -> 32 us
  other arithmetic: 57.7 us -> 68.9 us
    all_gather x1, waiting for transfers between devices: 93.9 us -> 0.01 us  [on_device(): ffn_all = lax.all_gather(ffn_in, EVERY, axis=0)]
    ppermute x61 -> x78, waiting for transfers between devices: 332 us -> 374 us  [send(): return lax.ppermute(values, EVERY, pairs)]
    pallas_call x4 -> x5, Pallas kernels: 89.2 us -> 121 us  [the longest x2 83.3 us: run_experts(): pl.pallas_call(functools.partial(experts_kernel, blocks=step), out_shape=...]
    dot_general x12 -> x13, matrix products: 57 us -> 32 us  [dot(): lax.dot_general(a, b, (contract, ((), ())), preferred_element_type=jnp.fl...]
    split x4 -> x0, local copies, waits for them, and re-layouts: 20.9 us -> none  [on_device(): jnp.split(back, 2)]
    unnamed x108 -> x120, local copies, waits for them, and re-layouts: 11.1 us -> 18.4 us
    ppermute x61 -> x78, starting transfers between devices: 84.8 us -> 92.1 us  [send(): return lax.ppermute(values, EVERY, pairs)]
  transfers between devices with their start and end apart: 68 -> 83, of which waited for: 39 -> 46; matrix products, arithmetic and copies ran while one was open for 17% -> 15% of each run, Pallas kernels for 14% -> 18%
where the time goes in v3:
time: 852 us; the launch traced here: 843 us
  waiting for transfers between devices  431 us (51%)
  Pallas kernels  156 us (18%)
  starting transfers between devices  92.5 us (11%)
  other arithmetic  68.9 us (8%)
  local copies, waits for them, and re-layouts  46.9 us (6%)
  matrix products  32 us (4%)
  between operations  16.4 us (2%)
    ppermute x78, waiting for transfers between devices, send(): return lax.ppermute(values, EVERY, pairs)  374 us
    ppermute x78, starting transfers between devices, send(): return lax.ppermute(values, EVERY, pairs)  92.1 us
    pallas_call x2, Pallas kernels, run_experts(): pl.pallas_call(functools.partial(experts_kernel, blocks=step), out_shape=...  83.3 us
    pallas_call x3, Pallas kernels, sum_of_products(): pl.pallas_call(functools.partial(product_kernel, parts=parts), out_shape=...  37.9 us
    all_gather x1, waiting for transfers between devices, on_device(): lax.all_gather(jnp.concatenate([scaled_qkv, extras], axis=1), 'wa', axis=...  34.4 us
    dot_general x13, matrix products, dot(): lax.dot_general(a, b, (contract, ((), ())), preferred_element_type=jnp.fl...  32 us
    all_gather x1, waiting for transfers between devices, on_device(): lax.all_gather(after(my_out.astype(f32), scaled_qkv.astype(f32)).astype(b...  21.8 us
    convert_element_type x4, other arithmetic, scatter_near(): mine = add(mine, to_core(other)).astype(mine.dtype)  20.3 us
  transfers between devices with their start and end apart: 83, of which 46 were waited for; matrix products, arithmetic and copies ran while one was open for 15% of the time, Pallas kernels for 18%

profile of v3, /device:TPU:0, one launch (start us, length us, event | category | flops | bytes accessed | tf_op | source)
XLA Modules:
  0.0 842.9 jit_solution(1245318925162174549)
XLA Ops:
  18.9 2.9 collective-permute-start
  24.8 8.9 %collective-permute-done = bf16[128,2048]{1,0:T(8,128)(2,1)S(1)} collective-permute-done((bf16[128,2048]{1,0:T(8,128)(2,1)S(1)}, bf16[128,2048]{1,0:T(8,128)(2,1)S(1)}, u32[]{:S(2)}, u32[]{:S(2)}) %collective-permute-start) | collective-permute-done | bytes 524320 | tf_op jit(solution)/shard_map/ppermute | solution.py:57
  38.8 2.6 collective-permute-done.2
  43.4 34.4 %all-gather.5.cloned.1.call-done = bf16[2048,1408]{1,0:T(8,128)(2,1)} async-done(((bf16[256,1408]{1,0:T(8,128)(2,1)}), bf16[2048,1408]{1,0:T(8,128)(2,1)}) %all-gather.5.cloned.1.call-update) | async-done | bytes 5767184 | tf_op jit(solution)/shard_map/all_gather | solution.py:587
  79.4 6.0 fusion.2.q_ref.k_ref.v_ref
  85.5 15.3 %attention.1.out_ref = bf16[512,1024]{1,0:T(8,128)(2,1)} custom-call(f32[512,1280]{1,0:T(8,128)S(1)} %fusion.2.q_ref.k_ref.v_ref, f32[512,1280]{1,0:T(8,128)S(1)} %fusion.2.q_ref.k_ref.v_ref, f32[512,1280]{1,0:T(8,128)S(1)} %fusion.2.q_ref.k_ref.v_ref, f32[1,128]{1,0:T(1,128)S(1)} %reshape.1521.gq_ref, f32[1,128]{1,0:T(1,128)S(1)} %reshape.1522.gk_ref, ...), custom_call_target="tpu_custom_call" | custom-call | tf_op jit(solution)/shard_map/attention/pallas_call | solution.py:353
  104.1 21.8 %all-gather.7.cloned.1.call-done = bf16[4096,512]{1,0:T(8,128)(2,1)} async-done(((bf16[512,512]{1,0:T(8,128)(2,1)}), bf16[4096,512]{1,0:T(8,128)(2,1)}) %all-gather.7.cloned.1.call-update) | async-done | bytes 4194320 | tf_op jit(solution)/shard_map/all_gather | solution.py:598
  125.9 2.4 fusion.63
  136.0 8.4 collective-permute-done.7
  150.6 2.6 collective-permute-done.8
  157.8 4.0 collective-permute-start.12
  161.8 18.4 %collective-permute-done.11 = bf16[128,2048]{1,0:T(8,128)(2,1)S(1)} collective-permute-done((bf16[128,2048]{1,0:T(8,128)(2,1)S(1)}, bf16[128,2048]{1,0:T(8,128)(2,1)S(1)}, u32[]{:S(2)}, u32[]{:S(2)}) %collective-permute-start.11) | collective-permute-done | bytes 524320 | tf_op jit(solution)/shard_map/ppermute | solution.py:57
  181.1 11.4 %collective-permute-done.12 = bf16[128,2048]{1,0:T(8,128)(2,1)S(1)} collective-permute-done((bf16[128,2048]{1,0:T(8,128)(2,1)S(1)}, bf16[128,2048]{1,0:T(8,128)(2,1)S(1)}, u32[]{:S(2)}, u32[]{:S(2)}) %collective-permute-start.12) | collective-permute-done | bytes 524320 | tf_op jit(solution)/shard_map/ppermute | solution.py:57
  197.1 34.6 %collective-permute-done.13 = bf16[256,2048]{1,0:T(8,128)(2,1)S(1)} collective-permute-done((bf16[256,2048]{1,0:T(8,128)(2,1)S(1)}, bf16[256,2048]{1,0:T(8,128)(2,1)S(1)}, u32[]{:S(2)}, u32[]{:S(2)}) %collective-permute-start.13) | collective-permute-done | bytes 1048608 | tf_op jit(solution)/shard_map/ppermute | solution.py:57
  232.3 8.8 %collective-permute-done.28 = bf16[128,2048]{1,0:T(8,128)(2,1)S(1)} collective-permute-done((bf16[128,2048]{1,0:T(8,128)(2,1)S(1)}, bf16[128,2048]{1,0:T(8,128)(2,1)S(1)}, u32[]{:S(2)}, u32[]{:S(2)}) %collective-permute-start.28) | collective-permute-done | bytes 524320 | tf_op jit(solution)/shard_map/ppermute | solution.py:57
  247.7 56.2 %collective-permute-done.16 = bf16[128,2048]{1,0:T(8,128)(2,1)S(1)} collective-permute-done((bf16[128,2048]{1,0:T(8,128)(2,1)S(1)}, bf16[128,2048]{1,0:T(8,128)(2,1)S(1)}, u32[]{:S(2)}, u32[]{:S(2)}) %collective-permute-start.16) | collective-permute-done | bytes 524320 | tf_op jit(solution)/shard_map/ppermute | solution.py:57
  309.9 9.3 %collective-permute-done.31 = bf16[128,2048]{1,0:T(8,128)(2,1)S(1)} collective-permute-done((bf16[128,2048]{1,0:T(8,128)(2,1)S(1)}, bf16[128,2048]{1,0:T(8,128)(2,1)S(1)}, u32[]{:S(2)}, u32[]{:S(2)}) %collective-permute-start.31) | collective-permute-done | bytes 524320 | tf_op jit(solution)/shard_map/ppermute | solution.py:57
  323.9 2.7 collective-permute-start.20
  326.6 5.6 collective-permute-done.18
  332.2 5.4 collective-permute-done.19
  341.6 41.6 %experts.2 = (bf16[1024,2048]{1,0:T(8,128)(2,1)}, bf16[1024,2048]{1,0:T(8,128)(2,1)}, bf16[1024,768]{1,0:T(8,128)(2,1)}, bf16[1024,768]{1,0:T(8,128)(2,1)}, bf16...) custom-call(s32[16]{0:T(128)} %stack.232.where_ref, ...), custom_call_target="tpu_custom_call" | custom-call | tf_op jit(solution)/shard_map/experts/pallas_call | solution.py:461
  383.3 2.5 dynamic-slice_bitcast_fusion.2
  390.0 41.8 %experts.3 = (bf16[1024,2048]{1,0:T(8,128)(2,1)}, bf16[1024,2048]{1,0:T(8,128)(2,1)}, bf16[1024,768]{1,0:T(8,128)(2,1)}, bf16[1024,768]{1,0:T(8,128)(2,1)}, bf16...) custom-call(s32[16]{0:T(128)} %stack.282.where_ref, ...), custom_call_target="tpu_custom_call" | custom-call | tf_op jit(solution)/shard_map/experts/pallas_call | solution.py:461
  435.2 6.4 collective-permute-done.37
  443.7 2.7 maximum_maximum_fusion.refs_1_
  446.4 5.4 add_convert_fusion.3
  454.0 4.1 add_convert_fusion.2
  462.5 15.8 %collective-permute-done.22 = bf16[256,2048]{1,0:T(8,128)(2,1)S(1)} collective-permute-done((bf16[256,2048]{1,0:T(8,128)(2,1)S(1)}, bf16[256,2048]{1,0:T(8,128)(2,1)S(1)}, u32[]{:S(2)}, u32[]{:S(2)}) %collective-permute-start.22) | collective-permute-done | bytes 1048608 | tf_op jit(solution)/shard_map/ppermute | solution.py:57
  479.7 4.8 collective-permute-done.41
  484.6 15.4 %collective-permute-done.39 = bf16[256,2048]{1,0:T(8,128)(2,1)S(1)} collective-permute-done((bf16[256,2048]{1,0:T(8,128)(2,1)S(1)}, bf16[256,2048]{1,0:T(8,128)(2,1)S(1)}, u32[]{:S(2)}, u32[]{:S(2)}) %collective-permute-start.39) | collective-permute-done | bytes 1048608 | tf_op jit(solution)/shard_map/ppermute | solution.py:57
  502.0 5.1 collective-permute-done.25
  507.0 10.4 %collective-permute-done.23 = bf16[128,2048]{1,0:T(8,128)(2,1)S(1)} collective-permute-done((bf16[128,2048]{1,0:T(8,128)(2,1)S(1)}, bf16[128,2048]{1,0:T(8,128)(2,1)S(1)}, u32[]{:S(2)}, u32[]{:S(2)}) %collective-permute-start.23) | collective-permute-done | bytes 524320 | tf_op jit(solution)/shard_map/ppermute | solution.py:57
  522.0 4.0 collective-permute-start.24
  526.4 4.8 collective-permute-done.26
  534.4 4.1 collective-permute-done.24
  538.4 29.3 %collective-permute-done.43 = bf16[128,2048]{1,0:T(8,128)(2,1)S(1)} collective-permute-done((bf16[128,2048]{1,0:T(8,128)(2,1)S(1)}, bf16[128,2048]{1,0:T(8,128)(2,1)S(1)}, u32[]{:S(2)}, u32[]{:S(2)}) %collective-permute-start.43) | collective-permute-done | bytes 524320 | tf_op jit(solution)/shard_map/ppermute | solution.py:57
  572.4 9.2 %collective-permute-done.57 = bf16[128,2048]{1,0:T(8,128)(2,1)S(1)} collective-permute-done((bf16[128,2048]{1,0:T(8,128)(2,1)S(1)}, bf16[128,2048]{1,0:T(8,128)(2,1)S(1)}, u32[]{:S(2)}, u32[]{:S(2)}) %collective-permute-start.57) | collective-permute-done | bytes 524320 | tf_op jit(solution)/shard_map/ppermute | solution.py:57
  584.9 3.7 collective-permute-done.59
  588.6 2.6 collective-permute-done.60
  592.5 4.4 convolution_convert_fusion.1
  597.3 5.4 add_convert_fusion.1
  608.1 5.4 add_convert_fusion
  621.4 19.1 %attention_back.1 = (bf16[512,1280]{1,0:T(8,128)(2,1)S(1)}, f32[8,128]{1,0:T(8,128)S(1)}) custom-call(f32[512,1280]{1,0:T(8,128)} %copy-done, f32[512,1280]{1,0:T(8,128)} %copy-done, f32[512,1280]{1,0:T(8,128)} %copy-done, f32[1,128]{1,0:T(1,128)S(1)} %reshape.1521.gq_ref, f32[1,128]{1,0:T(1,128)S(1)} %reshape.1522.gk_ref, ...), custom_call_target="tpu_custom_call" | custom-call | tf_op jit(solution)/shard_map/attention_back/pallas_call | solution.py:369
  640.5 6.9 convolution_convert_fusion.refs_4_
  651.9 12.7 %sum_of_products.4 = f32[2048,768]{1,0:T(8,128)} custom-call(bf16[1024,2048]{1,0:T(8,128)(2,1)} %get-tuple-element.36.refs_11_.refs_0_, bf16[1024,2048]{1,0:T(8,128)(2,1)} %get-tuple-element.44.refs_1_, bf16[1024,768]{1,0:T(8,128)(2,1)S(1)} %copy-done.3, bf16[1024,768]{1,0:T(8,128)(2,1)S(1)} %copy-done.6, bf16[2048,1280]{1,0:T(8,128)(2,1)} %convolution_convert_fusion.refs_4_), custom_call_target="tpu_custom_call" | custom-call | flops 6442450944 | bytes 6291456 | tf_op jit(solution)/shard_map/sum_of_products/pallas_call | solution.py:510
  664.6 5.8 fusion.5
  670.5 12.9 %sum_of_products.3 = f32[2048,768]{1,0:T(8,128)} custom-call(bf16[1024,2048]{1,0:T(8,128)(2,1)} %get-tuple-element.36.refs_11_.refs_0_, bf16[1024,2048]{1,0:T(8,128)(2,1)} %get-tuple-element.44.refs_1_, bf16[1024,768]{1,0:T(8,128)(2,1)S(1)} %copy-done.2, bf16[1024,768]{1,0:T(8,128)(2,1)S(1)} %copy-done.5, bf16[2048,1280]{1,0:T(8,128)(2,1)} %convolution_convert_fusion.refs_4_), custom_call_target="tpu_custom_call" | custom-call | flops 6442450944 | bytes 6291456 | tf_op jit(solution)/shard_map/sum_of_products/pallas_call | solution.py:510
  683.5 12.3 %sum_of_products.5 = f32[768,2048]{1,0:T(8,128)} custom-call(bf16[1024,768]{1,0:T(8,128)(2,1)S(1)} %copy-done.1, bf16[1024,768]{1,0:T(8,128)(2,1)S(1)} %copy-done.4, bf16[1024,2048]{1,0:T(8,128)(2,1)} %get-tuple-element.51.refs_2_, bf16[1024,2048]{1,0:T(8,128)(2,1)} %get-tuple-element.52.refs_3_, bf16[2048,1280]{1,0:T(8,128)(2,1)} %convolution_convert_fusion.refs_4_), custom_call_target="tpu_custom_call" | custom-call | flops 6442450944 | bytes 6291456 | tf_op jit(solution)/shard_map/sum_of_products/pallas_call | solution.py:510
  699.5 3.6 collective-permute-start.76
  705.3 4.1 collective-permute-start.77
  715.6 7.2 collective-permute-done.61
  725.0 2.8 fusion.30
  730.3 14.6 %collective-permute-done.62 = bf16[64,2048]{1,0:T(8,128)(2,1)S(1)} collective-permute-done((bf16[64,2048]{1,0:T(8,128)(2,1)S(1)}, bf16[64,2048]{1,0:T(8,128)(2,1)S(1)}, u32[]{:S(2)}, u32[]{:S(2)}) %collective-permute-start.62) | collective-permute-done | bytes 262176 | tf_op jit(solution)/shard_map/ppermute | solution.py:57
  745.2 2.5 fusion.41
  749.6 2.5 collective-permute-start.47
  755.0 4.7 collective-permute-done.49
  766.2 25.8 %collective-permute-done.56 = bf16[128,2048]{1,0:T(8,128)(2,1)} collective-permute-done((bf16[128,2048]{1,0:T(8,128)(2,1)}, bf16[128,2048]{1,0:T(8,128)(2,1)}, u32[]{:S(2)}, u32[]{:S(2)}) %collective-permute-start.56) | collective-permute-done | bytes 524320 | tf_op jit(solution)/shard_map/ppermute | solution.py:57
  792.1 2.8 fusion.35
  797.9 3.9 collective-permute-done.71
  801.8 3.5 collective-permute-done.72
  805.3 2.5 convert_element_type.585
  811.8 10.4 %collective-permute-done.65 = bf16[256,1280]{1,0:T(8,128)(2,1)S(1)} collective-permute-done((bf16[256,1280]{1,0:T(8,128)(2,1)}, bf16[256,1280]{1,0:T(8,128)(2,1)S(1)}, u32[]{:S(2)}, u32[]{:S(2)}) %collective-permute-start.65) | collective-permute-done | bytes 655392 | tf_op jit(solution)/shard_map/ppermute | solution.py:57
  824.5 4.9 collective-permute-done.67
  832.3 3.1 fusion.4
  (410 shorter events, 167.4 us)
Async XLA Ops:
  7.2 70.7 %all-gather.5.cloned.1.call-start = ((), (), s32[]{:S(2)}) async-start(), calls=%async_computation.2 | async-start | bytes 6488064 | tf_op jit(solution)/shard_map/all_gather | solution.py:587
  14.6 111.3 %all-gather.7.cloned.1.call-start = ((), (), s32[]{:S(2)}) async-start(), calls=%async_computation.3 | async-start | bytes 4718592 | tf_op jit(solution)/shard_map/all_gather | solution.py:598
  17.7 323.9 %all-gather.9.cloned.1.call-start = ((), (), s32[]{:S(2)}) async-start(), calls=%async_computation.6 | async-start | bytes 17301504 | tf_op jit(solution)/shard_map/all_gather | solution.py:633
  18.9 14.9 %collective-permute-start = (bf16[128,2048]{1,0:T(8,128)(2,1)S(1)}, bf16[128,2048]{1,0:T(8,128)(2,1)S(1)}, u32[]{:S(2)}, u32[]{:S(2)}) collective-permute-start(bf16[128,2048]{1,0:T(8,128)(2,1)S(1)} %get-tuple-element.64), channel_id=1, source_target_pairs={{0,8},{1,9},{2,10},{3,11},{4,12},{5,13},{6,14},{7,15},{8,0},{9,1},... | collective-permute-start | bytes 1572872 | tf_op jit(solution)/shard_map/ppermute | solution.py:57
  21.8 13.8 %collective-permute-start.1 = (bf16[128,2048]{1,0:T(8,128)(2,1)S(1)}, bf16[128,2048]{1,0:T(8,128)(2,1)S(1)}, u32[]{:S(2)}, u32[]{:S(2)}) collective-permute-start(bf16[128,2048]{1,0:T(8,128)(2,1)S(1)} %get-tuple-element.64), channel_id=1, source_target_pairs={{0,16},{1,17},{2,18},{3,19},{4,20},{5,21},{6,22},{7,23},{8,24},{9,... | collective-permute-start | bytes 1572872 | tf_op jit(solution)/shard_map/ppermute | solution.py:57
  100.7 27.6 %collective-permute-start.5 = (bf16[512,1024]{1,0:T(8,128)(2,1)}, bf16[512,1024]{1,0:T(8,128)(2,1)}, u32[]{:S(2)}, u32[]{:S(2)}) collective-permute-start(bf16[512,1024]{1,0:T(8,128)(2,1)} %attention.1.out_ref), channel_id=1, source_target_pairs={{0,16},{1,17},{2,18},{3,19},{4,20},{5,21},{6,22},{7,23},{8,24},{9,... | collective-permute-start | bytes 3145736 | tf_op jit(solution)/shard_map/ppermute | solution.py:57
  102.2 29.5 %collective-permute-start.4 = (bf16[512,1024]{1,0:T(8,128)(2,1)}, bf16[512,1024]{1,0:T(8,128)(2,1)S(1)}, u32[]{:S(2)}, u32[]{:S(2)}) collective-permute-start(bf16[512,1024]{1,0:T(8,128)(2,1)} %attention.1.out_ref), channel_id=1, source_target_pairs={{0,8},{1,9},{2,10},{3,11},{4,12},{5,13},{6,14},{7,15},{8,0},{9,1},... | collective-permute-start | bytes 3145736 | tf_op jit(solution)/shard_map/ppermute | solution.py:57
  130.4 14.1 %collective-permute-start.7 = (bf16[256,1024]{1,0:T(8,128)(2,1)S(1)}, bf16[256,1024]{1,0:T(8,128)(2,1)S(1)}, u32[]{:S(2)}, u32[]{:S(2)}) collective-permute-start(bf16[256,1024]{1,0:T(8,128)(2,1)S(1)} %get-tuple-element.106), channel_id=1, source_target_pairs={{0,8},{1,9},{2,10},{3,11},{4,12},{5,13},{6,14},{7,15},{8,0},{9,1},... | collective-permute-start | bytes 1572872 | tf_op jit(solution)/shard_map/ppermute | solution.py:57
  131.8 13.9 %collective-permute-start.6 = (bf16[256,1024]{1,0:T(8,128)(2,1)S(1)}, bf16[256,1024]{1,0:T(8,128)(2,1)S(1)}, u32[]{:S(2)}, u32[]{:S(2)}) collective-permute-start(bf16[256,1024]{1,0:T(8,128)(2,1)S(1)} %slice.689), channel_id=1, source_target_pairs={{0,16},{1,17},{2,18},{3,19},{4,20},{5,21},{6,22},{7,23},{8,24},{9,... | collective-permute-start | bytes 1572872 | tf_op jit(solution)/shard_map/ppermute | solution.py:57
  156.8 606.8 %reduce-scatter.5.cloned.1.call-start = ((), (), s32[]{:S(2)}) async-start(), calls=%async_computation.5 | async-start | bytes 4718592 | tf_op jit(solution)/shard_map/reduce_scatter | solution.py:699
  157.8 22.4 %collective-permute-start.11 = (bf16[128,2048]{1,0:T(8,128)(2,1)S(1)}, bf16[128,2048]{1,0:T(8,128)(2,1)S(1)}, u32[]{:S(2)}, u32[]{:S(2)}) collective-permute-start(bf16[128,2048]{1,0:T(8,128)(2,1)S(1)} %get-tuple-element.60), channel_id=1, source_target_pairs={{0,2},{1,3},{2,4},{3,5},{4,6},{5,7},{6,0},{7,1},{8,10},{9,11},{10,... | collective-permute-start | bytes 1572872 | tf_op jit(solution)/shard_map/ppermute | solution.py:57
  157.8 34.7 %collective-permute-start.12 = (bf16[128,2048]{1,0:T(8,128)(2,1)S(1)}, bf16[128,2048]{1,0:T(8,128)(2,1)S(1)}, u32[]{:S(2)}, u32[]{:S(2)}) collective-permute-start(bf16[128,2048]{1,0:T(8,128)(2,1)S(1)} %get-tuple-element.60), channel_id=1, source_target_pairs={{0,6},{1,7},{2,0},{3,1},{4,2},{5,3},{6,4},{7,5},{8,14},{9,15},{10,... | collective-permute-start | bytes 1572872 | tf_op jit(solution)/shard_map/ppermute | solution.py:57
  193.4 38.2 %collective-permute-start.13 = (bf16[256,2048]{1,0:T(8,128)(2,1)S(1)}, bf16[256,2048]{1,0:T(8,128)(2,1)S(1)}, u32[]{:S(2)}, u32[]{:S(2)}) collective-permute-start(bf16[256,2048]{1,0:T(8,128)(2,1)S(1)} %get-tuple-element.121), channel_id=1, source_target_pairs={{0,8},{1,9},{2,10},{3,11},{4,12},{5,13},{6,14},{7,15},{8,0},{9,1},... | collective-permute-start | bytes 3145736 | tf_op jit(solution)/shard_map/ppermute | solution.py:57
  194.3 49.7 %collective-permute-start.14 = (bf16[256,2048]{1,0:T(8,128)(2,1)S(1)}, bf16[256,2048]{1,0:T(8,128)(2,1)S(1)}, u32[]{:S(2)}, u32[]{:S(2)}) collective-permute-start(bf16[256,2048]{1,0:T(8,128)(2,1)S(1)} %get-tuple-element.121), channel_id=1, source_target_pairs={{0,16},{1,17},{2,18},{3,19},{4,20},{5,21},{6,22},{7,23},{8,24},{9,... | collective-permute-start | bytes 3145736 | tf_op jit(solution)/shard_map/ppermute | solution.py:57
  194.9 46.2 %collective-permute-start.28 = (bf16[128,2048]{1,0:T(8,128)(2,1)S(1)}, bf16[128,2048]{1,0:T(8,128)(2,1)S(1)}, u32[]{:S(2)}, u32[]{:S(2)}) collective-permute-start(bf16[128,2048]{1,0:T(8,128)(2,1)S(1)} %get-tuple-element.60), channel_id=1, source_target_pairs={{0,4},{1,5},{2,6},{3,7},{4,0},{5,1},{6,2},{7,3},{8,12},{9,13},{10,... | collective-permute-start | bytes 1572872 | tf_op jit(solution)/shard_map/ppermute | solution.py:57
  231.7 15.2 %collective-permute-start.15 = (bf16[128,2048]{1,0:T(8,128)(2,1)S(1)}, bf16[128,2048]{1,0:T(8,128)(2,1)S(1)}, u32[]{:S(2)}, u32[]{:S(2)}) collective-permute-start(bf16[128,2048]{1,0:T(8,128)(2,1)S(1)} %slice.705), channel_id=1, source_target_pairs={{0,16},{1,17},{2,18},{3,19},{4,20},{5,21},{6,22},{7,23},{8,24},{9,... | collective-permute-start | bytes 1572872 | tf_op jit(solution)/shard_map/ppermute | solution.py:57
  241.2 63.6 %collective-permute-start.29 = (bf16[256,2048]{1,0:T(8,128)(2,1)S(1)}, bf16[256,2048]{1,0:T(8,128)(2,1)S(1)}, u32[]{:S(2)}, u32[]{:S(2)}) collective-permute-start(bf16[256,2048]{1,0:T(8,128)(2,1)S(1)} %pad_maximum_fusion.5), channel_id=1, source_target_pairs={{0,8},{1,9},{2,10},{3,11},{4,12},{5,13},{6,14},{7,15},{8,0},{9,1},... | collective-permute-start | bytes 3145736 | tf_op jit(solution)/shard_map/ppermute | solution.py:57
  242.4 64.9 %collective-permute-start.30 = (bf16[256,2048]{1,0:T(8,128)(2,1)S(1)}, bf16[256,2048]{1,0:T(8,128)(2,1)S(1)}, u32[]{:S(2)}, u32[]{:S(2)}) collective-permute-start(bf16[256,2048]{1,0:T(8,128)(2,1)S(1)} %pad_maximum_fusion.5), channel_id=1, source_target_pairs={{0,16},{1,17},{2,18},{3,19},{4,20},{5,21},{6,22},{7,23},{8,24},{9,... | collective-permute-start | bytes 3145736 | tf_op jit(solution)/shard_map/ppermute | solution.py:57
  244.0 59.9 %collective-permute-start.16 = (bf16[128,2048]{1,0:T(8,128)(2,1)S(1)}, bf16[128,2048]{1,0:T(8,128)(2,1)S(1)}, u32[]{:S(2)}, u32[]{:S(2)}) collective-permute-start(bf16[128,2048]{1,0:T(8,128)(2,1)S(1)} %slice.706), channel_id=1, source_target_pairs={{0,8},{1,9},{2,10},{3,11},{4,12},{5,13},{6,14},{7,15},{8,0},{9,1},... | collective-permute-start | bytes 1572872 | tf_op jit(solution)/shard_map/ppermute | solution.py:57
  304.8 36.9 %collective-permute-start.17 = (bf16[1024,2048]{1,0:T(8,128)(2,1)}, bf16[1024,2048]{1,0:T(8,128)(2,1)}, u32[]{:S(2)}, u32[]{:S(2)}) collective-permute-start(bf16[1024,2048]{1,0:T(8,128)(2,1)} %constant_dynamic-update-slice_fusion.7), channel_id=1, source_target_pairs={{0,1},{1,0},{2,3},{3,2},{4,5},{5,4},{6,7},{7,6},{8,9},{9,8},{10,11... | collective-permute-start | bytes 12582920 | tf_op jit(solution)/shard_map/ppermute | solution.py:57
  304.8 14.4 %collective-permute-start.31 = (bf16[128,2048]{1,0:T(8,128)(2,1)S(1)}, bf16[128,2048]{1,0:T(8,128)(2,1)S(1)}, u32[]{:S(2)}, u32[]{:S(2)}) collective-permute-start(bf16[128,2048]{1,0:T(8,128)(2,1)S(1)} %slice.724), channel_id=1, source_target_pairs={{0,16},{1,17},{2,18},{3,19},{4,20},{5,21},{6,22},{7,23},{8,24},{9,... | collective-permute-start | bytes 1572872 | tf_op jit(solution)/shard_map/ppermute | solution.py:57
  307.3 14.1 %collective-permute-start.32 = (bf16[128,2048]{1,0:T(8,128)(2,1)S(1)}, bf16[128,2048]{1,0:T(8,128)(2,1)S(1)}, u32[]{:S(2)}, u32[]{:S(2)}) collective-permute-start(bf16[128,2048]{1,0:T(8,128)(2,1)S(1)} %slice.725), channel_id=1, source_target_pairs={{0,8},{1,9},{2,10},{3,11},{4,12},{5,13},{6,14},{7,15},{8,0},{9,1},... | collective-permute-start | bytes 1572872 | tf_op jit(solution)/shard_map/ppermute | solution.py:57
  322.2 67.8 %collective-permute-start.33 = (bf16[1024,2048]{1,0:T(8,128)(2,1)}, bf16[1024,2048]{1,0:T(8,128)(2,1)}, u32[]{:S(2)}, u32[]{:S(2)}) collective-permute-start(bf16[1024,2048]{1,0:T(8,128)(2,1)} %constant_dynamic-update-slice_fusion.13), channel_id=1, source_target_pairs={{0,1},{1,0},{2,3},{3,2},{4,5},{5,4},{6,7},{7,6},{8,9},{9,8},{10,11... | collective-permute-start | bytes 12582920 | tf_op jit(solution)/shard_map/ppermute | solution.py:57
  323.6 14.1 %collective-permute-start.19 = (bf16[1024,128]{1,0:T(8,128)(2,1)S(1)}, bf16[1024,128]{1,0:T(8,128)(2,1)S(1)}, u32[]{:S(2)}, u32[]{:S(2)}) collective-permute-start(bf16[1024,128]{1,0:T(8,128)(2,1)S(1)} %bitcast.306), channel_id=1, source_target_pairs={{0,16},{1,17},{2,18},{3,19},{4,20},{5,21},{6,22},{7,23},{8,24},{9,... | collective-permute-start | bytes 786440 | tf_op jit(solution)/shard_map/ppermute | solution.py:57
  323.9 13.7 %collective-permute-start.20 = (bf16[1024,128]{1,0:T(8,128)(2,1)S(1)}, bf16[1024,128]{1,0:T(8,128)(2,1)S(1)}, u32[]{:S(2)}, u32[]{:S(2)}) collective-permute-start(bf16[1024,128]{1,0:T(8,128)(2,1)S(1)} %bitcast.307), channel_id=1, source_target_pairs={{0,24},{1,25},{2,26},{3,27},{4,28},{5,29},{6,30},{7,31},{8,16},{9,... | collective-permute-start | bytes 786440 | tf_op jit(solution)/shard_map/ppermute | solution.py:57
  383.2 63.2 %collective-permute-start.21 = (bf16[8,128,2048]{2,1,0:T(8,128)(2,1)}, bf16[8,128,2048]{2,1,0:T(8,128)(2,1)}, u32[]{:S(2)}, u32[]{:S(2)}) collective-permute-start(bf16[8,128,2048]{2,1,0:T(8,128)(2,1)} %get-tuple-element.35), channel_id=1, source_target_pairs={{0,1},{1,0},{2,3},{3,2},{4,5},{5,4},{6,7},{7,6},{8,9},{9,8},{10,11... | collective-permute-start | bytes 12582920 | tf_op jit(solution)/shard_map/ppermute | solution.py:57
  385.9 46.0 %collective-permute-start.34 = (bf16[512,512]{1,0:T(8,128)(2,1)}, bf16[512,512]{1,0:T(8,128)(2,1)S(1)}, u32[]{:S(2)}, u32[]{:S(2)}) collective-permute-start(bf16[512,512]{1,0:T(8,128)(2,1)} %get-tuple-element.89), channel_id=1, source_target_pairs={{0,8},{1,9},{2,10},{3,11},{4,12},{5,13},{6,14},{7,15},{8,0},{9,1},... | collective-permute-start | bytes 1572872 | tf_op jit(solution)/shard_map/ppermute | solution.py:57
  387.4 44.5 %collective-permute-start.35 = (bf16[512,512]{1,0:T(8,128)(2,1)}, bf16[512,512]{1,0:T(8,128)(2,1)S(1)}, u32[]{:S(2)}, u32[]{:S(2)}) collective-permute-start(bf16[512,512]{1,0:T(8,128)(2,1)} %get-tuple-element.91), channel_id=1, source_target_pairs={{0,16},{1,17},{2,18},{3,19},{4,20},{5,21},{6,22},{7,23},{8,24},{9,... | collective-permute-start | bytes 1572872 | tf_op jit(solution)/shard_map/ppermute | solution.py:57
  387.9 44.0 %collective-permute-start.36 = (bf16[512,512]{1,0:T(8,128)(2,1)}, bf16[512,512]{1,0:T(8,128)(2,1)S(1)}, u32[]{:S(2)}, u32[]{:S(2)}) collective-permute-start(bf16[512,512]{1,0:T(8,128)(2,1)} %get-tuple-element.90), channel_id=1, source_target_pairs={{0,24},{1,25},{2,26},{3,27},{4,28},{5,29},{6,30},{7,31},{8,16},{9,... | collective-permute-start | bytes 1572872 | tf_op jit(solution)/shard_map/ppermute | solution.py:57
  431.8 22.1 %collective-permute-start.38 = (bf16[8,128,2048]{2,1,0:T(8,128)(2,1)}, bf16[8,128,2048]{2,1,0:T(8,128)(2,1)}, u32[]{:S(2)}, u32[]{:S(2)}) collective-permute-start(bf16[8,128,2048]{2,1,0:T(8,128)(2,1)} %get-tuple-element.38), channel_id=1, source_target_pairs={{0,1},{1,0},{2,3},{3,2},{4,5},{5,4},{6,7},{7,6},{8,9},{9,8},{10,11... | collective-permute-start | bytes 12582920 | tf_op jit(solution)/shard_map/ppermute | solution.py:57
  452.2 26.1 %collective-permute-start.22 = (bf16[256,2048]{1,0:T(8,128)(2,1)S(1)}, bf16[256,2048]{1,0:T(8,128)(2,1)S(1)}, u32[]{:S(2)}, u32[]{:S(2)}) collective-permute-start(bf16[256,2048]{1,0:T(8,128)(2,1)S(1)} %pad_maximum_fusion.3), channel_id=1, source_target_pairs={{0,8},{1,9},{2,10},{3,11},{4,12},{5,13},{6,14},{7,15},{8,0},{9,1},... | collective-permute-start | bytes 3145736 | tf_op jit(solution)/shard_map/ppermute | solution.py:57
  458.5 26.1 %collective-permute-start.41 = (bf16[256,2048]{1,0:T(8,128)(2,1)S(1)}, bf16[256,2048]{1,0:T(8,128)(2,1)S(1)}, u32[]{:S(2)}, u32[]{:S(2)}) collective-permute-start(bf16[256,2048]{1,0:T(8,128)(2,1)S(1)} %pad_maximum_fusion.7), channel_id=1, source_target_pairs={{0,16},{1,17},{2,18},{3,19},{4,20},{5,21},{6,22},{7,23},{8,24},{9,... | collective-permute-start | bytes 3145736 | tf_op jit(solution)/shard_map/ppermute | solution.py:57
  459.9 40.0 %collective-permute-start.39 = (bf16[256,2048]{1,0:T(8,128)(2,1)S(1)}, bf16[256,2048]{1,0:T(8,128)(2,1)S(1)}, u32[]{:S(2)}, u32[]{:S(2)}) collective-permute-start(bf16[256,2048]{1,0:T(8,128)(2,1)S(1)} %pad_maximum_fusion.6), channel_id=1, source_target_pairs={{0,8},{1,9},{2,10},{3,11},{4,12},{5,13},{6,14},{7,15},{8,0},{9,1},... | collective-permute-start | bytes 3145736 | tf_op jit(solution)/shard_map/ppermute | solution.py:57
  460.9 46.1 %collective-permute-start.25 = (bf16[256,2048]{1,0:T(8,128)(2,1)S(1)}, bf16[256,2048]{1,0:T(8,128)(2,1)S(1)}, u32[]{:S(2)}, u32[]{:S(2)}) collective-permute-start(bf16[256,2048]{1,0:T(8,128)(2,1)S(1)} %pad_maximum_fusion.4), channel_id=1, source_target_pairs={{0,16},{1,17},{2,18},{3,19},{4,20},{5,21},{6,22},{7,23},{8,24},{9,... | collective-permute-start | bytes 3145736 | tf_op jit(solution)/shard_map/ppermute | solution.py:57
  478.4 39.0 %collective-permute-start.23 = (bf16[128,2048]{1,0:T(8,128)(2,1)S(1)}, bf16[128,2048]{1,0:T(8,128)(2,1)S(1)}, u32[]{:S(2)}, u32[]{:S(2)}) collective-permute-start(bf16[128,2048]{1,0:T(8,128)(2,1)S(1)} %fusion.52), channel_id=1, source_target_pairs={{0,16},{1,17},{2,18},{3,19},{4,20},{5,21},{6,22},{7,23},{8,24},{9,... | collective-permute-start | bytes 1572872 | tf_op jit(solution)/shard_map/ppermute | solution.py:57
  500.3 25.7 %collective-permute-start.42 = (bf16[128,2048]{1,0:T(8,128)(2,1)S(1)}, bf16[128,2048]{1,0:T(8,128)(2,1)S(1)}, u32[]{:S(2)}, u32[]{:S(2)}) collective-permute-start(bf16[128,2048]{1,0:T(8,128)(2,1)S(1)} %get-tuple-element.84), channel_id=1, source_target_pairs={{0,8},{1,9},{2,10},{3,11},{4,12},{5,13},{6,14},{7,15},{8,0},{9,1},... | collective-permute-start | bytes 1572872 | tf_op jit(solution)/shard_map/ppermute | solution.py:57
  517.9 13.2 %collective-permute-start.26 = (bf16[128,2048]{1,0:T(8,128)(2,1)S(1)}, bf16[128,2048]{1,0:T(8,128)(2,1)S(1)}, u32[]{:S(2)}, u32[]{:S(2)}) collective-permute-start(bf16[128,2048]{1,0:T(8,128)(2,1)S(1)} %get-tuple-element.78), channel_id=1, source_target_pairs={{0,8},{1,9},{2,10},{3,11},{4,12},{5,13},{6,14},{7,15},{8,0},{9,1},... | collective-permute-start | bytes 1572872 | tf_op jit(solution)/shard_map/ppermute | solution.py:57
  521.4 12.9 %collective-permute-start.40 = (bf16[128,2048]{1,0:T(8,128)(2,1)S(1)}, bf16[128,2048]{1,0:T(8,128)(2,1)S(1)}, u32[]{:S(2)}, u32[]{:S(2)}) collective-permute-start(bf16[128,2048]{1,0:T(8,128)(2,1)S(1)} %get-tuple-element.83), channel_id=1, source_target_pairs={{0,16},{1,17},{2,18},{3,19},{4,20},{5,21},{6,22},{7,23},{8,24},{9,... | collective-permute-start | bytes 1572872 | tf_op jit(solution)/shard_map/ppermute | solution.py:57
  522.0 16.4 %collective-permute-start.24 = (bf16[128,2048]{1,0:T(8,128)(2,1)S(1)}, bf16[128,2048]{1,0:T(8,128)(2,1)S(1)}, u32[]{:S(2)}, u32[]{:S(2)}) collective-permute-start(bf16[128,2048]{1,0:T(8,128)(2,1)S(1)} %get-tuple-element.77), channel_id=1, source_target_pairs={{0,6},{1,7},{2,0},{3,1},{4,2},{5,3},{6,4},{7,5},{8,14},{9,15},{10,... | collective-permute-start | bytes 1572872 | tf_op jit(solution)/shard_map/ppermute | solution.py:57
  526.3 41.5 %collective-permute-start.43 = (bf16[128,2048]{1,0:T(8,128)(2,1)S(1)}, bf16[128,2048]{1,0:T(8,128)(2,1)S(1)}, u32[]{:S(2)}, u32[]{:S(2)}) collective-permute-start(bf16[128,2048]{1,0:T(8,128)(2,1)S(1)} %fusion.44), channel_id=1, source_target_pairs={{0,4},{1,5},{2,6},{3,7},{4,0},{5,1},{6,2},{7,3},{8,12},{9,13},{10,... | collective-permute-start | bytes 1572872 | tf_op jit(solution)/shard_map/ppermute | solution.py:57
  531.4 36.4 %collective-permute-start.27 = (bf16[128,2048]{1,0:T(8,128)(2,1)S(1)}, bf16[128,2048]{1,0:T(8,128)(2,1)S(1)}, u32[]{:S(2)}, u32[]{:S(2)}) collective-permute-start(bf16[128,2048]{1,0:T(8,128)(2,1)S(1)} %fusion.51), channel_id=1, source_target_pairs={{0,2},{1,3},{2,4},{3,5},{4,6},{5,7},{6,0},{7,1},{8,10},{9,11},{10,... | collective-permute-start | bytes 1572872 | tf_op jit(solution)/shard_map/ppermute | solution.py:57
  571.6 13.1 %collective-permute-start.58 = (bf16[128,2048]{1,0:T(8,128)(2,1)S(1)}, bf16[128,2048]{1,0:T(8,128)(2,1)S(1)}, u32[]{:S(2)}, u32[]{:S(2)}) collective-permute-start(bf16[128,2048]{1,0:T(8,128)(2,1)S(1)} %get-tuple-element.56), channel_id=1, source_target_pairs={{0,16},{1,17},{2,18},{3,19},{4,20},{5,21},{6,22},{7,23},{8,24},{9,... | collective-permute-start | bytes 1572872 | tf_op jit(solution)/shard_map/ppermute | solution.py:57
  572.3 25.0 %collective-permute-start.44 = (bf16[8,128,2048]{2,1,0:T(8,128)(2,1)}, bf16[8,128,2048]{2,1,0:T(8,128)(2,1)}, u32[]{:S(2)}, u32[]{:S(2)}) collective-permute-start(bf16[8,128,2048]{2,1,0:T(8,128)(2,1)} %get-tuple-element.39), channel_id=1, source_target_pairs={{0,1},{1,0},{2,3},{3,2},{4,5},{5,4},{6,7},{7,6},{8,9},{9,8},{10,11... | collective-permute-start | bytes 12582920 | tf_op jit(solution)/shard_map/ppermute | solution.py:57
  596.9 210.9 %reduce-scatter.3.cloned.1.call-start = ((), (), s32[]{:S(2)}) async-start(), calls=%async_computation.4 | async-start | bytes 5898240 | tf_op jit(solution)/shard_map/reduce_scatter | solution.py:703
  605.7 139.4 %collective-permute-start.48 = (bf16[256,2048]{1,0:T(8,128)(2,1)}, bf16[256,2048]{1,0:T(8,128)(2,1)}, u32[]{:S(2)}, u32[]{:S(2)}) collective-permute-start(bf16[256,2048]{1,0:T(8,128)(2,1)} %pad_maximum_fusion.9), channel_id=1, source_target_pairs={{0,16},{1,17},{2,18},{3,19},{4,20},{5,21},{6,22},{7,23},{8,24},{9,... | collective-permute-start | bytes 3145736 | tf_op jit(solution)/shard_map/ppermute | solution.py:57
  606.8 107.0 %collective-permute-start.45 = (bf16[256,2048]{1,0:T(8,128)(2,1)}, bf16[256,2048]{1,0:T(8,128)(2,1)}, u32[]{:S(2)}, u32[]{:S(2)}) collective-permute-start(bf16[256,2048]{1,0:T(8,128)(2,1)} %pad_maximum_fusion.8), channel_id=1, source_target_pairs={{0,8},{1,9},{2,10},{3,11},{4,12},{5,13},{6,14},{7,15},{8,0},{9,1},... | collective-permute-start | bytes 3145736 | tf_op jit(solution)/shard_map/ppermute | solution.py:57
  648.9 75.6 %collective-permute-start.54 = (bf16[256,2048]{1,0:T(8,128)(2,1)S(1)}, bf16[256,2048]{1,0:T(8,128)(2,1)S(1)}, u32[]{:S(2)}, u32[]{:S(2)}) collective-permute-start(bf16[256,2048]{1,0:T(8,128)(2,1)S(1)} %pad_maximum_fusion.11), channel_id=1, source_target_pairs={{0,16},{1,17},{2,18},{3,19},{4,20},{5,21},{6,22},{7,23},{8,24},{9,... | collective-permute-start | bytes 3145736 | tf_op jit(solution)/shard_map/ppermute | solution.py:57
  649.7 75.3 %collective-permute-start.52 = (bf16[256,2048]{1,0:T(8,128)(2,1)S(1)}, bf16[256,2048]{1,0:T(8,128)(2,1)S(1)}, u32[]{:S(2)}, u32[]{:S(2)}) collective-permute-start(bf16[256,2048]{1,0:T(8,128)(2,1)S(1)} %pad_maximum_fusion.10), channel_id=1, source_target_pairs={{0,8},{1,9},{2,10},{3,11},{4,12},{5,13},{6,14},{7,15},{8,0},{9,1},... | collective-permute-start | bytes 3145736 | tf_op jit(solution)/shard_map/ppermute | solution.py:57
  651.8 31.6 %collective-permute-start.73 = (f32[2304]{0:T(1024)S(1)}, f32[2304]{0:T(1024)S(1)}, u32[]{:S(2)}, u32[]{:S(2)}) collective-permute-start(f32[2304]{0:T(1024)S(1)} %pad_maximum_fusion.17), channel_id=1, source_target_pairs={{0,1},{1,0},{2,3},{3,2},{4,5},{5,4},{6,7},{7,6},{8,9},{9,8},{10,11... | collective-permute-start | bytes 27656 | tf_op jit(solution)/shard_map/ppermute | solution.py:57
  683.4 12.4 %collective-permute-start.74 = (f32[2304]{0:T(1024)S(1)}, f32[2304]{0:T(1024)S(1)}, u32[]{:S(2)}, u32[]{:S(2)}) collective-permute-start(f32[2304]{0:T(1024)S(1)} %fusion.96), channel_id=1, source_target_pairs={{0,8},{1,9},{2,10},{3,11},{4,12},{5,13},{6,14},{7,15},{8,0},{9,1},... | collective-permute-start | bytes 27656 | tf_op jit(solution)/shard_map/ppermute | solution.py:57
  711.1 11.7 %collective-permute-start.61 = (bf16[128,2048]{1,0:T(8,128)(2,1)S(1)}, bf16[128,2048]{1,0:T(8,128)(2,1)S(1)}, u32[]{:S(2)}, u32[]{:S(2)}) collective-permute-start(bf16[128,2048]{1,0:T(8,128)(2,1)S(1)} %pad_maximum_fusion.13), channel_id=1, source_target_pairs={{0,8},{1,9},{2,10},{3,11},{4,12},{5,13},{6,14},{7,15},{8,0},{9,1},... | collective-permute-start | bytes 1572872 | tf_op jit(solution)/shard_map/ppermute | solution.py:57
  713.8 15.4 %collective-permute-start.63 = (bf16[128,2048]{1,0:T(8,128)(2,1)S(1)}, bf16[128,2048]{1,0:T(8,128)(2,1)S(1)}, u32[]{:S(2)}, u32[]{:S(2)}) collective-permute-start(bf16[128,2048]{1,0:T(8,128)(2,1)S(1)} %pad_maximum_fusion.14), channel_id=1, source_target_pairs={{0,16},{1,17},{2,18},{3,19},{4,20},{5,21},{6,22},{7,23},{8,24},{9,... | collective-permute-start | bytes 1572872 | tf_op jit(solution)/shard_map/ppermute | solution.py:57
  722.8 22.3 %collective-permute-start.46 = (bf16[128,2048]{1,0:T(8,128)(2,1)S(1)}, bf16[128,2048]{1,0:T(8,128)(2,1)S(1)}, u32[]{:S(2)}, u32[]{:S(2)}) collective-permute-start(bf16[128,2048]{1,0:T(8,128)(2,1)S(1)} %fusion.39), channel_id=1, source_target_pairs={{0,16},{1,17},{2,18},{3,19},{4,20},{5,21},{6,22},{7,23},{8,24},{9,... | collective-permute-start | bytes 1572872 | tf_op jit(solution)/shard_map/ppermute | solution.py:57
  724.4 20.5 %collective-permute-start.62 = (bf16[64,2048]{1,0:T(8,128)(2,1)S(1)}, bf16[64,2048]{1,0:T(8,128)(2,1)S(1)}, u32[]{:S(2)}, u32[]{:S(2)}) collective-permute-start(bf16[64,2048]{1,0:T(8,128)(2,1)S(1)} %add_convert_fusion.7), channel_id=1, source_target_pairs={{0,16},{1,17},{2,18},{3,19},{4,20},{5,21},{6,22},{7,23},{8,24},{9,... | collective-permute-start | bytes 786440 | tf_op jit(solution)/shard_map/ppermute | solution.py:57
  727.8 24.4 %collective-permute-start.55 = (bf16[128,2048]{1,0:T(8,128)(2,1)S(1)}, bf16[128,2048]{1,0:T(8,128)(2,1)S(1)}, u32[]{:S(2)}, u32[]{:S(2)}) collective-permute-start(bf16[128,2048]{1,0:T(8,128)(2,1)S(1)} %get-tuple-element.72), channel_id=1, source_target_pairs={{0,8},{1,9},{2,10},{3,11},{4,12},{5,13},{6,14},{7,15},{8,0},{9,1},... | collective-permute-start | bytes 1572872 | tf_op jit(solution)/shard_map/ppermute | solution.py:57
  729.2 35.2 %collective-permute-start.53 = (bf16[128,2048]{1,0:T(8,128)(2,1)}, bf16[128,2048]{1,0:T(8,128)(2,1)S(1)}, u32[]{:S(2)}, u32[]{:S(2)}) collective-permute-start(bf16[128,2048]{1,0:T(8,128)(2,1)} %get-tuple-element.71), channel_id=1, source_target_pairs={{0,16},{1,17},{2,18},{3,19},{4,20},{5,21},{6,22},{7,23},{8,24},{9,... | collective-permute-start | bytes 1572872 | tf_op jit(solution)/shard_map/ppermute | solution.py:57
  747.6 12.1 %collective-permute-start.49 = (bf16[128,2048]{1,0:T(8,128)(2,1)S(1)}, bf16[128,2048]{1,0:T(8,128)(2,1)S(1)}, u32[]{:S(2)}, u32[]{:S(2)}) collective-permute-start(bf16[128,2048]{1,0:T(8,128)(2,1)S(1)} %get-tuple-element.66), channel_id=1, source_target_pairs={{0,8},{1,9},{2,10},{3,11},{4,12},{5,13},{6,14},{7,15},{8,0},{9,1},... | collective-permute-start | bytes 1572872 | tf_op jit(solution)/shard_map/ppermute | solution.py:57
  749.6 16.6 %collective-permute-start.47 = (bf16[128,2048]{1,0:T(8,128)(2,1)}, bf16[128,2048]{1,0:T(8,128)(2,1)S(1)}, u32[]{:S(2)}, u32[]{:S(2)}) collective-permute-start(bf16[128,2048]{1,0:T(8,128)(2,1)} %get-tuple-element.65), channel_id=1, source_target_pairs={{0,6},{1,7},{2,0},{3,1},{4,2},{5,3},{6,4},{7,5},{8,14},{9,15},{10,... | collective-permute-start | bytes 1572872 | tf_op jit(solution)/shard_map/ppermute | solution.py:57
  754.2 37.8 %collective-permute-start.56 = (bf16[128,2048]{1,0:T(8,128)(2,1)}, bf16[128,2048]{1,0:T(8,128)(2,1)}, u32[]{:S(2)}, u32[]{:S(2)}) collective-permute-start(bf16[128,2048]{1,0:T(8,128)(2,1)} %fusion.29), channel_id=1, source_target_pairs={{0,4},{1,5},{2,6},{3,7},{4,0},{5,1},{6,2},{7,3},{8,12},{9,13},{10,... | collective-permute-start | bytes 1572872 | tf_op jit(solution)/shard_map/ppermute | solution.py:57
  761.8 30.3 %collective-permute-start.50 = (bf16[128,2048]{1,0:T(8,128)(2,1)}, bf16[128,2048]{1,0:T(8,128)(2,1)}, u32[]{:S(2)}, u32[]{:S(2)}) collective-permute-start(bf16[128,2048]{1,0:T(8,128)(2,1)} %fusion.38), channel_id=1, source_target_pairs={{0,2},{1,3},{2,4},{3,5},{4,6},{5,7},{6,0},{7,1},{8,10},{9,11},{10,... | collective-permute-start | bytes 1572872 | tf_op jit(solution)/shard_map/ppermute | solution.py:57
  763.6 31.3 %collective-permute-start.69 = (bf16[512,512]{1,0:T(8,128)(2,1)}, bf16[512,512]{1,0:T(8,128)(2,1)S(1)}, u32[]{:S(2)}, u32[]{:S(2)}) collective-permute-start(bf16[512,512]{1,0:T(8,128)(2,1)} %reduce-scatter.5.cloned.1.call-done), channel_id=1, source_target_pairs={{0,8},{1,9},{2,10},{3,11},{4,12},{5,13},{6,14},{7,15},{8,0},{9,1},... | collective-permute-start | bytes 1572872 | tf_op jit(solution)/shard_map/ppermute | solution.py:57
  764.5 32.0 %collective-permute-start.70 = (bf16[512,512]{1,0:T(8,128)(2,1)}, bf16[512,512]{1,0:T(8,128)(2,1)S(1)}, u32[]{:S(2)}, u32[]{:S(2)}) collective-permute-start(bf16[512,512]{1,0:T(8,128)(2,1)} %reduce-scatter.5.cloned.1.call-done), channel_id=1, source_target_pairs={{0,16},{1,17},{2,18},{3,19},{4,20},{5,21},{6,22},{7,23},{8,24},{9,... | collective-permute-start | bytes 1572872 | tf_op jit(solution)/shard_map/ppermute | solution.py:57
  807.9 14.3 %collective-permute-start.65 = (bf16[256,1280]{1,0:T(8,128)(2,1)}, bf16[256,1280]{1,0:T(8,128)(2,1)S(1)}, u32[]{:S(2)}, u32[]{:S(2)}) collective-permute-start(bf16[256,1280]{1,0:T(8,128)(2,1)} %reduce-scatter.3.cloned.1.call-done), channel_id=1, source_target_pairs={{0,8},{1,9},{2,10},{3,11},{4,12},{5,13},{6,14},{7,15},{8,0},{9,1},... | collective-permute-start | bytes 1966088 | tf_op jit(solution)/shard_map/ppermute | solution.py:57
  809.1 13.9 %collective-permute-start.66 = (bf16[256,1280]{1,0:T(8,128)(2,1)}, bf16[256,1280]{1,0:T(8,128)(2,1)S(1)}, u32[]{:S(2)}, u32[]{:S(2)}) collective-permute-start(bf16[256,1280]{1,0:T(8,128)(2,1)} %reduce-scatter.3.cloned.1.call-done), channel_id=1, source_target_pairs={{0,16},{1,17},{2,18},{3,19},{4,20},{5,21},{6,22},{7,23},{8,24},{9,... | collective-permute-start | bytes 1966088 | tf_op jit(solution)/shard_map/ppermute | solution.py:57
  (69 other events, 468.1 us)
Sparse Core Ops, SparseCore 0:
  14.7 63.1 all-gather.4
  80.0 45.8 all-gather.6
  156.9 164.4 all-gather.8
  597.0 51.7 reduce-scatter.4
  651.0 58.8 reduce-scatter.2
